TPU v7x, 32 devices: a whole 2x2x4 slice. The times are simulated.
32 devices in a mesh: tm: 8 (over y, x, core), space: 4 (over z).
Axes of the slice: x: 2, y: 2, z: 4, core: 2. Of those that a mesh axis runs over, the one named last changes fastest.
Arguments:
- opening_guess_profile: float32 [8, 16, 128, 256], P('tm', 'space'), may hold values from -6 to 6
- capacity: float32 [16, 128, 256], P('space'), may hold values from 0.25 to 4
- thermal_forcing: float32 [8, 16, 128, 256], P('tm', 'space'), may hold values from -3 to 3
- rough_decay_factor: float32 [8, 16, 128, 256], P('tm', 'space'), may hold values from 0.2 to 1
- tile_ids: int32 [64, 32], P('tm', 'space'), may hold values from 0 to 2047, as said below
- tile_count: int32 [64, 4], P('tm', 'space'), may hold values from 2 to 8, as said below
- tile_blocks: float32 [64, 32, 64, 64], P('tm', 'space'), may hold values from -0.25 to 0.25
Outputs:
- updated_opening_state: float32 [8, 16, 128, 256], P('tm', 'space')
- accurate_ending_thermal_state: float32 [8, 16, 128, 256], P('tm', 'space')
Inputs may be any that keep to these rules, and one draw needn't show every extreme that they name: `tile_ids`: the 8 entries of one brick for one step are distinct tile numbers of that brick. `tile_count`: on every brick of every slab some step uses all 8 slots.
All inputs are finite; a program needn't handle non-finite values.
Results may differ from a plain program's by a relative error of at most 0.0003.
Values sent between devices are 32-bit elements; how exact they have to be, the bound alone decides.
No kernel may reach another device: no remote copies, remote signals or barrier semaphores. Data moves between devices by JAX's collectives and lax.ppermute only.
A program may use at most 128 MiB of HBM per device.

v0:
```python
import jax
import jax.numpy as jnp
from jax import lax
from jax.sharding import PartitionSpec as P

INCREMENTS = 8
SWEEPS = 4


COND = 1.0


def extended(cells, sides, width):
    for axis, dim in sides:
        count = lax.axis_size(axis)
        ends = count - 1
        head = lax.slice_in_dim(cells, 0, width, axis=dim)
        tail = lax.slice_in_dim(cells, cells.shape[dim] - width, cells.shape[dim], axis=dim)
        cells = jnp.concatenate(
            [
                lax.ppermute(tail, axis, [(i, (i + 1) % count) for i in range(ends)]),
                cells,
                lax.ppermute(head, axis, [((i + 1) % count, i) for i in range(ends)]),
            ],
            axis=dim,
        )
    return cells


def entering(value, axis, join, neutral):
    count, mine = (lax.axis_size(axis), lax.axis_index(axis))
    pieces = jax.tree.map(lambda part: lax.all_gather(part, axis), value)
    total = jax.tree.map(
        lambda part, zero: jnp.full_like(part, 0) + jnp.asarray(zero, part.dtype), value, neutral
    )

    def lap(position, total):
        longer = join(total, jax.tree.map(lambda part: part[position], pieces))
        return jax.tree.map(lambda new, old: jnp.where(position < mine, new, old), longer, total)

    return lax.fori_loop(0, count - 1, lap, total)


def beside_sum(wide):
    center = wide[1:-1]
    padded = jnp.pad(center, ((0, 0), (1, 1), (1, 1)))
    total = wide[2:] + wide[:-2]
    total = total + padded[:, 2:, 1:-1] + padded[:, :-2, 1:-1]
    return total + padded[:, 1:-1, 2:] + padded[:, 1:-1, :-2]


def interface_fix(field, previous, tile_rows, live_count, blocks):
    shape = field.shape
    tile_len = blocks.shape[-1]
    delta = (field - previous).reshape(-1, tile_len)
    picked = delta[tile_rows]
    fixes = jnp.einsum("src,sc->sr", blocks, picked, precision=lax.Precision.HIGHEST)
    live = (jnp.arange(tile_rows.shape[0]) < live_count)[:, None]
    fixes = jnp.where(live, fixes, 0.0)
    tiles = field.reshape(-1, tile_len).at[tile_rows].add(fixes)
    return tiles.reshape(shape)


def shards(
    opening_guess_profile,
    capacity,
    thermal_forcing,
    rough_decay_factor,
    tile_ids,
    tile_count,
    tile_blocks,
):
    opening_moment = opening_guess_profile[0]
    source = thermal_forcing[0]
    rough_estimate = rough_decay_factor[0]
    width = opening_moment.shape[0]
    stacked = jnp.stack([capacity, source])
    rims = extended(stacked, (("space", 1),), SWEEPS)
    broad_heat_capacity = rims[0]
    wide_source = rims[1]
    wide_inverse = 1.0 / (broad_heat_capacity + 6.0 * COND)
    first_cell = lax.axis_index("space") * width - SWEEPS
    position = first_cell + jnp.arange(width + 2 * SWEEPS)
    inside = ((position >= 0) & (position < width * lax.axis_size("space")))[:, None, None]

    def advance(previous):
        wide_previous = extended(previous, (("space", 0),), SWEEPS)
        wide_rhs = broad_heat_capacity * wide_previous + wide_source
        field = wide_previous
        for sweep_index in range(SWEEPS):
            padded_rows = jnp.pad(field, ((1, 1), (0, 0), (0, 0)))
            field = jnp.where(
                inside, (wide_rhs + COND * beside_sum(padded_rows)) * wide_inverse, 0.0
            )
        return field[SWEEPS : SWEEPS + width]

    def solitary_advance_routine(step_index, field):
        moved = advance(field)
        tile_rows = lax.dynamic_index_in_dim(tile_ids, step_index, 0, keepdims=False)
        live_count = lax.dynamic_index_in_dim(tile_count, step_index, 0, keepdims=False)[0]
        blocks = lax.dynamic_index_in_dim(tile_blocks, step_index, 0, keepdims=False)
        return interface_fix(moved, field, tile_rows, live_count, blocks)

    accurate_ending_thermal_state = lax.fori_loop(
        0, INCREMENTS, solitary_advance_routine, opening_moment
    )
    opening_window = lax.axis_index("tm") == 0
    own_scale = jnp.where(opening_window, 0.0, rough_estimate)
    own_shift = jnp.where(
        opening_window,
        accurate_ending_thermal_state,
        accurate_ending_thermal_state - rough_estimate * opening_moment,
    )

    def compose(prior_iterate, later):
        return (later[0] * prior_iterate[0], later[0] * prior_iterate[1] + later[1])

    scale, shift = entering(
        (own_scale, own_shift),
        "tm",
        compose,
        (jnp.ones_like(rough_estimate), jnp.zeros_like(rough_estimate)),
    )
    updated_opening_state = scale * opening_moment + shift
    return (updated_opening_state[None], accurate_ending_thermal_state[None])


def solution(mesh):
    in_specs = (
        P("tm", "space", None, None),
        P("space", None, None),
        P("tm", "space", None, None),
        P("tm", "space", None, None),
        P("tm", "space"),
        P("tm", "space"),
        P("tm", "space", None, None),
    )
    out_specs = (P("tm", "space", None, None), P("tm", "space", None, None))
    return jax.shard_map(shards, mesh=mesh, in_specs=in_specs, out_specs=out_specs, check_vma=False)
```

profile of v0, /device:TPU:8, one launch (start us, length us, event | category | flops | bytes accessed | tf_op | source)
XLA Modules:
  0.0 306.0 jit_solution(8534364683523705857)
XLA Ops:
  8.6 3.6 %collective-permute-start.2 = (f32[2,4,128,256]{3,2,1,0:T(8,128)S(1)}, f32[2,4,128,256]{3,2,1,0:T(8,128)}, u32[]{:S(2)}, u32[]{:S(2)}) collective-permute-start(f32[2,4,128,256]{3,2,1,0:T(8,128)S(1)} %pad_maximum_fusion.1), channel_id=1, source_target_pairs={{0,1},{1,2},{2,3},{4,5},{5,6},{6,7},{8,9},{9,10},{10,11},{12,13},{... | collective-permute-start | bytes 3145736 | tf_op jit(solution)/shard_map/ppermute | solution.py:21
  12.3 3.3 %collective-permute-start.3 = (f32[2,4,128,256]{3,2,1,0:T(8,128)S(1)}, f32[2,4,128,256]{3,2,1,0:T(8,128)}, u32[]{:S(2)}, u32[]{:S(2)}) collective-permute-start(f32[2,4,128,256]{3,2,1,0:T(8,128)S(1)} %pad_maximum_fusion.1), channel_id=1, source_target_pairs={{1,0},{2,1},{3,2},{5,4},{6,5},{7,6},{9,8},{10,9},{11,10},{13,12},{... | collective-permute-start | bytes 3145736 | tf_op jit(solution)/shard_map/ppermute | solution.py:23
  16.6 19.1 %collective-permute-done.2 = f32[2,4,128,256]{3,2,1,0:T(8,128)} collective-permute-done((f32[2,4,128,256]{3,2,1,0:T(8,128)S(1)}, f32[2,4,128,256]{3,2,1,0:T(8,128)}, u32[]{:S(2)}, u32[]{:S(2)}) %collective-permute-start.2) | collective-permute-done | bytes 1048608 | tf_op jit(solution)/shard_map/ppermute | solution.py:21
  35.7 3.2 %collective-permute-done.3 = f32[2,4,128,256]{3,2,1,0:T(8,128)} collective-permute-done((f32[2,4,128,256]{3,2,1,0:T(8,128)S(1)}, f32[2,4,128,256]{3,2,1,0:T(8,128)}, u32[]{:S(2)}, u32[]{:S(2)}) %collective-permute-start.3) | collective-permute-done | bytes 1048608 | tf_op jit(solution)/shard_map/ppermute | solution.py:23
  38.9 2.3 pad_maximum_fusion
  41.2 2.0 slice_bitcast_fusion
  43.8 204.3 %while.32 = (s32[]{:T(128)}, f32[4,128,256]{2,1,0:T(8,128)S(1)}, f32[12,128,256]{2,1,0:T(8,128)}, f32[12,128,256]{2,1,0:T(8,128)}, f32[12,128,256]{2,1,0:T(8,128...) while((s32[]{:T(128)}, f32[4,128,256]{2,1,0:T(8,128)S(1)}, ...), condition=%wide.region_2.3_spmd.clone, body=%wide.region_0.2_spmd.clone.sunk | while | flops 12322898 | bytes 60572668 | solution.py:104
  43.8 3.6 %collective-permute-start = (f32[4,128,256]{2,1,0:T(8,128)S(1)}, f32[4,128,256]{2,1,0:T(8,128)S(1)}, u32[]{:S(2)}, u32[]{:S(2)}) collective-permute-start(f32[4,128,256]{2,1,0:T(8,128)S(1)} %get-tuple-element.543), channel_id=1, source_target_pairs={{0,1},{1,2},{2,3},{4,5},{5,6},{6,7},{8,9},{9,10},{10,11},{12,13},{... | collective-permute-start | bytes 1572872 | tf_op jit(solution)/shard_map/while/body/eval_jaxpr/ppermute | solution.py:21
  47.4 2.3 collective-permute-start.1
  51.8 6.0 %collective-permute-done = f32[4,128,256]{2,1,0:T(8,128)S(1)} collective-permute-done((f32[4,128,256]{2,1,0:T(8,128)S(1)}, f32[4,128,256]{2,1,0:T(8,128)S(1)}, u32[]{:S(2)}, u32[]{:S(2)}) %collective-permute-start) | collective-permute-done | bytes 524320 | tf_op jit(solution)/shard_map/while/body/eval_jaxpr/ppermute | solution.py:21
  57.8 3.1 %collective-permute-done.1 = f32[4,128,256]{2,1,0:T(8,128)S(1)} collective-permute-done((f32[4,128,256]{2,1,0:T(8,128)S(1)}, f32[4,128,256]{2,1,0:T(8,128)S(1)}, u32[]{:S(2)}, u32[]{:S(2)}) %collective-permute-start.1) | collective-permute-done | bytes 524320 | tf_op jit(solution)/shard_map/while/body/eval_jaxpr/ppermute | solution.py:23
  67.9 1.8 gather_fusion
  72.6 2.2 collective-permute-start
  74.8 3.7 %collective-permute-start.1 = (f32[4,128,256]{2,1,0:T(8,128)S(1)}, f32[4,128,256]{2,1,0:T(8,128)S(1)}, u32[]{:S(2)}, u32[]{:S(2)}) collective-permute-start(f32[4,128,256]{2,1,0:T(8,128)S(1)} %get-tuple-element.543), channel_id=1, source_target_pairs={{1,0},{2,1},{3,2},{5,4},{6,5},{7,6},{9,8},{10,9},{11,10},{13,12},{... | collective-permute-start | bytes 1572872 | tf_op jit(solution)/shard_map/while/body/eval_jaxpr/ppermute | solution.py:23
  80.5 4.7 %collective-permute-done = f32[4,128,256]{2,1,0:T(8,128)S(1)} collective-permute-done((f32[4,128,256]{2,1,0:T(8,128)S(1)}, f32[4,128,256]{2,1,0:T(8,128)S(1)}, u32[]{:S(2)}, u32[]{:S(2)}) %collective-permute-start) | collective-permute-done | bytes 524320 | tf_op jit(solution)/shard_map/while/body/eval_jaxpr/ppermute | solution.py:21
  85.3 2.1 collective-permute-done.1
  94.4 1.8 gather_fusion
  99.0 2.2 collective-permute-start
  101.3 3.7 %collective-permute-start.1 = (f32[4,128,256]{2,1,0:T(8,128)S(1)}, f32[4,128,256]{2,1,0:T(8,128)S(1)}, u32[]{:S(2)}, u32[]{:S(2)}) collective-permute-start(f32[4,128,256]{2,1,0:T(8,128)S(1)} %get-tuple-element.543), channel_id=1, source_target_pairs={{1,0},{2,1},{3,2},{5,4},{6,5},{7,6},{9,8},{10,9},{11,10},{13,12},{... | collective-permute-start | bytes 1572872 | tf_op jit(solution)/shard_map/while/body/eval_jaxpr/ppermute | solution.py:23
  107.0 3.7 %collective-permute-done = f32[4,128,256]{2,1,0:T(8,128)S(1)} collective-permute-done((f32[4,128,256]{2,1,0:T(8,128)S(1)}, f32[4,128,256]{2,1,0:T(8,128)S(1)}, u32[]{:S(2)}, u32[]{:S(2)}) %collective-permute-start) | collective-permute-done | bytes 524320 | tf_op jit(solution)/shard_map/while/body/eval_jaxpr/ppermute | solution.py:21
  110.8 2.1 collective-permute-done.1
  119.9 1.8 gather_fusion
  124.6 2.2 collective-permute-start
  126.8 3.7 %collective-permute-start.1 = (f32[4,128,256]{2,1,0:T(8,128)S(1)}, f32[4,128,256]{2,1,0:T(8,128)S(1)}, u32[]{:S(2)}, u32[]{:S(2)}) collective-permute-start(f32[4,128,256]{2,1,0:T(8,128)S(1)} %get-tuple-element.543), channel_id=1, source_target_pairs={{1,0},{2,1},{3,2},{5,4},{6,5},{7,6},{9,8},{10,9},{11,10},{13,12},{... | collective-permute-start | bytes 1572872 | tf_op jit(solution)/shard_map/while/body/eval_jaxpr/ppermute | solution.py:23
  132.5 3.1 %collective-permute-done = f32[4,128,256]{2,1,0:T(8,128)S(1)} collective-permute-done((f32[4,128,256]{2,1,0:T(8,128)S(1)}, f32[4,128,256]{2,1,0:T(8,128)S(1)}, u32[]{:S(2)}, u32[]{:S(2)}) %collective-permute-start) | collective-permute-done | bytes 524320 | tf_op jit(solution)/shard_map/while/body/eval_jaxpr/ppermute | solution.py:21
  135.8 2.1 collective-permute-done.1
  144.9 1.8 gather_fusion
  149.5 1.9 collective-permute-start
  151.5 4.0 %collective-permute-start.1 = (f32[4,128,256]{2,1,0:T(8,128)S(1)}, f32[4,128,256]{2,1,0:T(8,128)S(1)}, u32[]{:S(2)}, u32[]{:S(2)}) collective-permute-start(f32[4,128,256]{2,1,0:T(8,128)S(1)} %get-tuple-element.543), channel_id=1, source_target_pairs={{1,0},{2,1},{3,2},{5,4},{6,5},{7,6},{9,8},{10,9},{11,10},{13,12},{... | collective-permute-start | bytes 1572872 | tf_op jit(solution)/shard_map/while/body/eval_jaxpr/ppermute | solution.py:23
  157.5 3.1 %collective-permute-done = f32[4,128,256]{2,1,0:T(8,128)S(1)} collective-permute-done((f32[4,128,256]{2,1,0:T(8,128)S(1)}, f32[4,128,256]{2,1,0:T(8,128)S(1)}, u32[]{:S(2)}, u32[]{:S(2)}) %collective-permute-start) | collective-permute-done | bytes 524320 | tf_op jit(solution)/shard_map/while/body/eval_jaxpr/ppermute | solution.py:21
  160.7 1.8 collective-permute-done.1
  169.5 1.8 gather_fusion
  174.2 1.9 collective-permute-start
  176.1 4.0 %collective-permute-start.1 = (f32[4,128,256]{2,1,0:T(8,128)S(1)}, f32[4,128,256]{2,1,0:T(8,128)S(1)}, u32[]{:S(2)}, u32[]{:S(2)}) collective-permute-start(f32[4,128,256]{2,1,0:T(8,128)S(1)} %get-tuple-element.543), channel_id=1, source_target_pairs={{1,0},{2,1},{3,2},{5,4},{6,5},{7,6},{9,8},{10,9},{11,10},{13,12},{... | collective-permute-start | bytes 1572872 | tf_op jit(solution)/shard_map/while/body/eval_jaxpr/ppermute | solution.py:23
  182.1 3.1 %collective-permute-done = f32[4,128,256]{2,1,0:T(8,128)S(1)} collective-permute-done((f32[4,128,256]{2,1,0:T(8,128)S(1)}, f32[4,128,256]{2,1,0:T(8,128)S(1)}, u32[]{:S(2)}, u32[]{:S(2)}) %collective-permute-start) | collective-permute-done | bytes 524320 | tf_op jit(solution)/shard_map/while/body/eval_jaxpr/ppermute | solution.py:21
  185.3 1.8 collective-permute-done.1
  194.2 1.8 gather_fusion
  198.8 1.9 collective-permute-start
  200.7 4.0 %collective-permute-start.1 = (f32[4,128,256]{2,1,0:T(8,128)S(1)}, f32[4,128,256]{2,1,0:T(8,128)S(1)}, u32[]{:S(2)}, u32[]{:S(2)}) collective-permute-start(f32[4,128,256]{2,1,0:T(8,128)S(1)} %get-tuple-element.543), channel_id=1, source_target_pairs={{1,0},{2,1},{3,2},{5,4},{6,5},{7,6},{9,8},{10,9},{11,10},{13,12},{... | collective-permute-start | bytes 1572872 | tf_op jit(solution)/shard_map/while/body/eval_jaxpr/ppermute | solution.py:23
  206.8 3.1 %collective-permute-done = f32[4,128,256]{2,1,0:T(8,128)S(1)} collective-permute-done((f32[4,128,256]{2,1,0:T(8,128)S(1)}, f32[4,128,256]{2,1,0:T(8,128)S(1)}, u32[]{:S(2)}, u32[]{:S(2)}) %collective-permute-start) | collective-permute-done | bytes 524320 | tf_op jit(solution)/shard_map/while/body/eval_jaxpr/ppermute | solution.py:21
  210.0 1.8 collective-permute-done.1
  223.5 1.9 collective-permute-start
  225.4 4.0 %collective-permute-start.1 = (f32[4,128,256]{2,1,0:T(8,128)S(1)}, f32[4,128,256]{2,1,0:T(8,128)S(1)}, u32[]{:S(2)}, u32[]{:S(2)}) collective-permute-start(f32[4,128,256]{2,1,0:T(8,128)S(1)} %get-tuple-element.543), channel_id=1, source_target_pairs={{1,0},{2,1},{3,2},{5,4},{6,5},{7,6},{9,8},{10,9},{11,10},{13,12},{... | collective-permute-start | bytes 1572872 | tf_op jit(solution)/shard_map/while/body/eval_jaxpr/ppermute | solution.py:23
  231.4 3.1 %collective-permute-done = f32[4,128,256]{2,1,0:T(8,128)S(1)} collective-permute-done((f32[4,128,256]{2,1,0:T(8,128)S(1)}, f32[4,128,256]{2,1,0:T(8,128)S(1)}, u32[]{:S(2)}, u32[]{:S(2)}) %collective-permute-start) | collective-permute-done | bytes 524320 | tf_op jit(solution)/shard_map/while/body/eval_jaxpr/ppermute | solution.py:21
  234.6 1.8 collective-permute-done.1
  248.1 2.4 subtract_select_fusion
  250.6 36.4 %all-gather.6.cloned.1.call-done = f32[32,128,256]{2,1,0:T(8,128)} async-done(((f32[4,128,256]{2,1,0:T(8,128)}), f32[32,128,256]{2,1,0:T(8,128)}) %all-gather.6.cloned.1.call-update) | async-done | bytes 4194320 | tf_op jit(solution)/shard_map/all_gather | solution.py:32
  287.0 11.2 %while.33 = (s32[]{:T(128)}, f32[4,128,256]{2,1,0:T(8,128)S(1)}, f32[4,128,256]{2,1,0:T(8,128)S(1)}, s32[]{:T(128)}, f32[8,4,128,256]{3,2,1,0:T(8,128)}, /*index=5*/f32[8,4,128,256]{3,2,1,0:T(8,128)}, s32[]{:T(128)}, s32[]{:T(128)}) while((s32[]{:T(128)}, f32[4,128,256]{2,1,0:T(8,128)S(1)}, f32[4,128,256]{2,1,0:T(8,128)S(1)}, ...), condition=%wide.region_4.5_spmd.clone, body=%wide.region_3.4_spmd.clone.sunk | while | flops 917508 | bytes 3145837 | solution.py:41
  (235 shorter events, 113.6 us)
Async XLA Ops:
  7.2 8.5 %copy-start.6 = (f32[1,4,128,256]{3,2,1,0:T(8,128)S(1)}, f32[1,4,128,256]{3,2,1,0:T(8,128)}, u32[]{:S(2)}) copy-start(f32[1,4,128,256]{3,2,1,0:T(8,128)} %param.14) | copy-start | bytes 1572868
  7.2 243.4 %all-gather.4.cloned.1.call-start = ((), (), s32[]{:S(2)}) async-start(), calls=%async_computation | async-start | bytes 4718592 | tf_op jit(solution)/shard_map/all_gather | solution.py:32
  7.2 9.3 %copy-start.4 = (f32[1,4,128,256]{3,2,1,0:T(8,128)S(1)}, f32[1,4,128,256]{3,2,1,0:T(8,128)}, u32[]{:S(2)}) copy-start(f32[1,4,128,256]{3,2,1,0:T(8,128)} %param.11) | copy-start | bytes 1572868
  8.6 30.3 %copy-start.7 = (f32[1,4,128,256]{3,2,1,0:T(8,128)S(1)}, f32[1,4,128,256]{3,2,1,0:T(8,128)}, u32[]{:S(2)}) copy-start(f32[1,4,128,256]{3,2,1,0:T(8,128)} %param.13) | copy-start | bytes 1572868
  8.6 30.3 %copy-start.8 = (f32[4,128,256]{2,1,0:T(8,128)S(1)}, f32[4,128,256]{2,1,0:T(8,128)}, u32[]{:S(2)}) copy-start(f32[4,128,256]{2,1,0:T(8,128)} %param.12) | copy-start | bytes 1572868
  8.6 27.0 %collective-permute-start.2 = (f32[2,4,128,256]{3,2,1,0:T(8,128)S(1)}, f32[2,4,128,256]{3,2,1,0:T(8,128)}, u32[]{:S(2)}, u32[]{:S(2)}) collective-permute-start(f32[2,4,128,256]{3,2,1,0:T(8,128)S(1)} %pad_maximum_fusion.1), channel_id=1, source_target_pairs={{0,1},{1,2},{2,3},{4,5},{5,6},{6,7},{8,9},{9,10},{10,11},{12,13},{... | collective-permute-start | bytes 3145736 | tf_op jit(solution)/shard_map/ppermute | solution.py:21
  12.3 26.6 %collective-permute-start.3 = (f32[2,4,128,256]{3,2,1,0:T(8,128)S(1)}, f32[2,4,128,256]{3,2,1,0:T(8,128)}, u32[]{:S(2)}, u32[]{:S(2)}) collective-permute-start(f32[2,4,128,256]{3,2,1,0:T(8,128)S(1)} %pad_maximum_fusion.1), channel_id=1, source_target_pairs={{1,0},{2,1},{3,2},{5,4},{6,5},{7,6},{9,8},{10,9},{11,10},{13,12},{... | collective-permute-start | bytes 3145736 | tf_op jit(solution)/shard_map/ppermute | solution.py:23
  16.5 270.5 %all-gather.6.cloned.1.call-start = ((), (), s32[]{:S(2)}) async-start(), calls=%async_computation.1 | async-start | bytes 4718592 | tf_op jit(solution)/shard_map/all_gather | solution.py:32
  43.8 13.9 %collective-permute-start = (f32[4,128,256]{2,1,0:T(8,128)S(1)}, f32[4,128,256]{2,1,0:T(8,128)S(1)}, u32[]{:S(2)}, u32[]{:S(2)}) collective-permute-start(f32[4,128,256]{2,1,0:T(8,128)S(1)} %get-tuple-element.543), channel_id=1, source_target_pairs={{0,1},{1,2},{2,3},{4,5},{5,6},{6,7},{8,9},{9,10},{10,11},{12,13},{... | collective-permute-start | bytes 1572872 | tf_op jit(solution)/shard_map/while/body/eval_jaxpr/ppermute | solution.py:21
  47.4 13.5 %collective-permute-start.1 = (f32[4,128,256]{2,1,0:T(8,128)S(1)}, f32[4,128,256]{2,1,0:T(8,128)S(1)}, u32[]{:S(2)}, u32[]{:S(2)}) collective-permute-start(f32[4,128,256]{2,1,0:T(8,128)S(1)} %get-tuple-element.543), channel_id=1, source_target_pairs={{1,0},{2,1},{3,2},{5,4},{6,5},{7,6},{9,8},{10,9},{11,10},{13,12},{... | collective-permute-start | bytes 1572872 | tf_op jit(solution)/shard_map/while/body/eval_jaxpr/ppermute | solution.py:23
  51.7 9.2 %copy-start.1 = (f32[12,128,256]{2,1,0:T(8,128)S(1)}, f32[12,128,256]{2,1,0:T(8,128)}, u32[]{:S(2)}) copy-start(f32[12,128,256]{2,1,0:T(8,128)} %get-tuple-element.556) | copy-start | bytes 4718596 | tf_op jit(solution)/shard_map/while
  51.7 9.2 %copy-start.2 = (f32[12,128,256]{2,1,0:T(8,128)S(1)}, f32[12,128,256]{2,1,0:T(8,128)}, u32[]{:S(2)}) copy-start(f32[12,128,256]{2,1,0:T(8,128)} %get-tuple-element.555) | copy-start | bytes 4718596 | tf_op jit(solution)/shard_map/while
  72.6 12.6 %collective-permute-start = (f32[4,128,256]{2,1,0:T(8,128)S(1)}, f32[4,128,256]{2,1,0:T(8,128)S(1)}, u32[]{:S(2)}, u32[]{:S(2)}) collective-permute-start(f32[4,128,256]{2,1,0:T(8,128)S(1)} %get-tuple-element.543), channel_id=1, source_target_pairs={{0,1},{1,2},{2,3},{4,5},{5,6},{6,7},{8,9},{9,10},{10,11},{12,13},{... | collective-permute-start | bytes 1572872 | tf_op jit(solution)/shard_map/while/body/eval_jaxpr/ppermute | solution.py:21
  74.8 12.6 %collective-permute-start.1 = (f32[4,128,256]{2,1,0:T(8,128)S(1)}, f32[4,128,256]{2,1,0:T(8,128)S(1)}, u32[]{:S(2)}, u32[]{:S(2)}) collective-permute-start(f32[4,128,256]{2,1,0:T(8,128)S(1)} %get-tuple-element.543), channel_id=1, source_target_pairs={{1,0},{2,1},{3,2},{5,4},{6,5},{7,6},{9,8},{10,9},{11,10},{13,12},{... | collective-permute-start | bytes 1572872 | tf_op jit(solution)/shard_map/while/body/eval_jaxpr/ppermute | solution.py:23
  80.5 6.9 %copy-start.1 = (f32[12,128,256]{2,1,0:T(8,128)S(1)}, f32[12,128,256]{2,1,0:T(8,128)}, u32[]{:S(2)}) copy-start(f32[12,128,256]{2,1,0:T(8,128)} %get-tuple-element.556) | copy-start | bytes 4718596 | tf_op jit(solution)/shard_map/while
  80.5 6.9 %copy-start.2 = (f32[12,128,256]{2,1,0:T(8,128)S(1)}, f32[12,128,256]{2,1,0:T(8,128)}, u32[]{:S(2)}) copy-start(f32[12,128,256]{2,1,0:T(8,128)} %get-tuple-element.555) | copy-start | bytes 4718596 | tf_op jit(solution)/shard_map/while
  92.9 1.3 copy-start.3
  99.0 11.7 %collective-permute-start = (f32[4,128,256]{2,1,0:T(8,128)S(1)}, f32[4,128,256]{2,1,0:T(8,128)S(1)}, u32[]{:S(2)}, u32[]{:S(2)}) collective-permute-start(f32[4,128,256]{2,1,0:T(8,128)S(1)} %get-tuple-element.543), channel_id=1, source_target_pairs={{0,1},{1,2},{2,3},{4,5},{5,6},{6,7},{8,9},{9,10},{10,11},{12,13},{... | collective-permute-start | bytes 1572872 | tf_op jit(solution)/shard_map/while/body/eval_jaxpr/ppermute | solution.py:21
  101.3 11.7 %collective-permute-start.1 = (f32[4,128,256]{2,1,0:T(8,128)S(1)}, f32[4,128,256]{2,1,0:T(8,128)S(1)}, u32[]{:S(2)}, u32[]{:S(2)}) collective-permute-start(f32[4,128,256]{2,1,0:T(8,128)S(1)} %get-tuple-element.543), channel_id=1, source_target_pairs={{1,0},{2,1},{3,2},{5,4},{6,5},{7,6},{9,8},{10,9},{11,10},{13,12},{... | collective-permute-start | bytes 1572872 | tf_op jit(solution)/shard_map/while/body/eval_jaxpr/ppermute | solution.py:23
  107.0 6.0 %copy-start.1 = (f32[12,128,256]{2,1,0:T(8,128)S(1)}, f32[12,128,256]{2,1,0:T(8,128)}, u32[]{:S(2)}) copy-start(f32[12,128,256]{2,1,0:T(8,128)} %get-tuple-element.556) | copy-start | bytes 4718596 | tf_op jit(solution)/shard_map/while
  107.0 6.0 %copy-start.2 = (f32[12,128,256]{2,1,0:T(8,128)S(1)}, f32[12,128,256]{2,1,0:T(8,128)}, u32[]{:S(2)}) copy-start(f32[12,128,256]{2,1,0:T(8,128)} %get-tuple-element.555) | copy-start | bytes 4718596 | tf_op jit(solution)/shard_map/while
  118.5 1.3 copy-start.3
  124.6 11.1 %collective-permute-start = (f32[4,128,256]{2,1,0:T(8,128)S(1)}, f32[4,128,256]{2,1,0:T(8,128)S(1)}, u32[]{:S(2)}, u32[]{:S(2)}) collective-permute-start(f32[4,128,256]{2,1,0:T(8,128)S(1)} %get-tuple-element.543), channel_id=1, source_target_pairs={{0,1},{1,2},{2,3},{4,5},{5,6},{6,7},{8,9},{9,10},{10,11},{12,13},{... | collective-permute-start | bytes 1572872 | tf_op jit(solution)/shard_map/while/body/eval_jaxpr/ppermute | solution.py:21
  126.8 11.1 %collective-permute-start.1 = (f32[4,128,256]{2,1,0:T(8,128)S(1)}, f32[4,128,256]{2,1,0:T(8,128)S(1)}, u32[]{:S(2)}, u32[]{:S(2)}) collective-permute-start(f32[4,128,256]{2,1,0:T(8,128)S(1)} %get-tuple-element.543), channel_id=1, source_target_pairs={{1,0},{2,1},{3,2},{5,4},{6,5},{7,6},{9,8},{10,9},{11,10},{13,12},{... | collective-permute-start | bytes 1572872 | tf_op jit(solution)/shard_map/while/body/eval_jaxpr/ppermute | solution.py:23
  132.5 5.4 %copy-start.1 = (f32[12,128,256]{2,1,0:T(8,128)S(1)}, f32[12,128,256]{2,1,0:T(8,128)}, u32[]{:S(2)}) copy-start(f32[12,128,256]{2,1,0:T(8,128)} %get-tuple-element.556) | copy-start | bytes 4718596 | tf_op jit(solution)/shard_map/while
  132.5 5.4 %copy-start.2 = (f32[12,128,256]{2,1,0:T(8,128)S(1)}, f32[12,128,256]{2,1,0:T(8,128)}, u32[]{:S(2)}) copy-start(f32[12,128,256]{2,1,0:T(8,128)} %get-tuple-element.555) | copy-start | bytes 4718596 | tf_op jit(solution)/shard_map/while
  143.4 1.3 copy-start.3
  149.5 11.1 %collective-permute-start = (f32[4,128,256]{2,1,0:T(8,128)S(1)}, f32[4,128,256]{2,1,0:T(8,128)S(1)}, u32[]{:S(2)}, u32[]{:S(2)}) collective-permute-start(f32[4,128,256]{2,1,0:T(8,128)S(1)} %get-tuple-element.543), channel_id=1, source_target_pairs={{0,1},{1,2},{2,3},{4,5},{5,6},{6,7},{8,9},{9,10},{10,11},{12,13},{... | collective-permute-start | bytes 1572872 | tf_op jit(solution)/shard_map/while/body/eval_jaxpr/ppermute | solution.py:21
  151.5 11.1 %collective-permute-start.1 = (f32[4,128,256]{2,1,0:T(8,128)S(1)}, f32[4,128,256]{2,1,0:T(8,128)S(1)}, u32[]{:S(2)}, u32[]{:S(2)}) collective-permute-start(f32[4,128,256]{2,1,0:T(8,128)S(1)} %get-tuple-element.543), channel_id=1, source_target_pairs={{1,0},{2,1},{3,2},{5,4},{6,5},{7,6},{9,8},{10,9},{11,10},{13,12},{... | collective-permute-start | bytes 1572872 | tf_op jit(solution)/shard_map/while/body/eval_jaxpr/ppermute | solution.py:23
  157.5 5.1 %copy-start.1 = (f32[12,128,256]{2,1,0:T(8,128)S(1)}, f32[12,128,256]{2,1,0:T(8,128)}, u32[]{:S(2)}) copy-start(f32[12,128,256]{2,1,0:T(8,128)} %get-tuple-element.556) | copy-start | bytes 4718596 | tf_op jit(solution)/shard_map/while
  157.5 5.1 %copy-start.2 = (f32[12,128,256]{2,1,0:T(8,128)S(1)}, f32[12,128,256]{2,1,0:T(8,128)}, u32[]{:S(2)}) copy-start(f32[12,128,256]{2,1,0:T(8,128)} %get-tuple-element.555) | copy-start | bytes 4718596 | tf_op jit(solution)/shard_map/while
  168.0 1.3 copy-start.3
  174.2 11.1 %collective-permute-start = (f32[4,128,256]{2,1,0:T(8,128)S(1)}, f32[4,128,256]{2,1,0:T(8,128)S(1)}, u32[]{:S(2)}, u32[]{:S(2)}) collective-permute-start(f32[4,128,256]{2,1,0:T(8,128)S(1)} %get-tuple-element.543), channel_id=1, source_target_pairs={{0,1},{1,2},{2,3},{4,5},{5,6},{6,7},{8,9},{9,10},{10,11},{12,13},{... | collective-permute-start | bytes 1572872 | tf_op jit(solution)/shard_map/while/body/eval_jaxpr/ppermute | solution.py:21
  176.1 11.1 %collective-permute-start.1 = (f32[4,128,256]{2,1,0:T(8,128)S(1)}, f32[4,128,256]{2,1,0:T(8,128)S(1)}, u32[]{:S(2)}, u32[]{:S(2)}) collective-permute-start(f32[4,128,256]{2,1,0:T(8,128)S(1)} %get-tuple-element.543), channel_id=1, source_target_pairs={{1,0},{2,1},{3,2},{5,4},{6,5},{7,6},{9,8},{10,9},{11,10},{13,12},{... | collective-permute-start | bytes 1572872 | tf_op jit(solution)/shard_map/while/body/eval_jaxpr/ppermute | solution.py:23
  182.1 5.1 %copy-start.1 = (f32[12,128,256]{2,1,0:T(8,128)S(1)}, f32[12,128,256]{2,1,0:T(8,128)}, u32[]{:S(2)}) copy-start(f32[12,128,256]{2,1,0:T(8,128)} %get-tuple-element.556) | copy-start | bytes 4718596 | tf_op jit(solution)/shard_map/while
  182.1 5.1 %copy-start.2 = (f32[12,128,256]{2,1,0:T(8,128)S(1)}, f32[12,128,256]{2,1,0:T(8,128)}, u32[]{:S(2)}) copy-start(f32[12,128,256]{2,1,0:T(8,128)} %get-tuple-element.555) | copy-start | bytes 4718596 | tf_op jit(solution)/shard_map/while
  192.7 1.3 copy-start.3
  198.8 11.1 %collective-permute-start = (f32[4,128,256]{2,1,0:T(8,128)S(1)}, f32[4,128,256]{2,1,0:T(8,128)S(1)}, u32[]{:S(2)}, u32[]{:S(2)}) collective-permute-start(f32[4,128,256]{2,1,0:T(8,128)S(1)} %get-tuple-element.543), channel_id=1, source_target_pairs={{0,1},{1,2},{2,3},{4,5},{5,6},{6,7},{8,9},{9,10},{10,11},{12,13},{... | collective-permute-start | bytes 1572872 | tf_op jit(solution)/shard_map/while/body/eval_jaxpr/ppermute | solution.py:21
  200.7 11.1 %collective-permute-start.1 = (f32[4,128,256]{2,1,0:T(8,128)S(1)}, f32[4,128,256]{2,1,0:T(8,128)S(1)}, u32[]{:S(2)}, u32[]{:S(2)}) collective-permute-start(f32[4,128,256]{2,1,0:T(8,128)S(1)} %get-tuple-element.543), channel_id=1, source_target_pairs={{1,0},{2,1},{3,2},{5,4},{6,5},{7,6},{9,8},{10,9},{11,10},{13,12},{... | collective-permute-start | bytes 1572872 | tf_op jit(solution)/shard_map/while/body/eval_jaxpr/ppermute | solution.py:23
  206.7 5.1 %copy-start.1 = (f32[12,128,256]{2,1,0:T(8,128)S(1)}, f32[12,128,256]{2,1,0:T(8,128)}, u32[]{:S(2)}) copy-start(f32[12,128,256]{2,1,0:T(8,128)} %get-tuple-element.556) | copy-start | bytes 4718596 | tf_op jit(solution)/shard_map/while
  206.8 5.1 %copy-start.2 = (f32[12,128,256]{2,1,0:T(8,128)S(1)}, f32[12,128,256]{2,1,0:T(8,128)}, u32[]{:S(2)}) copy-start(f32[12,128,256]{2,1,0:T(8,128)} %get-tuple-element.555) | copy-start | bytes 4718596 | tf_op jit(solution)/shard_map/while
  217.3 1.3 copy-start.3
  223.5 11.1 %collective-permute-start = (f32[4,128,256]{2,1,0:T(8,128)S(1)}, f32[4,128,256]{2,1,0:T(8,128)S(1)}, u32[]{:S(2)}, u32[]{:S(2)}) collective-permute-start(f32[4,128,256]{2,1,0:T(8,128)S(1)} %get-tuple-element.543), channel_id=1, source_target_pairs={{0,1},{1,2},{2,3},{4,5},{5,6},{6,7},{8,9},{9,10},{10,11},{12,13},{... | collective-permute-start | bytes 1572872 | tf_op jit(solution)/shard_map/while/body/eval_jaxpr/ppermute | solution.py:21
  225.4 11.1 %collective-permute-start.1 = (f32[4,128,256]{2,1,0:T(8,128)S(1)}, f32[4,128,256]{2,1,0:T(8,128)S(1)}, u32[]{:S(2)}, u32[]{:S(2)}) collective-permute-start(f32[4,128,256]{2,1,0:T(8,128)S(1)} %get-tuple-element.543), channel_id=1, source_target_pairs={{1,0},{2,1},{3,2},{5,4},{6,5},{7,6},{9,8},{10,9},{11,10},{13,12},{... | collective-permute-start | bytes 1572872 | tf_op jit(solution)/shard_map/while/body/eval_jaxpr/ppermute | solution.py:23
  231.4 5.1 %copy-start.1 = (f32[12,128,256]{2,1,0:T(8,128)S(1)}, f32[12,128,256]{2,1,0:T(8,128)}, u32[]{:S(2)}) copy-start(f32[12,128,256]{2,1,0:T(8,128)} %get-tuple-element.556) | copy-start | bytes 4718596 | tf_op jit(solution)/shard_map/while
  231.4 5.1 %copy-start.2 = (f32[12,128,256]{2,1,0:T(8,128)S(1)}, f32[12,128,256]{2,1,0:T(8,128)}, u32[]{:S(2)}) copy-start(f32[12,128,256]{2,1,0:T(8,128)} %get-tuple-element.555) | copy-start | bytes 4718596 | tf_op jit(solution)/shard_map/while
  248.1 38.9 %copy-start = (f32[4,128,256]{2,1,0:T(8,128)}, f32[4,128,256]{2,1,0:T(8,128)S(1)}, u32[]{:S(2)}) copy-start(f32[4,128,256]{2,1,0:T(8,128)S(1)} %get-tuple-element.332) | copy-start | bytes 1572868
  287.0 11.2 %copy-start.5 = (f32[1,4,128,256]{3,2,1,0:T(8,128)S(1)}, f32[1,4,128,256]{3,2,1,0:T(8,128)}, u32[]{:S(2)}) copy-start(f32[1,4,128,256]{3,2,1,0:T(8,128)} %param.11) | copy-start | bytes 1572868
  (3 other events, 3.2 us)
Sparse Core Ops, SparseCore 0:
  16.6 37.8 all-gather.3
  250.6 36.2 all-gather.5
where the time goes:
time: 309 us; the launch traced here: 306 us
  waiting for transfers between devices  106 us (34%)
  other arithmetic  82.2 us (27%)
  starting transfers between devices  54 us (17%)
  local copies, waits for them, and re-layouts  36.9 us (12%)
  between operations  14.2 us (5%)
  matrix products  11.8 us (4%)
    ppermute x9, waiting for transfers between devices, extended(): lax.ppermute(tail, axis, [(i, (i + 1) % count) for i in range(ends)])  49.1 us
    all_gather x2, waiting for transfers between devices, entering(): pieces = jax.tree.map(lambda part: lax.all_gather(part, axis), value)  36.4 us
    ppermute x9, starting transfers between devices, extended(): lax.ppermute(head, axis, [((i + 1) % count, i) for i in range(ends)])  32.4 us
    select_n x24, other arithmetic, advance(): jnp.where(inside, (wide_rhs + COND * beside_sum(padded_rows)) * wide_inve...  25.3 us
    ppermute x9, starting transfers between devices, extended(): lax.ppermute(tail, axis, [(i, (i + 1) % count) for i in range(ends)])  21.5 us
    ppermute x9, waiting for transfers between devices, extended(): lax.ppermute(head, axis, [((i + 1) % count, i) for i in range(ends)])  20.1 us
    gather x8, local copies, waits for them, and re-layouts, interface_fix(): picked = delta[tile_rows]  14.2 us
    dot_general x8, matrix products, interface_fix(): jnp.einsum('src,sc->sr', blocks, picked, precision=lax.Precision.HIGHEST)  11.8 us
  transfers between devices with their start and end apart: 20, of which 19 were waited for; matrix products, arithmetic and copies ran while one was open for 38% of the time, Pallas kernels for 0%

commit v1 on v0

v1 whole, which is shorter than its diff:
```python
import functools

import jax
import jax.numpy as jnp
from jax import lax
from jax.experimental import pallas as pl
from jax.experimental.pallas import tpu as pltpu
from jax.sharding import PartitionSpec as P

SWEEPS = 4
COND = 1.0
SUB = 8
LANE = 128
STAGES = 4


class Halves(list):
    def start(self):
        for copy in self:
            copy.start()

    def wait(self):
        for copy in self:
            copy.wait()


def steps_kernel(shape, slots, tile, first, with_pack, *refs):
    bricks, width, rows, depth = shape
    planes = bricks * width
    rung = rows // SUB
    half = depth // LANE
    count = bricks * slots
    place, lists = refs[0], refs[1]
    refs = refs[2:]
    if with_pack:
        packs, refs = refs[:bricks], refs[bricks:]
        states = [pack.at[0] for pack in packs]
    else:
        states, packs, refs = refs[:bricks], refs[bricks : 2 * bricks], refs[2 * bricks :]
    blocks, refs = refs[:bricks], refs[bricks:]
    outs, refs = refs[:bricks], refs[bricks:]
    stage, field, other, source, capacity, inverse, rhs, kept, picked, fixes, held, stage_sem, held_sem = refs
    steps = blocks[0].shape[0]
    all_steps = lists.shape[0] // (bricks * (slots + 1))

    def fetch_blocks(step, slot):
        return [
            pltpu.make_async_copy(blocks[i].at[step], held.at[slot, place[i]], held_sem.at[slot, i])
            for i in range(bricks)
        ]

    for copy in fetch_blocks(0, 0):
        copy.start()

    loads = []
    for i in range(bricks):
        loads.append((packs[i].at[2], capacity, i))
        loads.append((packs[i].at[1], source, i))
        loads.append((states[i], field, i))

    def halves(whole, n, inward):
        copies = Halves()
        for h in range(half):
            there, here = whole.at[:, :, pl.ds(h * LANE, LANE)], stage.at[n % STAGES, h]
            ends = (there, here) if inward else (here, there)
            copies.append(pltpu.make_async_copy(*ends, stage_sem.at[n % STAGES, h]))
        return copies

    def load_copy(n):
        return halves(loads[n][0], n, True)

    for n in range(min(STAGES, len(loads))):
        load_copy(n).start()
    zero = jnp.zeros((rung, SUB, depth), jnp.float32)
    for edge in (0, planes + 1):
        field[edge] = zero
        other[edge] = zero
    for n, (_, target, i) in enumerate(loads):
        load_copy(n).wait()
        offset = 1 if target is field else 0
        first_plane = place[i] * width + offset

        def spread(x, _, n=n, target=target, first_plane=first_plane):
            for r in range(rung):
                for h in range(half):
                    lanes = pl.ds(h * LANE, LANE)
                    value = stage[n % STAGES, h, x, pl.ds(r, SUB, stride=rung), :]
                    target[first_plane + x, r, :, lanes] = value
                    if target is capacity:
                        inverse[first_plane + x, r, :, lanes] = 1.0 / (value + 6.0 * COND)
            return 0

        lax.fori_loop(0, width, spread, 0)
        if n + STAGES < len(loads):
            load_copy(n + STAGES).start()

    lane = lax.broadcasted_iota(jnp.int32, (SUB, LANE), 1)
    low, high = lane == 0, lane == LANE - 1
    sub = lax.broadcasted_iota(jnp.int32, (SUB, LANE), 0)
    top, bottom = sub == 0, sub == SUB - 1

    def sweep(src, dst, opening):
        def plane(x, _):
            center = [[src[x + 1, r, :, pl.ds(h * LANE, LANE)] for h in range(half)] for r in range(rung)]
            for r in range(rung):
                row = center[r]
                lefts = [pltpu.roll(v, 1, 1) for v in row]
                rights = [pltpu.roll(v, LANE - 1, 1) for v in row]
                for h in range(half):
                    lanes = pl.ds(h * LANE, LANE)
                    left = jnp.where(low, lefts[h - 1] if h else 0.0, lefts[h])
                    right = jnp.where(high, rights[h + 1] if h + 1 < half else 0.0, rights[h])
                    if r:
                        above = center[r - 1][h]
                    else:
                        above = jnp.where(top, 0.0, pltpu.roll(center[rung - 1][h], 1, 0))
                    if r + 1 < rung:
                        below = center[r + 1][h]
                    else:
                        below = jnp.where(bottom, 0.0, pltpu.roll(center[0][h], SUB - 1, 0))
                    total = (src[x, r, :, lanes] + src[x + 2, r, :, lanes]) + (above + below) + (left + right)
                    if opening:
                        base = capacity[x, r, :, lanes] * row[h] + source[x, r, :, lanes]
                        rhs[x, r, :, lanes] = base
                    else:
                        base = rhs[x, r, :, lanes]
                    dst[x + 1, r, :, lanes] = (base + COND * total) * inverse[x, r, :, lanes]
            return 0

        lax.fori_loop(0, planes, plane, 0)

    quarter = lax.broadcasted_iota(jnp.int32, (1, depth), 1) // tile
    per_row = depth // tile
    tile_lane = lax.broadcasted_iota(jnp.int32, (1, LANE), 1)
    group = LANE // tile

    def cell_of(step, b, s):
        at = (b * all_steps + first + step) * (slots + 1)
        t = lists[at + s]
        live = s < lists[at + slots]
        line = t // per_row
        x, y = line // rows, line % rows
        part = jnp.where(live, t % per_row, -1)
        return b * width + x + 1, y % rung, y // rung, part

    def one_step(step, _):
        slot = step % 2

        @pl.when(step + 1 < steps)
        def _():
            for copy in fetch_blocks(step + 1, 1 - slot):
                copy.start()

        def keep(b, _):
            for s in range(slots):
                x, r, u, _unused = cell_of(step, b, s)
                kept[pl.ds(b * slots + s, 1), :] = field[x, r, pl.ds(u, 1), :]
            return 0

        lax.fori_loop(0, bricks, keep, 0)
        sweep(field, other, True)
        for _pair in range((SWEEPS - 2) // 2):
            sweep(other, field, False)
            sweep(field, other, False)
        sweep(other, field, False)

        def pick(b, _):
            for s in range(slots):
                x, r, u, part = cell_of(step, b, s)
                n = b * slots + s
                delta = field[x, r, pl.ds(u, 1), :] - kept[pl.ds(n, 1), :]
                delta = jnp.where(quarter == part, delta, 0.0)
                folded = delta[:, :LANE]
                for h in range(1, half):
                    folded = folded + delta[:, h * LANE : (h + 1) * LANE]
                whole = folded
                for g in range(1, group):
                    whole = whole + pltpu.roll(folded, g * tile, 1)
                picked[pl.ds(n, 1), :] = whole
            return 0

        lax.fori_loop(0, bricks, pick, 0)
        for copy in fetch_blocks(step, slot):
            copy.wait()

        def multiply(b, columns):
            for s in range(slots):
                n = b * slots + s
                products = held[slot, b, s] * picked[pl.ds(n, 1), :]
                parts = [
                    jnp.sum(jnp.where(tile_lane // tile == g, products, 0.0), axis=1, keepdims=True)
                    for g in range(group)
                ]
                column = jnp.concatenate(parts, axis=0)
                columns = jnp.where(tile_lane == n, column, columns)
            return columns

        columns = lax.fori_loop(0, bricks, multiply, jnp.zeros((tile, LANE), jnp.float32))
        fixes[...] = jnp.concatenate([columns] * group, axis=0).T

        def apply(b, _):
            for s in range(slots):
                x, r, u, part = cell_of(step, b, s)
                fix = fixes[pl.ds(b * slots + s, 1), :]
                fix = jnp.where(quarter == part, jnp.concatenate([fix] * half, axis=1), 0.0)
                field[x, r, pl.ds(u, 1), :] = field[x, r, pl.ds(u, 1), :] + fix
            return 0

        lax.fori_loop(0, bricks, apply, 0)
        return 0

    lax.fori_loop(0, steps, one_step, 0)

    def store_copy(i):
        return halves(outs[i], i, False)

    for i in range(bricks):
        if i >= STAGES:
            store_copy(i - STAGES).wait()
        first_plane = place[i] * width + 1

        def gather(x, _, i=i, first_plane=first_plane):
            for r in range(rung):
                for h in range(half):
                    lanes = pl.ds(h * LANE, LANE)
                    stage[i % STAGES, h, x, pl.ds(r, SUB, stride=rung), :] = field[first_plane + x, r, :, lanes]
            return 0

        lax.fori_loop(0, width, gather, 0)
        store_copy(i).start()
    for i in range(max(0, bricks - STAGES), bricks):
        store_copy(i).wait()


def run_steps(place, lists, states, packs, blocks, first, slots, tile):
    with_pack = states is None
    bricks = len(packs)
    _, width, rows, depth = packs[0].shape
    planes, rung = bricks * width, rows // SUB
    steps = blocks[0].shape[0]
    count = bricks * slots
    body = functools.partial(steps_kernel, (bricks, width, rows, depth), slots, tile, first, with_pack)
    smem = pl.BlockSpec(memory_space=pltpu.SMEM)
    hbm = pl.BlockSpec(memory_space=pl.ANY)
    operands = ([] if with_pack else list(states)) + list(packs) + list(blocks)
    grid_shape = (planes, rung, SUB, depth)
    wide_shape = (planes + 2, rung, SUB, depth)
    packed = blocks[0].shape[2:]
    cells = planes * rows * depth
    return pl.pallas_call(
        body,
        out_shape=[jax.ShapeDtypeStruct((width, rows, depth), jnp.float32)] * bricks,
        in_specs=[smem, smem] + [hbm] * len(operands),
        out_specs=[hbm] * bricks,
        scratch_shapes=[
            pltpu.VMEM((STAGES, depth // LANE, width, rows, LANE), jnp.float32),
            pltpu.VMEM(wide_shape, jnp.float32),
            pltpu.VMEM(wide_shape, jnp.float32),
            pltpu.VMEM(grid_shape, jnp.float32),
            pltpu.VMEM(grid_shape, jnp.float32),
            pltpu.VMEM(grid_shape, jnp.float32),
            pltpu.VMEM(grid_shape, jnp.float32),
            pltpu.VMEM((count, depth), jnp.float32),
            pltpu.VMEM((count, LANE), jnp.float32),
            pltpu.VMEM((LANE, LANE), jnp.float32),
            pltpu.VMEM((2, bricks, slots) + packed, jnp.float32),
            pltpu.SemaphoreType.DMA((STAGES, depth // LANE)),
            pltpu.SemaphoreType.DMA((2, bricks)),
        ],
        compiler_params=pltpu.CompilerParams(vmem_limit_bytes=60 * 1024 * 1024),
        cost_estimate=pl.CostEstimate(
            flops=cells * steps * SWEEPS * 10, bytes_accessed=cells * 4 * steps * 8, transcendentals=0
        ),
    )(place, lists, *operands)


def routes(windows, bricks):
    home = bricks // 2 - 1
    others = [z for z in range(bricks) if z != home]

    def at(t, z):
        return t * bricks + (z if t % 2 == 0 else bricks - 1 - z)

    rounds = [[(at(t, z), at(t, home)) for t in range(windows)] for z in others]
    return home, others, rounds


def shards(
    opening_guess_profile,
    capacity,
    thermal_forcing,
    rough_decay_factor,
    tile_ids,
    tile_count,
    tile_blocks,
):
    axes = ("tm", "space")
    windows, bricks = lax.axis_size("tm"), lax.axis_size("space")
    window, brick = lax.axis_index("tm"), lax.axis_index("space")
    opening = opening_guess_profile[0]
    rough = rough_decay_factor[0]
    width, rows, depth = opening.shape
    steps, slots = tile_ids.shape
    tile = tile_blocks.shape[-1]
    home, others, rounds = routes(windows, bricks)
    place = jnp.array([home] + others, jnp.int32)
    place = jnp.where(window % 2 == 0, place, bricks - 1 - place)

    lists = lax.all_gather(jnp.concatenate([tile_ids, tile_count], axis=1), "space").reshape(-1)
    pack = jnp.stack([opening, thermal_forcing[0], capacity])
    group = LANE // tile
    share = tile // group
    blocks = jnp.concatenate([tile_blocks[:, :, g * share : (g + 1) * share] for g in range(group)], axis=-1)
    early = steps // 2

    def spread(value):
        return [lax.ppermute(value, axes, pairs) for pairs in rounds]

    packs = spread(pack)
    blocks_early = spread(blocks[:early])
    states = run_steps(
        place, lists, None, [pack] + packs, [blocks[:early]] + blocks_early, 0, slots, tile
    )
    late, _ = lax.optimization_barrier((blocks[early:], packs[-1]))
    blocks_late = spread(late)
    states = run_steps(place, lists, states, [pack] + packs, [late] + blocks_late, early, slots, tile)

    held_here = brick == place[0]
    ending = jnp.where(held_here, states[0], 0.0)
    for pairs, state in zip(rounds, states[1:]):
        ending = ending + lax.ppermute(state, axes, [(b, a) for a, b in pairs])

    def swap(value):
        parts = value.reshape(windows, -1, depth)
        return lax.all_to_all(parts, "tm", 0, 0, tiled=True)

    factors = swap(rough)
    shift = jnp.where(window == 0, ending, ending - rough * opening)
    shifts = swap(shift)
    x = shifts[0]
    arrived = [x]
    for j in range(1, windows):
        arrived.append(x)
        x = factors[j] * x + shifts[j]
    result = swap(jnp.stack(arrived)).reshape(width, rows, depth)
    updated = jnp.where(window == 0, opening, result)
    return (updated[None], ending[None])


def solution(mesh):
    in_specs = (
        P("tm", "space", None, None),
        P("space", None, None),
        P("tm", "space", None, None),
        P("tm", "space", None, None),
        P("tm", "space"),
        P("tm", "space"),
        P("tm", "space", None, None),
    )
    out_specs = (P("tm", "space", None, None), P("tm", "space", None, None))
    return jax.shard_map(shards, mesh=mesh, in_specs=in_specs, out_specs=out_specs, check_vma=False)
```

time: 309 us -> 249 us (0.81)
  Pallas kernels: 0 us -> 110 us
  other arithmetic: 82.2 us -> 6.56 us
  waiting for transfers between devices: 106 us -> 61.5 us
  blocking collectives: 0 us -> 43.6 us
  local copies, waits for them, and re-layouts: 36.9 us -> 1.09 us
  starting transfers between devices: 54 us -> 21.4 us
  between operations: 14.2 us -> 1.03 us
  matrix products: 11.8 us -> 0 us
    pallas_call x0 -> x2, Pallas kernels: none -> 110 us  [run_steps(): pl.pallas_call(body, out_shape=[jax.ShapeDtypeStruct((width, rows, depth)...]
    select_n x41 -> x3, other arithmetic: 45.2 us -> 3.57 us  [the longest x1 2.2 us: shards(): shift = jnp.where(window == 0, ending, ending - rough * opening)]
    all_gather x2 -> x0, waiting for transfers between devices: 36.4 us -> none  [entering(): pieces = jax.tree.map(lambda part: lax.all_gather(part, axis), value)]
    ppermute x18 -> x12, starting transfers between devices: 53.9 us -> 17.9 us  [the longest x9 11.6 us: spread(): return [lax.ppermute(value, axes, pairs) for pairs in rounds]]
    all_to_all x0 -> x2, blocking collectives: none -> 25.4 us  [swap(): return lax.all_to_all(parts, 'tm', 0, 0, tiled=True)]
    all_gather x0 -> x1, blocking collectives: none -> 18.2 us  [shards(): lax.all_gather(jnp.concatenate([tile_ids, tile_count], axis=1), 'space')]
    ppermute x18 -> x12, waiting for transfers between devices: 69.2 us -> 51.9 us  [the longest x9 41.5 us: spread(): return [lax.ppermute(value, axes, pairs) for pairs in rounds]]
    gather x8 -> x0, local copies, waits for them, and re-layouts: 14.2 us -> none  [interface_fix(): picked = delta[tile_rows]]
  transfers between devices with their start and end apart: 20 -> 13, of which waited for: 19 -> 8; matrix products, arithmetic and copies ran while one was open for 38% -> 1% of each run, Pallas kernels for 0% -> 22%
where the time goes in v1:
time: 249 us; the launch traced here: 245 us
  Pallas kernels  110 us (44%)
  waiting for transfers between devices  61.5 us (25%)
  blocking collectives  43.6 us (18%)
  starting transfers between devices  21.4 us (9%)
  other arithmetic  6.56 us (3%)
    pallas_call x2, Pallas kernels, run_steps(): pl.pallas_call(body, out_shape=[jax.ShapeDtypeStruct((width, rows, depth)...  110 us
    ppermute x9, waiting for transfers between devices, spread(): return [lax.ppermute(value, axes, pairs) for pairs in rounds]  41.5 us
    all_to_all x2, blocking collectives, swap(): return lax.all_to_all(parts, 'tm', 0, 0, tiled=True)  25.4 us
    all_gather x1, blocking collectives, shards(): lax.all_gather(jnp.concatenate([tile_ids, tile_count], axis=1), 'space')  18.2 us
    ppermute x9, starting transfers between devices, spread(): return [lax.ppermute(value, axes, pairs) for pairs in rounds]  11.6 us
    ppermute x3, waiting for transfers between devices, shards(): ending = ending + lax.ppermute(state, axes, [(b, a) for a, b in pairs])  10.3 us
    all_to_all x1, waiting for transfers between devices, swap(): return lax.all_to_all(parts, 'tm', 0, 0, tiled=True)  9.65 us
    ppermute x3, starting transfers between devices, shards(): ending = ending + lax.ppermute(state, axes, [(b, a) for a, b in pairs])  6.32 us
  transfers between devices with their start and end apart: 13, of which 8 were waited for; matrix products, arithmetic and copies ran while one was open for 1% of the time, Pallas kernels for 22%

profile of v1, /device:TPU:8, one launch (start us, length us, event | category | flops | bytes accessed | tf_op | source)
XLA Modules:
  0.0 245.5 jit_solution(4712782725968188714)
XLA Ops:
  0.6 0.0 copy-start.3
  0.6 1.7 pad_maximum_fusion.refs_2_.refs_6_
  2.3 0.0 copy-start
  2.3 1.3 collective-permute-start.2
  3.6 1.3 collective-permute-start
  4.9 1.3 collective-permute-start.1
  6.2 0.0 copy-done.3
  6.2 0.2 fusion.2
  6.5 0.0 copy-start.10
  6.5 0.0 copy-start.9
  6.5 0.0 copy-start.11
  6.5 0.0 copy-start.12
  6.6 1.1 pad_maximum_fusion.1
  7.7 1.3 collective-permute-start.3
  9.0 1.3 collective-permute-start.4
  10.3 31.9 %collective-permute-done.2.refs_5_.refs_9_ = f32[3,4,128,256]{3,2,1,0:T(8,128)S(1)} collective-permute-done((f32[3,4,128,256]{3,2,1,0:T(8,128)S(1)}, f32[3,4,128,256]{3,2,1,0:T(8,128)S(1)}, u32[]{:S(2)}, u32[]{:S(2)}) %collective-permute-start.2) | collective-permute-done | bytes 1572896 | tf_op jit(solution)/shard_map/ppermute | solution.py:317
  42.1 1.3 collective-permute-start.5
  43.4 5.4 %collective-permute-done.3.refs_7_ = f32[4,8,32,128]{3,2,1,0:T(8,128)S(1)} collective-permute-done((f32[4,8,32,128]{3,2,1,0:T(8,128)S(1)}, f32[4,8,32,128]{3,2,1,0:T(8,128)S(1)}, u32[]{:S(2)}, u32[]{:S(2)}) %collective-permute-start.3) | collective-permute-done | bytes 524320 | tf_op jit(solution)/shard_map/ppermute | solution.py:317
  48.8 1.3 collective-permute-start.6
  50.1 2.9 %collective-permute-done.4.refs_8_ = f32[4,8,32,128]{3,2,1,0:T(8,128)S(1)} collective-permute-done((f32[4,8,32,128]{3,2,1,0:T(8,128)S(1)}, f32[4,8,32,128]{3,2,1,0:T(8,128)S(1)}, u32[]{:S(2)}, u32[]{:S(2)}) %collective-permute-start.4) | collective-permute-done | bytes 524320 | tf_op jit(solution)/shard_map/ppermute | solution.py:317
  53.0 1.3 collective-permute-start.7
  54.3 1.4 collective-permute-done.5.refs_9_
  55.7 1.3 collective-permute-start.8
  57.0 0.1 copy.11
  57.1 0.1 pad_add_fusion
  57.2 18.2 %all-gather = s32[32,9]{1,0:T(8,128)S(1)} all-gather(s32[8,9]{1,0:T(8,128)S(1)} %pad_add_fusion), channel_id=2, replica_groups=mesh['tm'=8,'space'=4] {'space'}, dimensions={0}, use_global_device_ids=true | all-gather | bytes 1440 | tf_op jit(solution)/shard_map/all_gather | solution.py:309
  75.4 0.7 reshape.15.refs_1_
  76.1 0.5 broadcast_select_fusion.1.refs_0_
  76.6 0.0 collective-permute-done.refs_3_.refs_7_
  76.6 0.0 collective-permute-done.1.refs_4_.refs_8_
  76.6 55.1 %shard_map.95 = (f32[4,128,256]{2,1,0:T(8,128)}, f32[4,128,256]{2,1,0:T(8,128)}, f32[4,128,256]{2,1,0:T(8,128)}, f32[4,128,256]{2,1,0:T(8,128)}) custom-call(s32[4]{0:T(128)} %broadcast_select_fusion.1.refs_0_, s32[288]{0:T(512)} %reshape.15.refs_1_, f32[3,4,128,256]{3,2,1,0:T(8,128)} %copy-done, f32[3,4,128,256]{3,2,1,0:T(8,128)} %collective-permute-done.refs_3_.refs_7_, ...), custom_call_target="tpu_custom_call" | custom-call | flops 83886080 | bytes 67108864 | tf_op jit(solution)/shard_map/pallas_call | solution.py:250
  131.7 0.0 collective-permute-done.6.refs_11_
  131.7 0.0 collective-permute-done.7.refs_12_
  131.7 0.0 collective-permute-done.8.refs_13_
  131.8 0.0 copy-start.2
  131.8 55.2 %shard_map.96 = (f32[4,128,256]{2,1,0:T(8,128)}, f32[4,128,256]{2,1,0:T(8,128)}, f32[4,128,256]{2,1,0:T(8,128)}, f32[4,128,256]{2,1,0:T(8,128)}) custom-call(s32[4]{0:T(128)} %broadcast_select_fusion.1.refs_0_, s32[288]{0:T(512)} %reshape.15.refs_1_, f32[4,128,256]{2,1,0:T(8,128)} %get-tuple-element.11.refs_2_, f32[4,128,256]{2,1,0:T(8,128)} %get-tuple-element.12.refs_3_, ...), custom_call_target="tpu_custom_call" | custom-call | flops 83886080 | bytes 67108864 | tf_op jit(solution)/shard_map/pallas_call | solution.py:250
  187.0 2.2 collective-permute-start.10
  189.2 2.8 %collective-permute-start.11 = (f32[4,128,256]{2,1,0:T(8,128)}, f32[4,128,256]{2,1,0:T(8,128)S(1)}, u32[]{:S(2)}, u32[]{:S(2)}) collective-permute-start(f32[4,128,256]{2,1,0:T(8,128)} %get-tuple-element.19), channel_id=1, source_target_pairs={{1,3},{6,4},{9,11},{14,12},{17,19},{22,20},{25,27},{30,28}} | collective-permute-start | bytes 1572872 | tf_op jit(solution)/shard_map/ppermute | solution.py:331
  192.0 1.3 collective-permute-start.9
  193.4 2.8 %collective-permute-done.10 = f32[4,128,256]{2,1,0:T(8,128)S(1)} collective-permute-done((f32[4,128,256]{2,1,0:T(8,128)}, f32[4,128,256]{2,1,0:T(8,128)S(1)}, u32[]{:S(2)}, u32[]{:S(2)}) %collective-permute-start.10) | collective-permute-done | bytes 524320 | tf_op jit(solution)/shard_map/ppermute | solution.py:331
  196.2 5.6 %collective-permute-done.11 = f32[4,128,256]{2,1,0:T(8,128)S(1)} collective-permute-done((f32[4,128,256]{2,1,0:T(8,128)}, f32[4,128,256]{2,1,0:T(8,128)S(1)}, u32[]{:S(2)}, u32[]{:S(2)}) %collective-permute-start.11) | collective-permute-done | bytes 524320 | tf_op jit(solution)/shard_map/ppermute | solution.py:331
  201.8 1.9 collective-permute-done.9
  203.7 2.2 subtract_select_fusion
  205.9 13.3 %all_to_all.15 = f32[8,64,256]{2,1,0:T(8,128)S(1)} all-to-all(f32[8,64,256]{2,1,0:T(8,128)S(1)} %bitcast.9), channel_id=1, replica_groups=mesh['tm'=8,'space'=4] {'tm'}, dimensions={0} | all-to-all | bytes 1048576 | tf_op jit(solution)/shard_map/all_to_all | solution.py:335
  219.1 3.5 %all-to-all-start.1 = ((f32[8,64,256]{2,1,0:T(8,128)}), f32[8,64,256]{2,1,0:T(8,128)S(1)}, u32[]{:S(2)}, u32[]{:S(2)}) async-start(f32[8,64,256]{2,1,0:T(8,128)} %bitcast.4), calls=%async_computation.1 | async-start | bytes 1048576 | tf_op jit(solution)/shard_map/all_to_all | solution.py:335
  222.7 9.6 %all-to-all-done.1 = f32[8,64,256]{2,1,0:T(8,128)S(1)} async-done(((f32[8,64,256]{2,1,0:T(8,128)}), f32[8,64,256]{2,1,0:T(8,128)S(1)}, u32[]{:S(2)}, u32[]{:S(2)}) %all-to-all-start.1) | async-done | bytes 524320 | tf_op jit(solution)/shard_map/all_to_all | solution.py:335
  232.5 12.2 %all_to_all.16 = f32[8,64,256]{2,1,0:T(8,128)S(1)} all-to-all(f32[8,64,256]{2,1,0:T(8,128)S(1)} %fusion.1), channel_id=1, replica_groups=mesh['tm'=8,'space'=4] {'tm'}, dimensions={0} | all-to-all | bytes 1048576 | tf_op jit(solution)/shard_map/all_to_all | solution.py:335
  244.6 0.9 broadcast_select_fusion
  (26 shorter events, 0.2 us)
Async XLA Ops:
  0.6 5.6 %copy-start.3 = (f32[8,8,64,64]{3,2,1,0:T(8,128)S(1)}, f32[8,8,64,64]{3,2,1,0:T(8,128)}, u32[]{:S(2)}) copy-start(f32[8,8,64,64]{3,2,1,0:T(8,128)} %param.14) | copy-start | bytes 3145732
  2.3 4.2 %copy-start = (f32[3,4,128,256]{3,2,1,0:T(8,128)}, f32[3,4,128,256]{3,2,1,0:T(8,128)S(1)}, u32[]{:S(2)}) copy-start(f32[3,4,128,256]{3,2,1,0:T(8,128)S(1)} %pad_maximum_fusion.refs_2_.refs_6_) | copy-start | bytes 4718596
  2.3 39.8 %collective-permute-start.2 = (f32[3,4,128,256]{3,2,1,0:T(8,128)S(1)}, f32[3,4,128,256]{3,2,1,0:T(8,128)S(1)}, u32[]{:S(2)}, u32[]{:S(2)}) collective-permute-start(f32[3,4,128,256]{3,2,1,0:T(8,128)S(1)} %pad_maximum_fusion.refs_2_.refs_6_), channel_id=1, source_target_pairs={{3,1},{4,6},{11,9},{12,14},{19,17},{20,22},{27,25},{28,30}} | collective-permute-start | bytes 4718600 | tf_op jit(solution)/shard_map/ppermute | solution.py:317
  3.6 73.0 %collective-permute-start = (f32[3,4,128,256]{3,2,1,0:T(8,128)S(1)}, f32[3,4,128,256]{3,2,1,0:T(8,128)}, u32[]{:S(2)}, u32[]{:S(2)}) collective-permute-start(f32[3,4,128,256]{3,2,1,0:T(8,128)S(1)} %pad_maximum_fusion.refs_2_.refs_6_), channel_id=1, source_target_pairs={{0,1},{7,6},{8,9},{15,14},{16,17},{23,22},{24,25},{31,30}} | collective-permute-start | bytes 4718600 | tf_op jit(solution)/shard_map/ppermute | solution.py:317
  4.9 71.7 %collective-permute-start.1 = (f32[3,4,128,256]{3,2,1,0:T(8,128)S(1)}, f32[3,4,128,256]{3,2,1,0:T(8,128)}, u32[]{:S(2)}, u32[]{:S(2)}) collective-permute-start(f32[3,4,128,256]{3,2,1,0:T(8,128)S(1)} %pad_maximum_fusion.refs_2_.refs_6_), channel_id=1, source_target_pairs={{2,1},{5,6},{10,9},{13,14},{18,17},{21,22},{26,25},{29,30}} | collective-permute-start | bytes 4718600 | tf_op jit(solution)/shard_map/ppermute | solution.py:317
  6.5 50.5 %copy-start.10 = (s32[8,1]{0,1:T(1,128)S(1)}, s32[8,1]{0,1:T(1,128)}, u32[]{:S(2)}) copy-start(s32[8,1]{0,1:T(1,128)} %param.13) | copy-start | bytes 100
  6.5 50.6 %copy-start.9 = (s32[8,8]{1,0:T(8,128)S(1)}, s32[8,8]{1,0:T(8,128)}, u32[]{:S(2)}) copy-start(s32[8,8]{1,0:T(8,128)} %param.12) | copy-start | bytes 772
  6.5 69.6 %copy-start.11 = (s32[4]{0:T(128)S(1)}, s32[4]{0:T(128)}, u32[]{:S(2)}) copy-start(s32[4]{0:T(128)} %constant.29.clone) | copy-start | bytes 52
  6.5 69.5 %copy-start.12 = (s32[4]{0:T(128)S(1)}, s32[4]{0:T(128)}, u32[]{:S(2)}) copy-start(s32[4]{0:T(128)} %constant.35) | copy-start | bytes 52
  7.7 34.5 %copy-start.4 = (f32[4,8,32,128]{3,2,1,0:T(8,128)}, f32[4,8,32,128]{3,2,1,0:T(8,128)S(1)}, u32[]{:S(2)}) copy-start(f32[4,8,32,128]{3,2,1,0:T(8,128)S(1)} %get-tuple-element.29.refs_6_) | copy-start | bytes 1572868
  7.7 41.2 %collective-permute-start.3 = (f32[4,8,32,128]{3,2,1,0:T(8,128)S(1)}, f32[4,8,32,128]{3,2,1,0:T(8,128)S(1)}, u32[]{:S(2)}, u32[]{:S(2)}) collective-permute-start(f32[4,8,32,128]{3,2,1,0:T(8,128)S(1)} %get-tuple-element.29.refs_6_), channel_id=1, source_target_pairs={{0,1},{7,6},{8,9},{15,14},{16,17},{23,22},{24,25},{31,30}} | collective-permute-start | bytes 1572872 | tf_op jit(solution)/shard_map/ppermute | solution.py:317
  9.0 44.1 %collective-permute-start.4 = (f32[4,8,32,128]{3,2,1,0:T(8,128)S(1)}, f32[4,8,32,128]{3,2,1,0:T(8,128)S(1)}, u32[]{:S(2)}, u32[]{:S(2)}) collective-permute-start(f32[4,8,32,128]{3,2,1,0:T(8,128)S(1)} %get-tuple-element.29.refs_6_), channel_id=1, source_target_pairs={{2,1},{5,6},{10,9},{13,14},{18,17},{21,22},{26,25},{29,30}} | collective-permute-start | bytes 1572872 | tf_op jit(solution)/shard_map/ppermute | solution.py:317
  42.1 34.5 %copy-start.1 = (f32[3,4,128,256]{3,2,1,0:T(8,128)}, f32[3,4,128,256]{3,2,1,0:T(8,128)S(1)}, u32[]{:S(2)}) copy-start(f32[3,4,128,256]{3,2,1,0:T(8,128)S(1)} %collective-permute-done.2.refs_5_.refs_9_) | copy-start | bytes 4718596
  42.1 13.5 %collective-permute-start.5 = (f32[4,8,32,128]{3,2,1,0:T(8,128)S(1)}, f32[4,8,32,128]{3,2,1,0:T(8,128)S(1)}, u32[]{:S(2)}, u32[]{:S(2)}) collective-permute-start(f32[4,8,32,128]{3,2,1,0:T(8,128)S(1)} %get-tuple-element.29.refs_6_), channel_id=1, source_target_pairs={{3,1},{4,6},{11,9},{12,14},{19,17},{20,22},{27,25},{28,30}} | collective-permute-start | bytes 1572872 | tf_op jit(solution)/shard_map/ppermute | solution.py:317
  48.8 6.8 %copy-start.5 = (f32[4,8,32,128]{3,2,1,0:T(8,128)}, f32[4,8,32,128]{3,2,1,0:T(8,128)S(1)}, u32[]{:S(2)}) copy-start(f32[4,8,32,128]{3,2,1,0:T(8,128)S(1)} %collective-permute-done.3.refs_7_) | copy-start | bytes 1572868
  48.8 82.9 %collective-permute-start.6 = (f32[4,8,32,128]{3,2,1,0:T(8,128)}, f32[4,8,32,128]{3,2,1,0:T(8,128)}, u32[]{:S(2)}, u32[]{:S(2)}) collective-permute-start(f32[4,8,32,128]{3,2,1,0:T(8,128)} %get-tuple-element.15.refs_10_), channel_id=1, source_target_pairs={{0,1},{7,6},{8,9},{15,14},{16,17},{23,22},{24,25},{31,30}} | collective-permute-start | bytes 1572872 | tf_op jit(solution)/shard_map/ppermute | solution.py:317
  53.0 3.9 %copy-start.6 = (f32[4,8,32,128]{3,2,1,0:T(8,128)}, f32[4,8,32,128]{3,2,1,0:T(8,128)S(1)}, u32[]{:S(2)}) copy-start(f32[4,8,32,128]{3,2,1,0:T(8,128)S(1)} %collective-permute-done.4.refs_8_) | copy-start | bytes 1572868
  53.0 78.7 %collective-permute-start.7 = (f32[4,8,32,128]{3,2,1,0:T(8,128)}, f32[4,8,32,128]{3,2,1,0:T(8,128)}, u32[]{:S(2)}, u32[]{:S(2)}) collective-permute-start(f32[4,8,32,128]{3,2,1,0:T(8,128)} %get-tuple-element.15.refs_10_), channel_id=1, source_target_pairs={{2,1},{5,6},{10,9},{13,14},{18,17},{21,22},{26,25},{29,30}} | collective-permute-start | bytes 1572872 | tf_op jit(solution)/shard_map/ppermute | solution.py:317
  55.7 1.3 copy-start.7
  55.7 76.1 %collective-permute-start.8 = (f32[4,8,32,128]{3,2,1,0:T(8,128)}, f32[4,8,32,128]{3,2,1,0:T(8,128)}, u32[]{:S(2)}, u32[]{:S(2)}) collective-permute-start(f32[4,8,32,128]{3,2,1,0:T(8,128)} %get-tuple-element.15.refs_10_), channel_id=1, source_target_pairs={{3,1},{4,6},{11,9},{12,14},{19,17},{20,22},{27,25},{28,30}} | collective-permute-start | bytes 1572872 | tf_op jit(solution)/shard_map/ppermute | solution.py:317
  131.8 61.6 %copy-start.8 = (s32[4]{0:T(128)S(1)}, s32[4]{0:T(128)}, u32[]{:S(2)}) copy-start(s32[4]{0:T(128)} %broadcast_select_fusion.1.refs_0_) | copy-start | bytes 52
  131.8 71.9 %copy-start.2 = (f32[1,4,128,256]{3,2,1,0:T(8,128)S(1)}, f32[1,4,128,256]{3,2,1,0:T(8,128)}, u32[]{:S(2)}) copy-start(f32[1,4,128,256]{3,2,1,0:T(8,128)} %param.8) | copy-start | bytes 1572868
  187.0 9.2 %collective-permute-start.10 = (f32[4,128,256]{2,1,0:T(8,128)}, f32[4,128,256]{2,1,0:T(8,128)S(1)}, u32[]{:S(2)}, u32[]{:S(2)}) collective-permute-start(f32[4,128,256]{2,1,0:T(8,128)} %get-tuple-element.18), channel_id=1, source_target_pairs={{1,2},{6,5},{9,10},{14,13},{17,18},{22,21},{25,26},{30,29}} | collective-permute-start | bytes 1572872 | tf_op jit(solution)/shard_map/ppermute | solution.py:331
  189.2 12.6 %collective-permute-start.11 = (f32[4,128,256]{2,1,0:T(8,128)}, f32[4,128,256]{2,1,0:T(8,128)S(1)}, u32[]{:S(2)}, u32[]{:S(2)}) collective-permute-start(f32[4,128,256]{2,1,0:T(8,128)} %get-tuple-element.19), channel_id=1, source_target_pairs={{1,3},{6,4},{9,11},{14,12},{17,19},{22,20},{25,27},{30,28}} | collective-permute-start | bytes 1572872 | tf_op jit(solution)/shard_map/ppermute | solution.py:331
  192.0 11.7 %collective-permute-start.9 = (f32[4,128,256]{2,1,0:T(8,128)}, f32[4,128,256]{2,1,0:T(8,128)S(1)}, u32[]{:S(2)}, u32[]{:S(2)}) collective-permute-start(f32[4,128,256]{2,1,0:T(8,128)} %get-tuple-element.17), channel_id=1, source_target_pairs={{1,0},{6,7},{9,8},{14,15},{17,16},{22,23},{25,24},{30,31}} | collective-permute-start | bytes 1572872 | tf_op jit(solution)/shard_map/ppermute | solution.py:331
  219.1 13.2 %all-to-all-start.1 = ((f32[8,64,256]{2,1,0:T(8,128)}), f32[8,64,256]{2,1,0:T(8,128)S(1)}, u32[]{:S(2)}, u32[]{:S(2)}) async-start(f32[8,64,256]{2,1,0:T(8,128)} %bitcast.4), calls=%async_computation.1 | async-start | bytes 1048576 | tf_op jit(solution)/shard_map/all_to_all | solution.py:335

commit v2 on v1

v2 whole, which is shorter than its diff:
```python
import functools

import jax
import jax.numpy as jnp
from jax import lax
from jax.experimental import pallas as pl
from jax.experimental.pallas import tpu as pltpu
from jax.sharding import PartitionSpec as P

SWEEPS = 4
COND = 1.0
SUB = 8
LANE = 128
EARLY = 3
SPAN = 8


def span_of(planes):
    return max(n for n in range(1, SPAN + 1) if planes % n == 0)


def steps_kernel(shape, slots, tile, first, with_pack, *refs):
    bricks, width, rung, depth = shape
    planes = bricks * width
    half = depth // LANE
    count = bricks * slots
    place, lists = refs[0], refs[1]
    refs = refs[2:]
    if with_pack:
        packs, refs = refs[:bricks], refs[bricks:]
        states = [pack.at[0] for pack in packs]
    else:
        states, packs, refs = refs[:bricks], refs[bricks : 2 * bricks], refs[2 * bricks :]
    blocks, refs = refs[:bricks], refs[bricks:]
    outs, refs = refs[:bricks], refs[bricks:]
    field, other, source, capacity, inverse, rhs, kept, current, picked, fixes, held, load_sem, held_sem = refs
    steps = blocks[0].shape[0]
    all_steps = lists.shape[0] // (count * 4)

    def fetch_blocks(step, slot):
        return [
            pltpu.make_async_copy(blocks[i].at[step], held.at[slot, place[i]], held_sem.at[slot, i])
            for i in range(bricks)
        ]

    loads = []
    for i in range(bricks):
        loads.append((packs[i].at[2], capacity.at[pl.ds(place[i] * width, width)]))
    for i in range(bricks):
        loads.append((states[i], field.at[pl.ds(place[i] * width + 1, width)]))
        loads.append((packs[i].at[1], source.at[pl.ds(place[i] * width, width)]))
    loads = [pltpu.make_async_copy(*ends, load_sem.at[n]) for n, ends in enumerate(loads)]
    for copy in loads:
        copy.start()
    for copy in fetch_blocks(0, 0):
        copy.start()

    zero = jnp.zeros((rung, SUB, depth), jnp.float32)
    for edge in (0, planes + 1):
        field[edge] = zero
        other[edge] = zero
    for copy in loads[:bricks]:
        copy.wait()

    def invert(x, _):
        inverse[x] = 1.0 / (capacity[x] + 6.0 * COND)
        return 0

    lax.fori_loop(0, planes, invert, 0)
    for copy in loads[bricks:]:
        copy.wait()

    sub = lax.broadcasted_iota(jnp.int32, (SUB, LANE), 0)
    top, bottom = sub == 0, sub == SUB - 1
    line = lax.broadcasted_iota(jnp.int32, (depth, depth), 0)
    column = lax.broadcasted_iota(jnp.int32, (depth, depth), 1)
    beside = jnp.where(jnp.abs(line - column) == 1, 1.0, 0.0).astype(jnp.bfloat16)
    span = span_of(planes)

    def split(value):
        coarse = value.astype(jnp.bfloat16)
        return coarse, (value - coarse.astype(jnp.float32)).astype(jnp.bfloat16)

    def product(value, matrix):
        coarse, fine = split(value)
        return jnp.dot(coarse, matrix, preferred_element_type=jnp.float32) + jnp.dot(
            fine, matrix, preferred_element_type=jnp.float32
        )

    def sweep(src, dst, opening):
        def chunk(n, _):
            whole = src[pl.ds(n * span + 1, span)].reshape(span * rung * SUB, depth)
            along = product(whole, beside).reshape(span, rung, SUB, depth)
            for p in range(span):
                x = n * span + p
                center = [[src[x + 1, r, :, pl.ds(h * LANE, LANE)] for h in range(half)] for r in range(rung)]
                for r in range(rung):
                    for h in range(half):
                        lanes = pl.ds(h * LANE, LANE)
                        if r:
                            above = center[r - 1][h]
                        else:
                            above = jnp.where(top, 0.0, pltpu.roll(center[rung - 1][h], 1, 0))
                        if r + 1 < rung:
                            below = center[r + 1][h]
                        else:
                            below = jnp.where(bottom, 0.0, pltpu.roll(center[0][h], SUB - 1, 0))
                        total = src[x, r, :, lanes] + src[x + 2, r, :, lanes]
                        total = total + (above + below) + along[p, r, :, h * LANE : (h + 1) * LANE]
                        if opening:
                            base = capacity[x, r, :, lanes] * center[r][h] + source[x, r, :, lanes]
                            rhs[x, r, :, lanes] = base
                        else:
                            base = rhs[x, r, :, lanes]
                        dst[x + 1, r, :, lanes] = (base + COND * total) * inverse[x, r, :, lanes]
            return 0

        lax.fori_loop(0, planes // span, chunk, 0)

    quarter = lax.broadcasted_iota(jnp.int32, (1, depth), 1) // tile
    group = LANE // tile
    share = tile // group
    from_lane = lax.broadcasted_iota(jnp.int32, (LANE, LANE), 0)
    to_lane = lax.broadcasted_iota(jnp.int32, (LANE, LANE), 1)
    gathers = jnp.where(from_lane // tile == (to_lane % tile) // share, 1.0, 0.0).astype(jnp.bfloat16)
    own_line = lax.broadcasted_iota(jnp.int32, (share, LANE), 0)
    own_lane = lax.broadcasted_iota(jnp.int32, (share, LANE), 1)
    diagonal = own_line == own_lane % share

    def cell_of(step, b, s):
        at = ((b * all_steps + first + step) * slots + s) * 4
        return lists[at], lists[at + 1], lists[at + 2], lists[at + 3]

    def one_step(step, _):
        slot = step % 2

        @pl.when(step + 1 < steps)
        def _():
            for copy in fetch_blocks(step + 1, 1 - slot):
                copy.start()

        def keep(b, _):
            for s in range(slots):
                x, r, u, _unused = cell_of(step, b, s)
                kept[pl.ds(b * slots + s, 1), :] = field[x, r, pl.ds(u, 1), :]
            return 0

        lax.fori_loop(0, bricks, keep, 0)
        sweep(field, other, True)
        for _pair in range((SWEEPS - 2) // 2):
            sweep(other, field, False)
            sweep(field, other, False)
        sweep(other, field, False)

        def pick(b, _):
            for s in range(slots):
                x, r, u, part = cell_of(step, b, s)
                n = b * slots + s
                value = field[x, r, pl.ds(u, 1), :]
                current[pl.ds(n, 1), :] = value
                delta = jnp.where(quarter == part, value - kept[pl.ds(n, 1), :], 0.0)
                folded = delta[:, :LANE]
                for h in range(1, half):
                    folded = folded + delta[:, h * LANE : (h + 1) * LANE]
                whole = folded
                for g in range(1, group):
                    whole = whole + pltpu.roll(folded, g * tile, 1)
                picked[pl.ds(n, 1), :] = whole
            return 0

        lax.fori_loop(0, bricks, pick, 0)
        for copy in fetch_blocks(step, slot):
            copy.wait()

        def multiply(b, _):
            terms = [held[slot, b, s] * picked[pl.ds(b * slots + s, 1), :] for s in range(slots)]
            sums = product(jnp.concatenate(terms, axis=0), gathers)
            for s in range(slots):
                fix = jnp.where(diagonal, sums[s * share : (s + 1) * share], 0.0)
                fixes[pl.ds(b * slots + s, 1), :] = jnp.sum(fix, axis=0, keepdims=True)
            return 0

        lax.fori_loop(0, bricks, multiply, 0)

        def apply(b, _):
            for s in range(slots):
                x, r, u, part = cell_of(step, b, s)
                n = b * slots + s
                fix = jnp.concatenate([fixes[pl.ds(n, 1), :]] * half, axis=1)
                pltpu.store(field.at[x, r, pl.ds(u, 1), :], current[pl.ds(n, 1), :] + fix, mask=quarter == part)
            return 0

        lax.fori_loop(0, bricks, apply, 0)
        return 0

    lax.fori_loop(0, steps, one_step, 0)
    stores = [
        pltpu.make_async_copy(field.at[pl.ds(place[i] * width + 1, width)], outs[i], load_sem.at[i]) for i in range(bricks)
    ]
    for copy in stores:
        copy.start()
    for copy in stores:
        copy.wait()


def run_steps(place, lists, states, packs, blocks, first, slots, tile):
    with_pack = states is None
    bricks = len(packs)
    _, width, rung, _, depth = packs[0].shape
    planes = bricks * width
    steps = blocks[0].shape[0]
    count = bricks * slots
    body = functools.partial(steps_kernel, (bricks, width, rung, depth), slots, tile, first, with_pack)
    smem = pl.BlockSpec(memory_space=pltpu.SMEM)
    hbm = pl.BlockSpec(memory_space=pl.ANY)
    operands = ([] if with_pack else list(states)) + list(packs) + list(blocks)
    grid_shape = (planes, rung, SUB, depth)
    wide_shape = (planes + 2, rung, SUB, depth)
    packed = blocks[0].shape[2:]
    cells = planes * rung * SUB * depth
    return pl.pallas_call(
        body,
        out_shape=[jax.ShapeDtypeStruct((width, rung, SUB, depth), jnp.float32)] * bricks,
        in_specs=[smem, smem] + [hbm] * len(operands),
        out_specs=[hbm] * bricks,
        scratch_shapes=[
            pltpu.VMEM(wide_shape, jnp.float32),
            pltpu.VMEM(wide_shape, jnp.float32),
            pltpu.VMEM(grid_shape, jnp.float32),
            pltpu.VMEM(grid_shape, jnp.float32),
            pltpu.VMEM(grid_shape, jnp.float32),
            pltpu.VMEM(grid_shape, jnp.float32),
            pltpu.VMEM((count, depth), jnp.float32),
            pltpu.VMEM((count, depth), jnp.float32),
            pltpu.VMEM((count, LANE), jnp.float32),
            pltpu.VMEM((count, LANE), jnp.float32),
            pltpu.VMEM((2, bricks, slots) + packed, jnp.float32),
            pltpu.SemaphoreType.DMA((3 * bricks,)),
            pltpu.SemaphoreType.DMA((2, bricks)),
        ],
        compiler_params=pltpu.CompilerParams(vmem_limit_bytes=60 * 1024 * 1024),
        cost_estimate=pl.CostEstimate(
            flops=cells * steps * SWEEPS * 10, bytes_accessed=cells * 4 * steps * 8, transcendentals=0
        ),
    )(place, lists, *operands)


def routes(windows, bricks):
    home = bricks // 2 - 1
    others = [z for z in range(bricks) if z != home]

    def at(t, z):
        return t * bricks + (z if t % 2 == 0 else bricks - 1 - z)

    rounds = [[(at(t, z), at(t, home)) for t in range(windows)] for z in others]
    return home, others, rounds


def shards(
    opening_guess_profile,
    capacity,
    thermal_forcing,
    rough_decay_factor,
    tile_ids,
    tile_count,
    tile_blocks,
):
    axes = ("tm", "space")
    windows, bricks = lax.axis_size("tm"), lax.axis_size("space")
    window, brick = lax.axis_index("tm"), lax.axis_index("space")
    opening = opening_guess_profile[0]
    rough = rough_decay_factor[0]
    width, rows, depth = opening.shape
    steps, slots = tile_ids.shape
    tile = tile_blocks.shape[-1]
    home, others, rounds = routes(windows, bricks)
    place = jnp.array([home] + others, jnp.int32)
    place = jnp.where(window % 2 == 0, place, bricks - 1 - place)

    rung = rows // SUB
    ids = jnp.concatenate([tile_ids, tile_count], axis=1).astype(jnp.float32)
    ids = lax.all_gather(ids, "space").astype(jnp.int32)
    t, live = ids[..., :slots], jnp.arange(slots) < ids[..., slots:]
    per_row = depth // tile
    line = t // per_row
    plane = line // rows + width * jnp.arange(bricks, dtype=jnp.int32)[:, None, None] + 1
    part = jnp.where(live, t % per_row, -1)
    lists = jnp.stack([plane, line % rung, line % rows // rung, part], axis=-1).reshape(-1)

    pack = jnp.stack([opening, thermal_forcing[0], capacity])
    pack = pack.reshape(3, width, SUB, rung, depth).swapaxes(2, 3)
    group = LANE // tile
    share = tile // group
    blocks = jnp.concatenate([tile_blocks[:, :, g * share : (g + 1) * share] for g in range(group)], axis=-1)
    early = EARLY * steps // 8

    def spread(value):
        return [lax.ppermute(value, axes, pairs) for pairs in rounds]

    def swap(value):
        parts = value.reshape(windows, -1, depth)
        return lax.all_to_all(parts, "tm", 0, 0, tiled=True)

    packs = spread(pack)
    blocks_early = spread(blocks[:early])
    factors = swap(rough)
    place, factors = lax.optimization_barrier((place, factors))
    states = run_steps(
        place, lists, None, [pack] + packs, [blocks[:early]] + blocks_early, 0, slots, tile
    )
    late, _ = lax.optimization_barrier((blocks[early:], packs[-1]))
    blocks_late = spread(late)
    states = run_steps(place, lists, states, [pack] + packs, [late] + blocks_late, early, slots, tile)

    held_here = brick == place[0]
    ending = jnp.where(held_here, states[0], 0.0)
    for pairs, state in zip(rounds, states[1:]):
        ending = ending + lax.ppermute(state, axes, [(b, a) for a, b in pairs])

    ending = ending.swapaxes(1, 2).reshape(width, rows, depth)
    shift = jnp.where(window == 0, ending, ending - rough * opening)
    shifts = swap(shift)
    x = shifts[0]
    arrived = [x]
    for j in range(1, windows):
        arrived.append(x)
        x = factors[j] * x + shifts[j]
    result = swap(jnp.stack(arrived)).reshape(width, rows, depth)
    updated = jnp.where(window == 0, opening, result)
    return (updated[None], ending[None])


def solution(mesh):
    in_specs = (
        P("tm", "space", None, None),
        P("space", None, None),
        P("tm", "space", None, None),
        P("tm", "space", None, None),
        P("tm", "space"),
        P("tm", "space"),
        P("tm", "space", None, None),
    )
    out_specs = (P("tm", "space", None, None), P("tm", "space", None, None))
    return jax.shard_map(shards, mesh=mesh, in_specs=in_specs, out_specs=out_specs, check_vma=False)
```

time: 249 us -> 181 us (0.73)
  Pallas kernels: 110 us -> 56.6 us
  waiting for transfers between devices: 61.5 us -> 33.9 us
  local copies, waits for them, and re-layouts: 1.09 us -> 7.75 us
  starting transfers between devices: 21.4 us -> 26.7 us
  other arithmetic: 6.56 us -> 11.3 us
  blocking collectives: 43.6 us -> 40.9 us
    pallas_call x2, Pallas kernels: 110 us -> 56.6 us  [run_steps(): pl.pallas_call(body, out_shape=[jax.ShapeDtypeStruct((width, rung, SUB, d...]
    ppermute x9, waiting for transfers between devices: 41.5 us -> 22.7 us  [spread(): return [lax.ppermute(value, axes, pairs) for pairs in rounds]]
    all_to_all x1, waiting for transfers between devices: 9.65 us -> 0.01 us  [swap(): return lax.all_to_all(parts, 'tm', 0, 0, tiled=True)]
    unnamed x5, other arithmetic: 0.1 us -> 4.37 us
    another operation x0 -> x4, local copies, waits for them, and re-layouts: none -> 4.16 us  [the longest x3 3.07 us: shards(): pack = jnp.stack([opening, thermal_forcing[0], capacity])]
    all_to_all x1, starting transfers between devices: 3.5 us -> 7.6 us  [swap(): return lax.all_to_all(parts, 'tm', 0, 0, tiled=True)]
    all_gather x1, blocking collectives: 18.2 us -> 15.5 us  [shards(): ids = lax.all_gather(ids, 'space').astype(jnp.int32)]
  transfers between devices with their start and end apart: 13 -> 13, of which waited for: 8 -> 3; matrix products, arithmetic and copies ran while one was open for 1% -> 3% of each run, Pallas kernels for 22% -> 13%
where the time goes in v2:
time: 181 us; the launch traced here: 178 us
  Pallas kernels  56.6 us (31%)
  blocking collectives  40.9 us (23%)
  waiting for transfers between devices  33.9 us (19%)
  starting transfers between devices  26.7 us (15%)
  other arithmetic  11.3 us (6%)
  local copies, waits for them, and re-layouts  7.75 us (4%)
    pallas_call x2, Pallas kernels, run_steps(): pl.pallas_call(body, out_shape=[jax.ShapeDtypeStruct((width, rung, SUB, d...  56.6 us
    all_to_all x2, blocking collectives, swap(): return lax.all_to_all(parts, 'tm', 0, 0, tiled=True)  25.4 us
    ppermute x9, waiting for transfers between devices, spread(): return [lax.ppermute(value, axes, pairs) for pairs in rounds]  22.7 us
    all_gather x1, blocking collectives, shards(): ids = lax.all_gather(ids, 'space').astype(jnp.int32)  15.5 us
    ppermute x9, starting transfers between devices, spread(): return [lax.ppermute(value, axes, pairs) for pairs in rounds]  11.9 us
    ppermute x3, waiting for transfers between devices, shards(): ending = ending + lax.ppermute(state, axes, [(b, a) for a, b in pairs])  11.2 us
    all_to_all x1, starting transfers between devices, swap(): return lax.all_to_all(parts, 'tm', 0, 0, tiled=True)  7.6 us
    ppermute x3, starting transfers between devices, shards(): ending = ending + lax.ppermute(state, axes, [(b, a) for a, b in pairs])  7.26 us
  transfers between devices with their start and end apart: 13, of which 3 were waited for; matrix products, arithmetic and copies ran while one was open for 3% of the time, Pallas kernels for 13%

profile of v2, /device:TPU:8, one launch (start us, length us, event | category | flops | bytes accessed | tf_op | source)
XLA Modules:
  0.0 178.2 jit_solution(6011957202592461690)
XLA Ops:
  0.6 1.4 copy.22
  2.0 1.4 copy.21
  3.4 0.3 copy.20
  3.7 0.1 maximum_bitcast_fusion.refs_2_.refs_6_
  3.9 1.6 collective-permute-start.2
  5.4 1.3 collective-permute-start.1
  6.7 1.3 collective-permute-start
  8.0 0.2 fusion.15
  8.3 1.1 copy-done.1
  9.3 0.2 pad_maximum_fusion.1.refs_6_
  9.5 1.3 collective-permute-start.5
  10.8 1.3 collective-permute-start.4
  12.1 7.6 %all-to-all-start = ((f32[8,64,256]{2,1,0:T(8,128)}), f32[8,64,256]{2,1,0:T(8,128)}, u32[]{:S(2)}, u32[]{:S(2)}) async-start(f32[8,64,256]{2,1,0:T(8,128)} %bitcast.28), calls=%async_computation | async-start | bytes 1048576 | tf_op jit(solution)/shard_map/all_to_all | solution.py:302
  19.7 0.1 copy.18
  19.9 22.6 %collective-permute-done.2.refs_5_.refs_9_ = f32[3,4,16,8,256]{4,3,2,1,0:T(8,128)} collective-permute-done((f32[3,4,16,8,256]{4,3,2,1,0:T(8,128)S(1)}, f32[3,4,16,8,256]{4,3,2,1,0:T(8,128)}, u32[]{:S(2)}, u32[]{:S(2)}) %collective-permute-start.2) | collective-permute-done | bytes 1572896 | tf_op jit(solution)/shard_map/ppermute | solution.py:298
  42.5 1.3 collective-permute-start.3
  43.9 15.5 %all_gather.4 = f32[4,8,9]{2,1,0:T(8,128)S(1)} all-gather(f32[1,8,9]{2,1,0:T(8,128)S(1)} %add_convert_fusion), channel_id=1, replica_groups=mesh['tm'=8,'space'=4] {'space'}, dimensions={0}, use_global_device_ids=true | all-gather | bytes 1440 | tf_op jit(solution)/shard_map/all_gather | solution.py:282
  59.4 2.2 %pad_maximum_fusion.refs_10_ = f32[5,8,32,128]{3,2,1,0:T(8,128)} fusion(f32[8,8,32,64]{3,2,1,0:T(8,128)} %copy-done.1, f32[8,8,32,64]{3,2,1,0:T(8,128)S(1)} %get-tuple-element.33), kind=kLoop, calls=%fused_computation.2 | loop fusion | flops 163840 | bytes 1703936 | tf_op jit(solution)/shard_map/concatenate | solution.py:294
  61.7 1.3 collective-permute-start.8
  63.0 1.3 collective-permute-start.7
  64.3 1.3 collective-permute-start.6
  65.6 0.2 slice_reduce_fusion
  65.8 0.1 fusion.4
  65.9 0.6 pad_add_fusion
  66.5 1.1 copy.19
  67.6 0.7 reshape.57.refs_1_
  68.3 0.5 broadcast_select_fusion.1.refs_0_
  68.9 22.4 %shard_map.95 = (f32[4,16,8,256]{3,2,1,0:T(8,128)}, f32[4,16,8,256]{3,2,1,0:T(8,128)}, f32[4,16,8,256]{3,2,1,0:T(8,128)}, f32[4,16,8,256]{3,2,1,0:T(8,128)}) custom-call(s32[4]{0:T(128)} %broadcast_select_fusion.1.refs_0_, s32[1024]{0:T(1024)} %reshape.57.refs_1_, f32[3,4,16,8,256]{4,3,2,1,0:T(8,128)} %copy-done, ...), custom_call_target="tpu_custom_call" | custom-call | flops 62914560 | bytes 50331648 | tf_op jit(solution)/shard_map/pallas_call | solution.py:221
  91.4 0.8 copy-done.7
  92.2 0.3 copy-done.8
  92.5 34.1 %shard_map.96 = (f32[4,16,8,256]{3,2,1,0:T(8,128)}, f32[4,16,8,256]{3,2,1,0:T(8,128)}, f32[4,16,8,256]{3,2,1,0:T(8,128)}, f32[4,16,8,256]{3,2,1,0:T(8,128)}) custom-call(s32[4]{0:T(128)} %broadcast_select_fusion.1.refs_0_, s32[1024]{0:T(1024)} %reshape.57.refs_1_, f32[4,16,8,256]{3,2,1,0:T(8,128)} %get-tuple-element.14.refs_2_, ...), custom_call_target="tpu_custom_call" | custom-call | flops 104857600 | bytes 83886080 | tf_op jit(solution)/shard_map/pallas_call | solution.py:221
  126.6 4.6 %collective-permute-start.9 = (f32[4,16,8,256]{3,2,1,0:T(8,128)}, f32[4,16,8,256]{3,2,1,0:T(8,128)S(1)}, u32[]{:S(2)}, u32[]{:S(2)}) collective-permute-start(f32[4,16,8,256]{3,2,1,0:T(8,128)} %get-tuple-element.20), channel_id=1, source_target_pairs={{1,0},{6,7},{9,8},{14,15},{17,16},{22,23},{25,24},{30,31}} | collective-permute-start | bytes 1572872 | tf_op jit(solution)/shard_map/ppermute | solution.py:318
  131.2 1.3 collective-permute-start.10
  132.5 1.3 collective-permute-start.11
  133.9 9.9 %collective-permute-done.9 = f32[4,16,8,256]{3,2,1,0:T(8,128)S(1)} collective-permute-done((f32[4,16,8,256]{3,2,1,0:T(8,128)}, f32[4,16,8,256]{3,2,1,0:T(8,128)S(1)}, u32[]{:S(2)}, u32[]{:S(2)}) %collective-permute-start.9) | collective-permute-done | bytes 524320 | tf_op jit(solution)/shard_map/ppermute | solution.py:318
  143.8 1.3 collective-permute-done.11
  145.1 1.2 add_bitcast_fusion
  146.3 0.2 copy.23
  146.5 0.1 subtract_select_fusion
  146.7 13.3 %all_to_all.15 = f32[8,64,256]{2,1,0:T(8,128)S(1)} all-to-all(f32[8,64,256]{2,1,0:T(8,128)S(1)} %subtract_select_fusion), channel_id=1, replica_groups=mesh['tm'=8,'space'=4] {'tm'}, dimensions={0} | all-to-all | bytes 1048576 | tf_op jit(solution)/shard_map/all_to_all | solution.py:302
  159.9 0.9 constant_dynamic-update-slice_fusion.4
  160.8 0.9 constant_dynamic-update-slice_fusion.3
  161.7 0.9 constant_dynamic-update-slice_fusion.2
  162.6 0.9 constant_dynamic-update-slice_fusion.1
  163.4 0.9 constant_dynamic-update-slice_fusion
  164.3 0.9 fusion
  165.2 12.2 %all_to_all.16 = f32[8,64,256]{2,1,0:T(8,128)S(1)} all-to-all(f32[8,64,256]{2,1,0:T(8,128)S(1)} %fusion), channel_id=1, replica_groups=mesh['tm'=8,'space'=4] {'tm'}, dimensions={0} | all-to-all | bytes 1048576 | tf_op jit(solution)/shard_map/all_to_all | solution.py:302
  177.3 0.9 broadcast_select_fusion
  (41 shorter events, 0.3 us)
Async XLA Ops:
  0.6 2.8 %copy-start.2 = (f32[1,4,128,256]{3,2,1,0:T(8,128)S(1)}, f32[1,4,128,256]{3,2,1,0:T(8,128)}, u32[]{:S(2)}) copy-start(f32[1,4,128,256]{3,2,1,0:T(8,128)} %param.8) | copy-start | bytes 1572868
  3.7 4.3 %copy-start.5 = (f32[8,8,64,64]{3,2,1,0:T(8,128)S(1)}, f32[8,8,64,64]{3,2,1,0:T(8,128)}, u32[]{:S(2)}) copy-start(f32[8,8,64,64]{3,2,1,0:T(8,128)} %param.14) | copy-start | bytes 3145732
  3.8 4.4 %copy-start = (f32[3,4,16,8,256]{4,3,2,1,0:T(8,128)}, f32[3,4,16,8,256]{4,3,2,1,0:T(8,128)S(1)}, u32[]{:S(2)}) copy-start(f32[3,4,16,8,256]{4,3,2,1,0:T(8,128)S(1)} %maximum_bitcast_fusion.refs_2_.refs_6_) | copy-start | bytes 4718596
  3.9 38.7 %collective-permute-start.2 = (f32[3,4,16,8,256]{4,3,2,1,0:T(8,128)S(1)}, f32[3,4,16,8,256]{4,3,2,1,0:T(8,128)}, u32[]{:S(2)}, u32[]{:S(2)}) collective-permute-start(f32[3,4,16,8,256]{4,3,2,1,0:T(8,128)S(1)} %maximum_bitcast_fusion.refs_2_.refs_6_), channel_id=1, source_target_pairs={{3,1},{4,6},{11,9},{12,14},{19,17},{20,22},{27,25},{28,30}} | collective-permute-start | bytes 4718600 | tf_op jit(solution)/shard_map/ppermute | solution.py:298
  5.4 63.4 %collective-permute-start.1 = (f32[3,4,16,8,256]{4,3,2,1,0:T(8,128)S(1)}, f32[3,4,16,8,256]{4,3,2,1,0:T(8,128)}, u32[]{:S(2)}, u32[]{:S(2)}) collective-permute-start(f32[3,4,16,8,256]{4,3,2,1,0:T(8,128)S(1)} %maximum_bitcast_fusion.refs_2_.refs_6_), channel_id=1, source_target_pairs={{2,1},{5,6},{10,9},{13,14},{18,17},{21,22},{26,25},{29,30}} | collective-permute-start | bytes 4718600 | tf_op jit(solution)/shard_map/ppermute | solution.py:298
  6.7 62.1 %collective-permute-start = (f32[3,4,16,8,256]{4,3,2,1,0:T(8,128)S(1)}, f32[3,4,16,8,256]{4,3,2,1,0:T(8,128)}, u32[]{:S(2)}, u32[]{:S(2)}) collective-permute-start(f32[3,4,16,8,256]{4,3,2,1,0:T(8,128)S(1)} %maximum_bitcast_fusion.refs_2_.refs_6_), channel_id=1, source_target_pairs={{0,1},{7,6},{8,9},{15,14},{16,17},{23,22},{24,25},{31,30}} | collective-permute-start | bytes 4718600 | tf_op jit(solution)/shard_map/ppermute | solution.py:298
  8.3 1.1 copy-start.1
  9.3 10.4 %copy-start.11 = (s32[8,1]{0,1:T(1,128)S(1)}, s32[8,1]{0,1:T(1,128)}, u32[]{:S(2)}) copy-start(s32[8,1]{0,1:T(1,128)} %param.13) | copy-start | bytes 100
  9.3 10.5 %copy-start.10 = (s32[8,8]{1,0:T(8,128)S(1)}, s32[8,8]{1,0:T(8,128)}, u32[]{:S(2)}) copy-start(s32[8,8]{1,0:T(8,128)} %param.12) | copy-start | bytes 772
  9.5 52.1 %copy-start.6 = (f32[3,8,32,128]{3,2,1,0:T(8,128)}, f32[3,8,32,128]{3,2,1,0:T(8,128)S(1)}, u32[]{:S(2)}) copy-start(f32[3,8,32,128]{3,2,1,0:T(8,128)S(1)} %pad_maximum_fusion.1.refs_6_) | copy-start | bytes 1179652
  9.5 52.1 %collective-permute-start.5 = (f32[3,8,32,128]{3,2,1,0:T(8,128)S(1)}, f32[3,8,32,128]{3,2,1,0:T(8,128)}, u32[]{:S(2)}, u32[]{:S(2)}) collective-permute-start(f32[3,8,32,128]{3,2,1,0:T(8,128)S(1)} %pad_maximum_fusion.1.refs_6_), channel_id=1, source_target_pairs={{3,1},{4,6},{11,9},{12,14},{19,17},{20,22},{27,25},{28,30}} | collective-permute-start | bytes 1179656 | tf_op jit(solution)/shard_map/ppermute | solution.py:298
  10.8 52.1 %collective-permute-start.4 = (f32[3,8,32,128]{3,2,1,0:T(8,128)S(1)}, f32[3,8,32,128]{3,2,1,0:T(8,128)}, u32[]{:S(2)}, u32[]{:S(2)}) collective-permute-start(f32[3,8,32,128]{3,2,1,0:T(8,128)S(1)} %pad_maximum_fusion.1.refs_6_), channel_id=1, source_target_pairs={{2,1},{5,6},{10,9},{13,14},{18,17},{21,22},{26,25},{29,30}} | collective-permute-start | bytes 1179656 | tf_op jit(solution)/shard_map/ppermute | solution.py:298
  12.1 56.7 %all-to-all-start = ((f32[8,64,256]{2,1,0:T(8,128)}), f32[8,64,256]{2,1,0:T(8,128)}, u32[]{:S(2)}, u32[]{:S(2)}) async-start(f32[8,64,256]{2,1,0:T(8,128)} %bitcast.28), calls=%async_computation | async-start | bytes 1048576 | tf_op jit(solution)/shard_map/all_to_all | solution.py:302
  42.5 21.7 %collective-permute-start.3 = (f32[3,8,32,128]{3,2,1,0:T(8,128)S(1)}, f32[3,8,32,128]{3,2,1,0:T(8,128)}, u32[]{:S(2)}, u32[]{:S(2)}) collective-permute-start(f32[3,8,32,128]{3,2,1,0:T(8,128)S(1)} %pad_maximum_fusion.1.refs_6_), channel_id=1, source_target_pairs={{0,1},{7,6},{8,9},{15,14},{16,17},{23,22},{24,25},{31,30}} | collective-permute-start | bytes 1179656 | tf_op jit(solution)/shard_map/ppermute | solution.py:298
  59.4 8.9 %copy-start.12 = (s32[4]{0:T(128)S(1)}, s32[4]{0:T(128)}, u32[]{:S(2)}) copy-start(s32[4]{0:T(128)} %constant.101) | copy-start | bytes 52
  59.4 8.9 %copy-start.13 = (s32[4]{0:T(128)S(1)}, s32[4]{0:T(128)}, u32[]{:S(2)}) copy-start(s32[4]{0:T(128)} %constant.95.clone) | copy-start | bytes 52
  61.7 29.7 %collective-permute-start.8 = (f32[5,8,32,128]{3,2,1,0:T(8,128)}, f32[5,8,32,128]{3,2,1,0:T(8,128)S(1)}, u32[]{:S(2)}, u32[]{:S(2)}) collective-permute-start(f32[5,8,32,128]{3,2,1,0:T(8,128)} %pad_maximum_fusion.refs_10_), channel_id=1, source_target_pairs={{3,1},{4,6},{11,9},{12,14},{19,17},{20,22},{27,25},{28,30}} | collective-permute-start | bytes 1966088 | tf_op jit(solution)/shard_map/ppermute | solution.py:298
  63.0 28.4 %collective-permute-start.7 = (f32[5,8,32,128]{3,2,1,0:T(8,128)}, f32[5,8,32,128]{3,2,1,0:T(8,128)}, u32[]{:S(2)}, u32[]{:S(2)}) collective-permute-start(f32[5,8,32,128]{3,2,1,0:T(8,128)} %pad_maximum_fusion.refs_10_), channel_id=1, source_target_pairs={{2,1},{5,6},{10,9},{13,14},{18,17},{21,22},{26,25},{29,30}} | collective-permute-start | bytes 1966088 | tf_op jit(solution)/shard_map/ppermute | solution.py:298
  64.3 27.1 %collective-permute-start.6 = (f32[5,8,32,128]{3,2,1,0:T(8,128)}, f32[5,8,32,128]{3,2,1,0:T(8,128)S(1)}, u32[]{:S(2)}, u32[]{:S(2)}) collective-permute-start(f32[5,8,32,128]{3,2,1,0:T(8,128)} %pad_maximum_fusion.refs_10_), channel_id=1, source_target_pairs={{0,1},{7,6},{8,9},{15,14},{16,17},{23,22},{24,25},{31,30}} | collective-permute-start | bytes 1966088 | tf_op jit(solution)/shard_map/ppermute | solution.py:298
  91.3 0.9 copy-start.7
  91.4 1.1 copy-start.8
  92.5 41.4 %copy-start.9 = (s32[4]{0:T(128)S(1)}, s32[4]{0:T(128)}, u32[]{:S(2)}) copy-start(s32[4]{0:T(128)} %broadcast_select_fusion.1.refs_0_) | copy-start | bytes 52
  126.6 17.2 %collective-permute-start.9 = (f32[4,16,8,256]{3,2,1,0:T(8,128)}, f32[4,16,8,256]{3,2,1,0:T(8,128)S(1)}, u32[]{:S(2)}, u32[]{:S(2)}) collective-permute-start(f32[4,16,8,256]{3,2,1,0:T(8,128)} %get-tuple-element.20), channel_id=1, source_target_pairs={{1,0},{6,7},{9,8},{14,15},{17,16},{22,23},{25,24},{30,31}} | collective-permute-start | bytes 1572872 | tf_op jit(solution)/shard_map/ppermute | solution.py:318
  131.2 12.6 %collective-permute-start.10 = (f32[4,16,8,256]{3,2,1,0:T(8,128)}, f32[4,16,8,256]{3,2,1,0:T(8,128)S(1)}, u32[]{:S(2)}, u32[]{:S(2)}) collective-permute-start(f32[4,16,8,256]{3,2,1,0:T(8,128)} %get-tuple-element.21), channel_id=1, source_target_pairs={{1,2},{6,5},{9,10},{14,13},{17,18},{22,21},{25,26},{30,29}} | collective-permute-start | bytes 1572872 | tf_op jit(solution)/shard_map/ppermute | solution.py:318
  132.5 12.6 %collective-permute-start.11 = (f32[4,16,8,256]{3,2,1,0:T(8,128)}, f32[4,16,8,256]{3,2,1,0:T(8,128)S(1)}, u32[]{:S(2)}, u32[]{:S(2)}) collective-permute-start(f32[4,16,8,256]{3,2,1,0:T(8,128)} %get-tuple-element.22), channel_id=1, source_target_pairs={{1,3},{6,4},{9,11},{14,12},{17,19},{22,20},{25,27},{30,28}} | collective-permute-start | bytes 1572872 | tf_op jit(solution)/shard_map/ppermute | solution.py:318
  145.1 1.4 copy-start.3
  146.5 13.4 %copy-start.4 = (f32[4,8,16,256]{3,2,1,0:T(8,128)}, f32[4,8,16,256]{3,2,1,0:T(8,128)S(1)}, u32[]{:S(2)}) copy-start(f32[4,8,16,256]{3,2,1,0:T(8,128)S(1)} %copy.23) | copy-start | bytes 1572868

commit v3 on v2

v3 whole, which is shorter than its diff:
```python
import functools

import jax
import jax.numpy as jnp
from jax import lax
from jax.experimental import pallas as pl
from jax.experimental.pallas import tpu as pltpu
from jax.sharding import PartitionSpec as P

SWEEPS = 4
COND = 1.0
SUB = 8
LANE = 128
EARLY = 3
SPAN = 8


def span_of(planes):
    return max(n for n in range(1, SPAN + 1) if planes % n == 0)


def steps_kernel(shape, slots, tile, first, steps, own_blocks, *refs):
    bricks, width, rung, depth = shape
    planes, thick = bricks * width, width * rung
    half = depth // LANE
    count = bricks * slots
    share = tile * tile // depth

    def take(n):
        nonlocal refs
        head, refs = refs[:n], refs[n:]
        return head

    (place,) = take(1)
    if own_blocks:
        packs = take(bricks)
        states = [pack.at[pl.ds(0, thick)] for pack in packs]
        blocks = [pack.at[pl.ds(3 * thick, steps * slots * share // SUB)] for pack in packs]
    else:
        states, packs, blocks = take(bricks), take(bricks), take(bricks)
    outs, (mark,) = take(bricks), take(1)
    field, other, source, capacity, inverse, rhs, kept, current, picked, fixes, held, raw, whole_lists, lists, load_sem, held_sem, list_sem = refs
    stack = slots * share // SUB

    def fetch_blocks(step, slot):
        return [
            pltpu.make_async_copy(blocks[i].at[pl.ds(step * stack, stack)], held.at[slot, i], held_sem.at[slot, i])
            for i in range(bricks)
        ]

    def slab(i, lead):
        return pl.ds((place[i] * width + lead) * rung, thick)

    loads = []
    for i in range(bricks):
        loads.append((packs[i].at[pl.ds(2 * thick, thick)], capacity.at[slab(i, 0)]))
    for i in range(bricks):
        loads.append((states[i], field.at[slab(i, 1)]))
        loads.append((packs[i].at[pl.ds(thick, thick)], source.at[slab(i, 0)]))
    loads = [pltpu.make_async_copy(*ends, load_sem.at[n]) for n, ends in enumerate(loads)]
    tail = packs[0].shape[0] - 1
    raw_copies = [pltpu.make_async_copy(packs[i].at[tail], raw.at[i], list_sem.at[i]) for i in range(bricks)]
    for copy in raw_copies:
        copy.start()
    for copy in loads:
        copy.start()
    for copy in fetch_blocks(0, 0):
        copy.start()

    zero = jnp.zeros((rung, SUB, depth), jnp.float32)
    for edge in (0, planes + 1):
        field[pl.ds(edge * rung, rung)] = zero
        other[pl.ds(edge * rung, rung)] = zero
    for copy in raw_copies:
        copy.wait()
    whole_lists[...] = raw[:, : whole_lists.shape[1], :].astype(jnp.int32)
    list_copy = pltpu.make_async_copy(whole_lists, lists, list_sem.at[0])
    list_copy.start()
    for copy in loads[:bricks]:
        copy.wait()

    def invert(x, _):
        plane = pl.ds(x * rung, rung)
        inverse[plane] = 1.0 / (capacity[plane] + 6.0 * COND)
        return 0

    lax.fori_loop(0, planes, invert, 0)
    for copy in loads[bricks:]:
        copy.wait()
    list_copy.wait()

    sub = lax.broadcasted_iota(jnp.int32, (SUB, LANE), 0)
    top, bottom = sub == 0, sub == SUB - 1
    line = lax.broadcasted_iota(jnp.int32, (depth, depth), 0)
    column = lax.broadcasted_iota(jnp.int32, (depth, depth), 1)
    beside = jnp.where(jnp.abs(line - column) == 1, 1.0, 0.0).astype(jnp.bfloat16)
    span = span_of(planes)

    def split(value):
        coarse = value.astype(jnp.bfloat16)
        return coarse, (value - coarse.astype(jnp.float32)).astype(jnp.bfloat16)

    def product(value, matrix):
        coarse, fine = split(value)
        return jnp.dot(coarse, matrix, preferred_element_type=jnp.float32) + jnp.dot(
            fine, matrix, preferred_element_type=jnp.float32
        )

    def sweep(src, dst, opening):
        def chunk(n, _):
            whole = src[pl.ds((n * span + 1) * rung, span * rung)].reshape(span * rung * SUB, depth)
            along = product(whole, beside).reshape(span * rung, SUB, depth)
            for p in range(span):
                x = (n * span + p) * rung
                center = [[src[x + rung + r, :, pl.ds(h * LANE, LANE)] for h in range(half)] for r in range(rung)]
                for r in range(rung):
                    for h in range(half):
                        lanes = pl.ds(h * LANE, LANE)
                        if r:
                            above = center[r - 1][h]
                        else:
                            above = jnp.where(top, 0.0, pltpu.roll(center[rung - 1][h], 1, 0))
                        if r + 1 < rung:
                            below = center[r + 1][h]
                        else:
                            below = jnp.where(bottom, 0.0, pltpu.roll(center[0][h], SUB - 1, 0))
                        total = src[x + r, :, lanes] + src[x + 2 * rung + r, :, lanes]
                        total = total + (above + below) + along[p * rung + r, :, h * LANE : (h + 1) * LANE]
                        if opening:
                            base = capacity[x + r, :, lanes] * center[r][h] + source[x + r, :, lanes]
                            rhs[x + r, :, lanes] = base
                        else:
                            base = rhs[x + r, :, lanes]
                        dst[x + rung + r, :, lanes] = (base + COND * total) * inverse[x + r, :, lanes]
            return 0

        lax.fori_loop(0, planes // span, chunk, 0)

    quarter = lax.broadcasted_iota(jnp.int32, (1, depth), 1) // tile
    group = depth // tile
    gathers = jnp.where(line // tile == (column % tile) // share, 1.0, 0.0).astype(jnp.bfloat16)
    own_line = lax.broadcasted_iota(jnp.int32, (share, depth), 0)
    own_lane = lax.broadcasted_iota(jnp.int32, (share, depth), 1)
    diagonal = own_line == own_lane % share
    tiles = [(i, s) for i in range(bricks) for s in range(slots)]

    def cell_of(step, i, s):
        at = ((first + step) * slots + s) * 4
        spot = [lists[i, (at + k) // depth, (at + k) % depth] for k in range(3)]
        return spot[0] + (place[i] * width + 1) * rung, spot[1], spot[2]

    def one_step(step, _):
        slot = step % 2

        @pl.when(step + 1 < steps)
        def _():
            for copy in fetch_blocks(step + 1, 1 - slot):
                copy.start()

        for n, (i, s) in enumerate(tiles):
            x, u, _unused = cell_of(step, i, s)
            kept[n : n + 1, :] = field[x, pl.ds(u, 1), :]
        sweep(field, other, True)
        for _pair in range((SWEEPS - 2) // 2):
            sweep(other, field, False)
            sweep(field, other, False)
        sweep(other, field, False)

        for n, (i, s) in enumerate(tiles):
            x, u, part = cell_of(step, i, s)
            value = field[x, pl.ds(u, 1), :]
            current[n : n + 1, :] = value
            delta = jnp.where(quarter == part, value - kept[n : n + 1, :], 0.0)
            whole = delta
            for g in range(1, group):
                whole = whole + pltpu.roll(delta, g * tile, 1)
            picked[n : n + 1, :] = whole
        for copy in fetch_blocks(step, slot):
            copy.wait()

        def multiply(b, _):
            terms = [
                held[slot, b, pl.ds(s * (share // SUB), share // SUB)].reshape(share, depth)
                * picked[pl.ds(b * slots + s, 1), :]
                for s in range(slots)
            ]
            sums = product(jnp.concatenate(terms, axis=0), gathers)
            for s in range(slots):
                fix = jnp.where(diagonal, sums[s * share : (s + 1) * share], 0.0)
                fixes[pl.ds(b * slots + s, 1), :] = jnp.sum(fix, axis=0, keepdims=True)
            return 0

        lax.fori_loop(0, bricks, multiply, 0)

        for n, (i, s) in enumerate(tiles):
            x, u, part = cell_of(step, i, s)
            value = current[n : n + 1, :] + fixes[n : n + 1, :]
            pltpu.store(field.at[x, pl.ds(u, 1), :], value, mask=quarter == part)
        return 0

    lax.fori_loop(0, steps, one_step, 0)
    stores = [
        pltpu.make_async_copy(field.at[slab(i, 1)], outs[i], load_sem.at[i]) for i in range(bricks)
    ]
    for copy in stores:
        copy.start()
    mark[...] = jnp.zeros_like(mark)
    for copy in stores:
        copy.wait()


def run_steps(place, states, packs, blocks, shape, list_rows, first, steps, slots, tile):
    bricks, width, rung, depth = shape
    planes = bricks * width
    count = bricks * slots
    body = functools.partial(steps_kernel, shape, slots, tile, first, steps, blocks is None)
    smem = pl.BlockSpec(memory_space=pltpu.SMEM)
    hbm = pl.BlockSpec(memory_space=pl.ANY)
    operands = list(packs) if blocks is None else list(states) + list(packs) + list(blocks)
    grid_shape = (planes * rung, SUB, depth)
    wide_shape = ((planes + 2) * rung, SUB, depth)
    cells = planes * rung * SUB * depth
    return pl.pallas_call(
        body,
        out_shape=[jax.ShapeDtypeStruct((width * rung, SUB, depth), jnp.float32)] * bricks
        + [jax.ShapeDtypeStruct((SUB, LANE), jnp.float32)],
        in_specs=[smem] + [hbm] * len(operands),
        out_specs=[hbm] * bricks + [pl.BlockSpec(memory_space=pltpu.VMEM)],
        scratch_shapes=[
            pltpu.VMEM(wide_shape, jnp.float32),
            pltpu.VMEM(wide_shape, jnp.float32),
            pltpu.VMEM(grid_shape, jnp.float32),
            pltpu.VMEM(grid_shape, jnp.float32),
            pltpu.VMEM(grid_shape, jnp.float32),
            pltpu.VMEM(grid_shape, jnp.float32),
            pltpu.VMEM((count, depth), jnp.float32),
            pltpu.VMEM((count, depth), jnp.float32),
            pltpu.VMEM((count, depth), jnp.float32),
            pltpu.VMEM((count, depth), jnp.float32),
            pltpu.VMEM((2, bricks, slots * tile * tile // depth // SUB, SUB, depth), jnp.float32),
            pltpu.VMEM((bricks, SUB, depth), jnp.float32),
            pltpu.VMEM((bricks, list_rows, depth), jnp.int32),
            pltpu.SMEM((bricks, list_rows, depth), jnp.int32),
            pltpu.SemaphoreType.DMA((3 * bricks,)),
            pltpu.SemaphoreType.DMA((2, bricks)),
            pltpu.SemaphoreType.DMA((bricks,)),
        ],
        compiler_params=pltpu.CompilerParams(vmem_limit_bytes=60 * 1024 * 1024),
        cost_estimate=pl.CostEstimate(
            flops=cells * steps * SWEEPS * 10, bytes_accessed=cells * 4 * steps * 8, transcendentals=0
        ),
    )(place, *operands)


def recurrence(factors, shifts):
    def body(factor, shift, out):
        x = shift[0]
        out[0] = x
        for j in range(1, shifts.shape[0]):
            out[j] = x
            x = factor[j] * x + shift[j]

    return pl.pallas_call(body, out_shape=jax.ShapeDtypeStruct(shifts.shape, jnp.float32))(factors, shifts)


def routes(windows, bricks):
    home = bricks // 2 - 1
    others = [z for z in range(bricks) if z != home]

    def at(t, z):
        return t * bricks + (z if t % 2 == 0 else bricks - 1 - z)

    rounds = [[(at(t, z), at(t, home)) for t in range(windows)] for z in others]
    return home, others, rounds


def shards(
    opening_guess_profile,
    capacity,
    thermal_forcing,
    rough_decay_factor,
    tile_ids,
    tile_count,
    tile_blocks,
):
    axes = ("tm", "space")
    windows, bricks = lax.axis_size("tm"), lax.axis_size("space")
    window, brick = lax.axis_index("tm"), lax.axis_index("space")
    opening = opening_guess_profile[0]
    rough = rough_decay_factor[0]
    width, rows, depth = opening.shape
    steps, slots = tile_ids.shape
    tile = tile_blocks.shape[-1]
    home, others, rounds = routes(windows, bricks)
    place = jnp.array([home] + others, jnp.int32)
    place = jnp.where(window % 2 == 0, place, bricks - 1 - place)

    rung = rows // SUB
    live = jnp.arange(slots) < tile_count
    per_row = depth // tile
    line = tile_ids // per_row
    part = jnp.where(live, tile_ids % per_row, -1)
    cells = jnp.stack([line // rows * rung + line % rung, line % rows // rung, part, part], axis=-1)
    cells = cells.astype(jnp.float32).reshape(-1, depth)
    list_rows = cells.shape[0]
    cells = jnp.pad(cells, ((0, SUB - cells.shape[0]), (0, 0)))[None]

    def blocked(value):
        return value.reshape(-1, SUB, rung, depth).swapaxes(1, 2).reshape(-1, SUB, depth)

    group = depth // tile
    share = tile // group
    blocks = jnp.concatenate([tile_blocks[:, :, g * share : (g + 1) * share] for g in range(group)], axis=-1)
    blocks = blocks.reshape(-1, SUB, depth)
    early = EARLY * steps // 8
    cut = early * (blocks.shape[0] // steps)
    fields = [blocked(value) for value in (opening, thermal_forcing[0], capacity)]
    pack = jnp.concatenate(fields + [blocks[:cut], cells])
    shape = (bricks, width, rung, depth)

    def spread(value):
        return [lax.ppermute(value, axes, pairs) for pairs in rounds]

    def swap(value):
        parts = value.reshape(windows, -1, depth)
        return lax.all_to_all(parts, "tm", 0, 0, tiled=True)

    packs = [pack] + spread(pack)
    blocks_late = [blocks[cut:]] + spread(blocks[cut:])
    *states, mark = run_steps(place, None, packs, None, shape, list_rows, 0, early, slots, tile)
    rough_late, _ = lax.optimization_barrier((rough, mark))
    factors = lax.all_gather(rough_late, "tm").reshape(windows, windows, -1, depth)
    factors = lax.dynamic_index_in_dim(factors, window, 1, keepdims=False)
    *states, mark = run_steps(place, states, packs, blocks_late, shape, list_rows, early, steps - early, slots, tile)

    held_here = brick == place[0]
    ending = jnp.where(held_here, states[0], 0.0)
    for pairs, state in zip(rounds, states[1:]):
        ending = ending + lax.ppermute(state, axes, [(b, a) for a, b in pairs])

    ending = ending.reshape(width, rung, SUB, depth).swapaxes(1, 2).reshape(width, rows, depth)
    shift = jnp.where(window == 0, ending, ending - rough * opening)
    shifts = swap(shift)
    result = swap(recurrence(factors, shifts)).reshape(width, rows, depth)
    updated = jnp.where(window == 0, opening, result)
    return (updated[None], ending[None])


def solution(mesh):
    in_specs = (
        P("tm", "space", None, None),
        P("space", None, None),
        P("tm", "space", None, None),
        P("tm", "space", None, None),
        P("tm", "space"),
        P("tm", "space"),
        P("tm", "space", None, None),
    )
    out_specs = (P("tm", "space", None, None), P("tm", "space", None, None))
    return jax.shard_map(shards, mesh=mesh, in_specs=in_specs, out_specs=out_specs, check_vma=False)
```

time: 181 us -> 179 us (0.989)
  blocking collectives: 40.9 us -> 13.1 us
  waiting for transfers between devices: 33.9 us -> 60.4 us
  between operations: 1.06 us -> 14.5 us
  starting transfers between devices: 26.7 us -> 16.2 us
  other arithmetic: 11.3 us -> 4.24 us
  local copies, waits for them, and re-layouts: 7.75 us -> 10.3 us
  Pallas kernels: 56.6 us -> 59 us
    ppermute x9 -> x6, waiting for transfers between devices: 22.7 us -> 41.4 us  [spread(): return [lax.ppermute(value, axes, pairs) for pairs in rounds]]
    all_gather x1 -> x0, blocking collectives: 15.5 us -> none  [shards(): ids = lax.all_gather(ids, 'space').astype(jnp.int32)]
    all_to_all x2 -> x1, blocking collectives: 25.4 us -> 13.1 us  [swap(): return lax.all_to_all(parts, 'tm', 0, 0, tiled=True)]
    all_to_all x1, waiting for transfers between devices: 0.01 us -> 7.84 us  [swap(): return lax.all_to_all(parts, 'tm', 0, 0, tiled=True)]
    unnamed x5 -> x0, other arithmetic: 4.37 us -> none
    ppermute x9 -> x6, starting transfers between devices: 11.9 us -> 7.74 us  [spread(): return [lax.ppermute(value, axes, pairs) for pairs in rounds]]
    all_to_all x1, starting transfers between devices: 7.6 us -> 3.72 us  [swap(): return lax.all_to_all(parts, 'tm', 0, 0, tiled=True)]
    ppermute x3, starting transfers between devices: 7.26 us -> 4.65 us  [shards(): ending = ending + lax.ppermute(state, axes, [(b, a) for a, b in pairs])]
  transfers between devices with their start and end apart: 13 -> 11, of which waited for: 3 -> 6; matrix products, arithmetic and copies ran while one was open for 3% -> 6% of each run, Pallas kernels for 13% -> 32%
where the time goes in v3:
time: 179 us; the launch traced here: 178 us
  waiting for transfers between devices  60.4 us (34%)
  Pallas kernels  59 us (33%)
  starting transfers between devices  16.2 us (9%)
  between operations  14.5 us (8%)
  blocking collectives  13.1 us (7%)
  local copies, waits for them, and re-layouts  10.3 us (6%)
  other arithmetic  4.24 us (2%)
    pallas_call x2, Pallas kernels, run_steps(): pl.pallas_call(body, out_shape=[jax.ShapeDtypeStruct((width * rung, SUB,...  57 us
    ppermute x6, waiting for transfers between devices, spread(): return [lax.ppermute(value, axes, pairs) for pairs in rounds]  41.4 us
    all_to_all x1, blocking collectives, swap(): return lax.all_to_all(parts, 'tm', 0, 0, tiled=True)  13.1 us
    ppermute x3, waiting for transfers between devices, shards(): ending = ending + lax.ppermute(state, axes, [(b, a) for a, b in pairs])  10.4 us
    all_to_all x1, waiting for transfers between devices, swap(): return lax.all_to_all(parts, 'tm', 0, 0, tiled=True)  7.84 us
    ppermute x6, starting transfers between devices, spread(): return [lax.ppermute(value, axes, pairs) for pairs in rounds]  7.74 us
    ppermute x3, starting transfers between devices, shards(): ending = ending + lax.ppermute(state, axes, [(b, a) for a, b in pairs])  4.65 us
    unnamed x36, local copies, waits for them, and re-layouts  3.94 us
  transfers between devices with their start and end apart: 11, of which 6 were waited for; matrix products, arithmetic and copies ran while one was open for 6% of the time, Pallas kernels for 32%

profile of v3, /device:TPU:8, one launch (start us, length us, event | category | flops | bytes accessed | tf_op | source)
XLA Modules:
  0.0 177.7 jit_solution(5723011534710660679)
XLA Ops:
  7.2 0.0 all-gather.3.cloned.1.call-start
  7.2 0.7 all-gather.3.cloned.1.call-update
  7.9 2.2 %copy.23 = f32[4,8,16,256]{3,1,2,0:T(8,128)} copy(f32[4,8,16,256]{3,2,1,0:T(8,128)} %bitcast.39) | data formatting | bytes 1048576 | tf_op jit(solution)/shard_map/reshape;squeeze | solution.py:309
  10.1 1.3 copy.24
  11.5 0.3 copy.25
  11.8 0.1 fusion.2
  11.9 0.1 copy.26
  12.0 0.1 convert_element_type.16
  12.2 0.2 fusion.13
  12.4 0.0 copy-start.8
  12.4 0.2 pad_maximum_fusion.3
  12.6 0.8 copy-done.8
  13.6 0.0 copy-start.14
  13.6 0.0 copy-start.15
  13.6 1.3 collective-permute-start
  14.9 1.3 collective-permute-start.1
  16.2 1.3 collective-permute-start.2
  17.5 0.3 pad_maximum_fusion
  17.9 1.3 collective-permute-start.3
  19.2 1.3 collective-permute-start.4
  20.5 38.4 %collective-permute-done.refs_2_.refs_6_ = f32[241,8,256]{2,1,0:T(8,128)S(1)} collective-permute-done((f32[241,8,256]{2,1,0:T(8,128)S(1)}, f32[241,8,256]{2,1,0:T(8,128)S(1)}, u32[]{:S(2)}, u32[]{:S(2)}) %collective-permute-start) | collective-permute-done | bytes 1974304 | tf_op jit(solution)/shard_map/ppermute | solution.py:322
  58.9 1.3 copy-done.1
  60.2 1.3 collective-permute-start.5
  61.5 0.5 broadcast_select_fusion.1.refs_0_
  62.1 0.0 collective-permute-done.1.refs_3_.refs_7_
  62.1 3.0 %collective-permute-done.2.refs_4_.refs_8_ = f32[241,8,256]{2,1,0:T(8,128)} collective-permute-done((f32[241,8,256]{2,1,0:T(8,128)S(1)}, f32[241,8,256]{2,1,0:T(8,128)}, u32[]{:S(2)}, u32[]{:S(2)}) %collective-permute-start.2) | collective-permute-done | bytes 1974304 | tf_op jit(solution)/shard_map/ppermute | solution.py:322
  65.1 22.8 %shard_map.95 = (f32[64,8,256]{2,1,0:T(8,128)}, f32[64,8,256]{2,1,0:T(8,128)}, f32[64,8,256]{2,1,0:T(8,128)}, f32[64,8,256]{2,1,0:T(8,128)}, f32[8,128]{1,0:T(8,128)}) custom-call(s32[4]{0:T(128)} %broadcast_select_fusion.1.refs_0_, f32[241,8,256]{2,1,0:T(8,128)} %copy-done, f32[241,8,256]{2,1,0:T(8,128)} %copy-done.1, ...), custom_call_target="tpu_custom_call" | custom-call | flops 62914560 | bytes 50331648 | tf_op jit(solution)/shard_map/pallas_call | solution.py:223
  88.0 0.8 copy-done.9
  88.8 34.2 %shard_map.96 = (f32[64,8,256]{2,1,0:T(8,128)}, f32[64,8,256]{2,1,0:T(8,128)}, f32[64,8,256]{2,1,0:T(8,128)}, f32[64,8,256]{2,1,0:T(8,128)}, f32[8,128]{1,0:T(8,128)}) custom-call(s32[4]{0:T(128)} %broadcast_select_fusion.1.refs_0_, f32[64,8,256]{2,1,0:T(8,128)} %get-tuple-element.10.refs_1_, f32[64,8,256]{2,1,0:T(8,128)} %get-tuple-element.11.refs_2_, ...), custom_call_target="tpu_custom_call" | custom-call | flops 104857600 | bytes 83886080 | tf_op jit(solution)/shard_map/pallas_call | solution.py:223
  123.0 1.3 collective-permute-start.6
  124.3 1.3 collective-permute-start.7
  125.6 2.0 %collective-permute-start.8 = (f32[64,8,256]{2,1,0:T(8,128)}, f32[64,8,256]{2,1,0:T(8,128)S(1)}, u32[]{:S(2)}, u32[]{:S(2)}) collective-permute-start(f32[64,8,256]{2,1,0:T(8,128)} %get-tuple-element.17), channel_id=1, source_target_pairs={{1,3},{6,4},{9,11},{14,12},{17,19},{22,20},{25,27},{30,28}} | collective-permute-start | bytes 1572872 | tf_op jit(solution)/shard_map/ppermute | solution.py:339
  127.7 0.1 mul.15
  127.8 3.5 %collective-permute-done.6 = f32[64,8,256]{2,1,0:T(8,128)S(1)} collective-permute-done((f32[64,8,256]{2,1,0:T(8,128)}, f32[64,8,256]{2,1,0:T(8,128)S(1)}, u32[]{:S(2)}, u32[]{:S(2)}) %collective-permute-start.6) | collective-permute-done | bytes 524320 | tf_op jit(solution)/shard_map/ppermute | solution.py:339
  131.3 1.3 collective-permute-done.7
  132.6 5.6 %collective-permute-done.8 = f32[64,8,256]{2,1,0:T(8,128)S(1)} collective-permute-done((f32[64,8,256]{2,1,0:T(8,128)}, f32[64,8,256]{2,1,0:T(8,128)S(1)}, u32[]{:S(2)}, u32[]{:S(2)}) %collective-permute-start.8) | collective-permute-done | bytes 524320 | tf_op jit(solution)/shard_map/ppermute | solution.py:339
  138.2 1.2 add_add_fusion
  139.4 0.2 copy.27
  139.6 0.0 copy-start.7
  139.6 1.0 subtract_select_fusion
  140.5 3.7 %all-to-all-start = ((f32[8,64,256]{2,1,0:T(8,128)}), f32[8,64,256]{2,1,0:T(8,128)S(1)}, u32[]{:S(2)}, u32[]{:S(2)}) async-start(f32[8,64,256]{2,1,0:T(8,128)} %subtract_select_fusion), calls=%async_computation | async-start | bytes 1048576 | tf_op jit(solution)/shard_map/all_to_all | solution.py:326
  144.3 0.0 all-gather.3.cloned.1.call-done
  144.3 1.9 %dynamic-slice_bitcast_fusion.factor = f32[8,64,256]{2,1,0:T(8,128)} fusion(f32[8,8,64,256]{3,2,1,0:T(8,128)} %bitcast.56, s32[]{:T(128)S(6)} %select_n.73), kind=kLoop, calls=%fused_computation.5 | loop fusion | bytes 1048580 | tf_op jit(solution)/shard_map/jit(dynamic_index_in_dim)/squeeze | solution.py:333
  146.2 7.8 %all-to-all-done.shift = f32[8,64,256]{2,1,0:T(8,128)S(1)} async-done(((f32[8,64,256]{2,1,0:T(8,128)}), f32[8,64,256]{2,1,0:T(8,128)S(1)}, u32[]{:S(2)}, u32[]{:S(2)}) %all-to-all-start) | async-done | bytes 524320 | tf_op jit(solution)/shard_map/all_to_all | solution.py:326
  154.0 0.8 copy-done.5
  154.8 2.1 %shard_map.97 = f32[8,64,256]{2,1,0:T(8,128)} custom-call(f32[8,64,256]{2,1,0:T(8,128)} %dynamic-slice_bitcast_fusion.factor, f32[8,64,256]{2,1,0:T(8,128)} %copy-done.5), custom_call_target="tpu_custom_call" | custom-call | tf_op jit(solution)/shard_map/pallas_call | solution.py:263
  156.8 13.1 %all_to_all.10 = f32[8,64,256]{2,1,0:T(8,128)S(1)} all-to-all(f32[8,64,256]{2,1,0:T(8,128)} %shard_map.97), channel_id=1, replica_groups=mesh['tm'=8,'space'=4] {'tm'}, dimensions={0} | all-to-all | bytes 1048576 | tf_op jit(solution)/shard_map/all_to_all | solution.py:326
  170.0 0.9 broadcast_select_fusion
  (33 shorter events, 0.2 us)
Async XLA Ops:
  7.2 4.7 %copy-start.13 = (s32[8,1]{0,1:T(1,128)S(1)}, s32[8,1]{0,1:T(1,128)}, u32[]{:S(2)}) copy-start(s32[8,1]{0,1:T(1,128)} %param.13) | copy-start | bytes 100
  7.2 4.7 %copy-start.12 = (s32[8,8]{1,0:T(8,128)S(1)}, s32[8,8]{1,0:T(8,128)}, u32[]{:S(2)}) copy-start(s32[8,8]{1,0:T(8,128)} %param.12) | copy-start | bytes 772
  7.2 5.0 %copy-start.6 = (f32[8,8,64,64]{3,2,1,0:T(8,128)S(1)}, f32[8,8,64,64]{3,2,1,0:T(8,128)}, u32[]{:S(2)}) copy-start(f32[8,8,64,64]{3,2,1,0:T(8,128)} %param.14) | copy-start | bytes 3145732
  7.2 137.1 %all-gather.3.cloned.1.call-start = ((), (), s32[]{:S(2)}) async-start(), calls=%async_computation.2 | async-start | bytes 4718592 | tf_op jit(solution)/shard_map/all_gather | solution.py:332
  7.9 3.6 %copy-start.10 = (f32[4,128,256]{2,1,0:T(8,128)S(1)}, f32[4,128,256]{2,1,0:T(8,128)}, u32[]{:S(2)}) copy-start(f32[4,128,256]{2,1,0:T(8,128)} %param.9) | copy-start | bytes 1572868
  12.4 1.0 copy-start.8
  13.6 47.9 %copy-start.14 = (s32[4]{0:T(128)S(1)}, s32[4]{0:T(128)}, u32[]{:S(2)}) copy-start(s32[4]{0:T(128)} %constant.100.clone) | copy-start | bytes 52
  13.6 47.9 %copy-start.15 = (s32[4]{0:T(128)S(1)}, s32[4]{0:T(128)}, u32[]{:S(2)}) copy-start(s32[4]{0:T(128)} %constant.108) | copy-start | bytes 52
  13.6 51.5 %copy-start = (f32[241,8,256]{2,1,0:T(8,128)}, f32[241,8,256]{2,1,0:T(8,128)S(1)}, u32[]{:S(2)}) copy-start(f32[241,8,256]{2,1,0:T(8,128)S(1)} %constant_dynamic-update-slice_fusion.refs_1_.refs_5_) | copy-start | bytes 5922820
  13.6 45.2 %collective-permute-start = (f32[241,8,256]{2,1,0:T(8,128)S(1)}, f32[241,8,256]{2,1,0:T(8,128)S(1)}, u32[]{:S(2)}, u32[]{:S(2)}) collective-permute-start(f32[241,8,256]{2,1,0:T(8,128)S(1)} %constant_dynamic-update-slice_fusion.refs_1_.refs_5_), channel_id=1, source_target_pairs={{0,1},{7,6},{8,9},{15,14},{16,17},{23,22},{24,25},{31,30}} | collective-permute-start | bytes 5922824 | tf_op jit(solution)/shard_map/ppermute | solution.py:322
  14.9 47.1 %collective-permute-start.1 = (f32[241,8,256]{2,1,0:T(8,128)S(1)}, f32[241,8,256]{2,1,0:T(8,128)}, u32[]{:S(2)}, u32[]{:S(2)}) collective-permute-start(f32[241,8,256]{2,1,0:T(8,128)S(1)} %constant_dynamic-update-slice_fusion.refs_1_.refs_5_), channel_id=1, source_target_pairs={{2,1},{5,6},{10,9},{13,14},{18,17},{21,22},{26,25},{29,30}} | collective-permute-start | bytes 5922824 | tf_op jit(solution)/shard_map/ppermute | solution.py:322
  16.2 48.8 %collective-permute-start.2 = (f32[241,8,256]{2,1,0:T(8,128)S(1)}, f32[241,8,256]{2,1,0:T(8,128)}, u32[]{:S(2)}, u32[]{:S(2)}) collective-permute-start(f32[241,8,256]{2,1,0:T(8,128)S(1)} %constant_dynamic-update-slice_fusion.refs_1_.refs_5_), channel_id=1, source_target_pairs={{3,1},{4,6},{11,9},{12,14},{19,17},{20,22},{27,25},{28,30}} | collective-permute-start | bytes 5922824 | tf_op jit(solution)/shard_map/ppermute | solution.py:322
  17.9 70.1 %copy-start.3 = (f32[5,8,16,256]{3,2,1,0:T(8,128)}, f32[5,8,16,256]{3,2,1,0:T(8,128)S(1)}, u32[]{:S(2)}) copy-start(f32[5,8,16,256]{3,2,1,0:T(8,128)S(1)} %pad_maximum_fusion) | copy-start | bytes 1966084
  17.9 70.0 %collective-permute-start.3 = (f32[80,8,256]{2,1,0:T(8,128)S(1)}, f32[80,8,256]{2,1,0:T(8,128)S(1)}, u32[]{:S(2)}, u32[]{:S(2)}) collective-permute-start(f32[80,8,256]{2,1,0:T(8,128)S(1)} %bitcast.40), channel_id=1, source_target_pairs={{0,1},{7,6},{8,9},{15,14},{16,17},{23,22},{24,25},{31,30}} | collective-permute-start | bytes 1966088 | tf_op jit(solution)/shard_map/ppermute | solution.py:322
  19.2 68.8 %collective-permute-start.4 = (f32[80,8,256]{2,1,0:T(8,128)S(1)}, f32[80,8,256]{2,1,0:T(8,128)}, u32[]{:S(2)}, u32[]{:S(2)}) collective-permute-start(f32[80,8,256]{2,1,0:T(8,128)S(1)} %bitcast.41), channel_id=1, source_target_pairs={{2,1},{5,6},{10,9},{13,14},{18,17},{21,22},{26,25},{29,30}} | collective-permute-start | bytes 1966088 | tf_op jit(solution)/shard_map/ppermute | solution.py:322
  58.9 1.3 copy-start.1
  60.2 27.8 %collective-permute-start.5 = (f32[80,8,256]{2,1,0:T(8,128)S(1)}, f32[80,8,256]{2,1,0:T(8,128)}, u32[]{:S(2)}, u32[]{:S(2)}) collective-permute-start(f32[80,8,256]{2,1,0:T(8,128)S(1)} %bitcast.42), channel_id=1, source_target_pairs={{3,1},{4,6},{11,9},{12,14},{19,17},{20,22},{27,25},{28,30}} | collective-permute-start | bytes 1966088 | tf_op jit(solution)/shard_map/ppermute | solution.py:322
  87.9 0.9 copy-start.9
  88.8 38.8 %copy-start.2 = (f32[1,4,128,256]{3,2,1,0:T(8,128)S(1)}, f32[1,4,128,256]{3,2,1,0:T(8,128)}, u32[]{:S(2)}) copy-start(f32[1,4,128,256]{3,2,1,0:T(8,128)} %param.8) | copy-start | bytes 1572868
  88.8 38.9 %copy-start.4 = (f32[1,4,128,256]{3,2,1,0:T(8,128)S(1)}, f32[1,4,128,256]{3,2,1,0:T(8,128)}, u32[]{:S(2)}) copy-start(f32[1,4,128,256]{3,2,1,0:T(8,128)} %param.11) | copy-start | bytes 1572868
  88.8 38.9 %copy-start.11 = (s32[4]{0:T(128)S(1)}, s32[4]{0:T(128)}, u32[]{:S(2)}) copy-start(s32[4]{0:T(128)} %broadcast_select_fusion.1.refs_0_) | copy-start | bytes 52
  123.0 8.3 %collective-permute-start.6 = (f32[64,8,256]{2,1,0:T(8,128)}, f32[64,8,256]{2,1,0:T(8,128)S(1)}, u32[]{:S(2)}, u32[]{:S(2)}) collective-permute-start(f32[64,8,256]{2,1,0:T(8,128)} %get-tuple-element.15), channel_id=1, source_target_pairs={{1,0},{6,7},{9,8},{14,15},{17,16},{22,23},{25,24},{30,31}} | collective-permute-start | bytes 1572872 | tf_op jit(solution)/shard_map/ppermute | solution.py:339
  124.3 8.3 %collective-permute-start.7 = (f32[64,8,256]{2,1,0:T(8,128)}, f32[64,8,256]{2,1,0:T(8,128)S(1)}, u32[]{:S(2)}, u32[]{:S(2)}) collective-permute-start(f32[64,8,256]{2,1,0:T(8,128)} %get-tuple-element.16), channel_id=1, source_target_pairs={{1,2},{6,5},{9,10},{14,13},{17,18},{22,21},{25,26},{30,29}} | collective-permute-start | bytes 1572872 | tf_op jit(solution)/shard_map/ppermute | solution.py:339
  125.6 12.6 %collective-permute-start.8 = (f32[64,8,256]{2,1,0:T(8,128)}, f32[64,8,256]{2,1,0:T(8,128)S(1)}, u32[]{:S(2)}, u32[]{:S(2)}) collective-permute-start(f32[64,8,256]{2,1,0:T(8,128)} %get-tuple-element.17), channel_id=1, source_target_pairs={{1,3},{6,4},{9,11},{14,12},{17,19},{22,20},{25,27},{30,28}} | collective-permute-start | bytes 1572872 | tf_op jit(solution)/shard_map/ppermute | solution.py:339
  139.6 17.3 %copy-start.7 = (f32[4,16,8,256]{3,1,2,0:T(8,128)}, f32[4,16,8,256]{3,1,2,0:T(8,128)S(1)}, u32[]{:S(2)}) copy-start(f32[4,16,8,256]{3,1,2,0:T(8,128)S(1)} %copy.27) | copy-start | bytes 1572868
  140.5 13.5 %all-to-all-start = ((f32[8,64,256]{2,1,0:T(8,128)}), f32[8,64,256]{2,1,0:T(8,128)S(1)}, u32[]{:S(2)}, u32[]{:S(2)}) async-start(f32[8,64,256]{2,1,0:T(8,128)} %subtract_select_fusion), calls=%async_computation | async-start | bytes 1048576 | tf_op jit(solution)/shard_map/all_to_all | solution.py:326
  154.0 0.8 copy-start.5
Sparse Core Ops, SparseCore 0:
  9.9 37.8 all-gather.2

commit v4 on v3

--- a/solution.py
+++ b/solution.py
@@ -11,7 +11,7 @@
 COND = 1.0
 SUB = 8
 LANE = 128
-EARLY = 3
+EARLY = 2
 SPAN = 8
 
 
@@ -38,7 +38,7 @@
         blocks = [pack.at[pl.ds(3 * thick, steps * slots * share // SUB)] for pack in packs]
     else:
         states, packs, blocks = take(bricks), take(bricks), take(bricks)
-    outs, (mark,) = take(bricks), take(1)
+    outs = take(bricks)
     field, other, source, capacity, inverse, rhs, kept, current, picked, fixes, held, raw, whole_lists, lists, load_sem, held_sem, list_sem = refs
     stack = slots * share // SUB
 
@@ -204,7 +204,6 @@
     ]
     for copy in stores:
         copy.start()
-    mark[...] = jnp.zeros_like(mark)
     for copy in stores:
         copy.wait()
 
@@ -222,10 +221,9 @@
     cells = planes * rung * SUB * depth
     return pl.pallas_call(
         body,
-        out_shape=[jax.ShapeDtypeStruct((width * rung, SUB, depth), jnp.float32)] * bricks
-        + [jax.ShapeDtypeStruct((SUB, LANE), jnp.float32)],
+        out_shape=[jax.ShapeDtypeStruct((width * rung, SUB, depth), jnp.float32)] * bricks,
         in_specs=[smem] + [hbm] * len(operands),
-        out_specs=[hbm] * bricks + [pl.BlockSpec(memory_space=pltpu.VMEM)],
+        out_specs=[hbm] * bricks,
         scratch_shapes=[
             pltpu.VMEM(wide_shape, jnp.float32),
             pltpu.VMEM(wide_shape, jnp.float32),
@@ -252,20 +250,23 @@
     )(place, *operands)
 
 
-def recurrence(factors, shifts):
-    def body(factor, shift, out):
-        x = shift[0]
+def recurrence(parts):
+    windows, lines, depth = parts.shape
+    share = lines // 2
+
+    def body(part, out):
+        x = part[0, :share]
         out[0] = x
-        for j in range(1, shifts.shape[0]):
+        for j in range(1, windows):
             out[j] = x
-            x = factor[j] * x + shift[j]
-
-    return pl.pallas_call(body, out_shape=jax.ShapeDtypeStruct(shifts.shape, jnp.float32))(factors, shifts)
+            x = part[j, share:] * x + part[j, :share]
+
+    return pl.pallas_call(body, out_shape=jax.ShapeDtypeStruct((windows, share, depth), jnp.float32))(parts)
 
 
 def routes(windows, bricks):
     home = bricks // 2 - 1
-    others = [z for z in range(bricks) if z != home]
+    others = [z for z in range(home + 1, bricks)] + [z for z in range(home)]
 
     def at(t, z):
         return t * bricks + (z if t % 2 == 0 else bricks - 1 - z)
@@ -322,26 +323,22 @@
         return [lax.ppermute(value, axes, pairs) for pairs in rounds]
 
     def swap(value):
-        parts = value.reshape(windows, -1, depth)
-        return lax.all_to_all(parts, "tm", 0, 0, tiled=True)
+        return lax.all_to_all(value, "tm", 0, 0, tiled=True)
 
     packs = [pack] + spread(pack)
     blocks_late = [blocks[cut:]] + spread(blocks[cut:])
-    *states, mark = run_steps(place, None, packs, None, shape, list_rows, 0, early, slots, tile)
-    rough_late, _ = lax.optimization_barrier((rough, mark))
-    factors = lax.all_gather(rough_late, "tm").reshape(windows, windows, -1, depth)
-    factors = lax.dynamic_index_in_dim(factors, window, 1, keepdims=False)
-    *states, mark = run_steps(place, states, packs, blocks_late, shape, list_rows, early, steps - early, slots, tile)
+    states = run_steps(place, None, packs, None, shape, list_rows, 0, early, slots, tile)
+    states = run_steps(place, states, packs, blocks_late, shape, list_rows, early, steps - early, slots, tile)
 
     held_here = brick == place[0]
     ending = jnp.where(held_here, states[0], 0.0)
-    for pairs, state in zip(rounds, states[1:]):
+    for pairs, state in reversed(list(zip(rounds, states[1:]))):
         ending = ending + lax.ppermute(state, axes, [(b, a) for a, b in pairs])
 
     ending = ending.reshape(width, rung, SUB, depth).swapaxes(1, 2).reshape(width, rows, depth)
     shift = jnp.where(window == 0, ending, ending - rough * opening)
-    shifts = swap(shift)
-    result = swap(recurrence(factors, shifts)).reshape(width, rows, depth)
+    parts = jnp.concatenate([shift.reshape(windows, -1, depth), rough.reshape(windows, -1, depth)], axis=1)
+    result = swap(recurrence(swap(parts))).reshape(width, rows, depth)
     updated = jnp.where(window == 0, opening, result)
     return (updated[None], ending[None])
 

time: 179 us -> 164 us (0.916)
  blocking collectives: 13.1 us -> 32.1 us
  between operations: 14.5 us -> 1.01 us
  waiting for transfers between devices: 60.4 us -> 49.8 us
  local copies, waits for them, and re-layouts: 10.3 us -> 5.84 us
  starting transfers between devices: 16.2 us -> 12.3 us
    all_to_all x1 -> x2, blocking collectives: 13.1 us -> 32.1 us  [swap(): return lax.all_to_all(value, 'tm', 0, 0, tiled=True)]
    all_to_all x1 -> x0, waiting for transfers between devices: 7.84 us -> none  [swap(): return lax.all_to_all(parts, 'tm', 0, 0, tiled=True)]
    all_to_all x1 -> x0, starting transfers between devices: 3.72 us -> none  [swap(): return lax.all_to_all(parts, 'tm', 0, 0, tiled=True)]
    ppermute x6, waiting for transfers between devices: 41.4 us -> 39.2 us  [spread(): return [lax.ppermute(value, axes, pairs) for pairs in rounds]]
    unnamed x36 -> x24, local copies, waits for them, and re-layouts: 3.94 us -> 2.01 us
    another operation x2, local copies, waits for them, and re-layouts: 3.55 us -> 1.66 us  [blocked(): value.reshape(-1, SUB, rung, depth).swapaxes(1, 2).reshape(-1, SUB, depth)]
    squeeze x1 -> x0, local copies, waits for them, and re-layouts: 1.88 us -> none  [shards(): factors = lax.dynamic_index_in_dim(factors, window, 1, keepdims=False)]
  transfers between devices with their start and end apart: 11 -> 9, of which waited for: 6 -> 6; matrix products, arithmetic and copies ran while one was open for 6% -> 1% of each run, Pallas kernels for 32% -> 10%
where the time goes in v4:
time: 164 us; the launch traced here: 163 us
  Pallas kernels  57.9 us (35%)
  waiting for transfers between devices  49.8 us (30%)
  blocking collectives  32.1 us (20%)
  starting transfers between devices  12.3 us (8%)
  local copies, waits for them, and re-layouts  5.84 us (4%)
  other arithmetic  4.12 us (3%)
    pallas_call x2, Pallas kernels, run_steps(): pl.pallas_call(body, out_shape=[jax.ShapeDtypeStruct((width * rung, SUB,...  55.8 us
    ppermute x6, waiting for transfers between devices, spread(): return [lax.ppermute(value, axes, pairs) for pairs in rounds]  39.2 us
    all_to_all x2, blocking collectives, swap(): return lax.all_to_all(value, 'tm', 0, 0, tiled=True)  32.1 us
    ppermute x3, waiting for transfers between devices, shards(): ending = ending + lax.ppermute(state, axes, [(b, a) for a, b in pairs])  10.7 us
    ppermute x6, starting transfers between devices, spread(): return [lax.ppermute(value, axes, pairs) for pairs in rounds]  7.74 us
    ppermute x3, starting transfers between devices, shards(): ending = ending + lax.ppermute(state, axes, [(b, a) for a, b in pairs])  4.54 us
  transfers between devices with their start and end apart: 9, of which 6 were waited for; matrix products, arithmetic and copies ran while one was open for 1% of the time, Pallas kernels for 10%

profile of v4, /device:TPU:8, one launch (start us, length us, event | category | flops | bytes accessed | tf_op | source)
XLA Modules:
  0.0 163.1 jit_solution(17743225454856094123)
XLA Ops:
  0.6 0.0 copy-start.2
  0.6 0.8 fusion.2
  1.5 0.1 copy.18
  1.6 0.1 convert_element_type.16
  1.7 0.0 copy-start.5
  1.7 1.5 copy.17
  3.2 1.4 copy.16
  4.6 0.0 copy-done.2
  4.6 0.3 copy.15
  4.9 0.0 copy-done.5
  4.9 0.3 fusion.13
  5.3 0.2 pad_maximum_fusion.4
  5.5 0.0 copy-start.8
  5.5 0.0 copy-start.9
  5.6 1.3 collective-permute-start.2
  6.9 1.3 collective-permute-start.1
  8.2 1.3 collective-permute-start
  9.5 0.4 pad_maximum_fusion.1
  9.8 1.3 collective-permute-start.5
  11.1 1.3 collective-permute-start.4
  12.4 36.9 %collective-permute-done.2.refs_4_.refs_8_ = f32[225,8,256]{2,1,0:T(8,128)S(1)} collective-permute-done((f32[225,8,256]{2,1,0:T(8,128)S(1)}, f32[225,8,256]{2,1,0:T(8,128)S(1)}, u32[]{:S(2)}, u32[]{:S(2)}) %collective-permute-start.2) | collective-permute-done | bytes 1843232 | tf_op jit(solution)/shard_map/ppermute | solution.py:323
  49.3 1.3 copy-done.1
  50.6 1.3 collective-permute-start.3
  51.9 0.5 broadcast_select_fusion.1.refs_0_
  52.4 0.5 collective-permute-done.1.refs_3_.refs_7_
  52.9 0.3 collective-permute-done.refs_2_.refs_6_
  53.2 16.6 %shard_map.95 = (f32[64,8,256]{2,1,0:T(8,128)}, f32[64,8,256]{2,1,0:T(8,128)}, f32[64,8,256]{2,1,0:T(8,128)}, f32[64,8,256]{2,1,0:T(8,128)}) custom-call(s32[4]{0:T(128)} %broadcast_select_fusion.1.refs_0_, f32[225,8,256]{2,1,0:T(8,128)} %copy-done, f32[225,8,256]{2,1,0:T(8,128)} %collective-permute-done.refs_2_.refs_6_, ...), custom_call_target="tpu_custom_call" | custom-call | flops 41943040 | bytes 33554432 | tf_op jit(solution)/shard_map/pallas_call | solution.py:222
  69.8 0.0 collective-permute-done.5.refs_12_
  69.8 0.0 collective-permute-done.4.refs_11_
  69.8 1.5 collective-permute-done.3.refs_10_
  71.4 39.2 %shard_map.96 = (f32[64,8,256]{2,1,0:T(8,128)}, f32[64,8,256]{2,1,0:T(8,128)}, f32[64,8,256]{2,1,0:T(8,128)}, f32[64,8,256]{2,1,0:T(8,128)}) custom-call(s32[4]{0:T(128)} %broadcast_select_fusion.1.refs_0_, f32[64,8,256]{2,1,0:T(8,128)} %get-tuple-element.10.refs_1_, f32[64,8,256]{2,1,0:T(8,128)} %get-tuple-element.11.refs_2_, ...), custom_call_target="tpu_custom_call" | custom-call | flops 125829120 | bytes 100663296 | tf_op jit(solution)/shard_map/pallas_call | solution.py:222
  110.6 1.3 collective-permute-start.6
  111.9 1.3 collective-permute-start.7
  113.2 1.9 %collective-permute-start.8 = (f32[64,8,256]{2,1,0:T(8,128)}, f32[64,8,256]{2,1,0:T(8,128)S(1)}, u32[]{:S(2)}, u32[]{:S(2)}) collective-permute-start(f32[64,8,256]{2,1,0:T(8,128)} %get-tuple-element.17), channel_id=1, source_target_pairs={{1,2},{6,5},{9,10},{14,13},{17,18},{22,21},{25,26},{30,29}} | collective-permute-start | bytes 1572872 | tf_op jit(solution)/shard_map/ppermute | solution.py:336
  115.2 0.0 copy-start.6
  115.2 8.4 %collective-permute-done.6 = f32[64,8,256]{2,1,0:T(8,128)S(1)} collective-permute-done((f32[64,8,256]{2,1,0:T(8,128)}, f32[64,8,256]{2,1,0:T(8,128)S(1)}, u32[]{:S(2)}, u32[]{:S(2)}) %collective-permute-start.6) | collective-permute-done | bytes 524320 | tf_op jit(solution)/shard_map/ppermute | solution.py:336
  123.6 0.0 collective-permute-done.7
  123.6 2.2 %collective-permute-done.8 = f32[64,8,256]{2,1,0:T(8,128)S(1)} collective-permute-done((f32[64,8,256]{2,1,0:T(8,128)}, f32[64,8,256]{2,1,0:T(8,128)S(1)}, u32[]{:S(2)}, u32[]{:S(2)}) %collective-permute-start.8) | collective-permute-done | bytes 524320 | tf_op jit(solution)/shard_map/ppermute | solution.py:336
  125.9 1.2 add_add_fusion
  127.0 0.2 copy.19
  127.2 0.0 copy-start.4
  127.2 0.1 subtract_select_fusion
  127.4 0.1 pad_maximum_fusion
  127.4 0.6 copy-done.4
  128.0 19.0 %all_to_all.10.part = f32[8,128,256]{2,1,0:T(8,128)} all-to-all(f32[8,128,256]{2,1,0:T(8,128)S(1)} %pad_maximum_fusion), channel_id=1, replica_groups=mesh['tm'=8,'space'=4] {'tm'}, dimensions={0} | all-to-all | bytes 2097152 | tf_op jit(solution)/shard_map/all_to_all | solution.py:326
  147.0 2.1 %shard_map.97 = f32[8,64,256]{2,1,0:T(8,128)} custom-call(f32[8,128,256]{2,1,0:T(8,128)} %all_to_all.10.part), custom_call_target="tpu_custom_call" | custom-call | tf_op jit(solution)/shard_map/pallas_call | solution.py:264
  149.0 13.1 %all_to_all.11 = f32[8,64,256]{2,1,0:T(8,128)S(1)} all-to-all(f32[8,64,256]{2,1,0:T(8,128)} %shard_map.97), channel_id=1, replica_groups=mesh['tm'=8,'space'=4] {'tm'}, dimensions={0} | all-to-all | bytes 1048576 | tf_op jit(solution)/shard_map/all_to_all | solution.py:326
  162.2 0.9 broadcast_select_fusion
  (16 shorter events, 0.2 us)
Async XLA Ops:
  0.6 3.9 %copy-start.2 = (f32[1,4,128,256]{3,2,1,0:T(8,128)S(1)}, f32[1,4,128,256]{3,2,1,0:T(8,128)}, u32[]{:S(2)}) copy-start(f32[1,4,128,256]{3,2,1,0:T(8,128)} %param.8) | copy-start | bytes 1572868
  1.7 3.2 %copy-start.5 = (f32[8,8,64,64]{3,2,1,0:T(8,128)S(1)}, f32[8,8,64,64]{3,2,1,0:T(8,128)}, u32[]{:S(2)}) copy-start(f32[8,8,64,64]{3,2,1,0:T(8,128)} %param.14) | copy-start | bytes 3145732
  5.5 46.4 %copy-start.8 = (s32[4]{0:T(128)S(1)}, s32[4]{0:T(128)}, u32[]{:S(2)}) copy-start(s32[4]{0:T(128)} %constant.103) | copy-start | bytes 52
  5.5 46.4 %copy-start.9 = (s32[4]{0:T(128)S(1)}, s32[4]{0:T(128)}, u32[]{:S(2)}) copy-start(s32[4]{0:T(128)} %constant.95.clone) | copy-start | bytes 52
  5.5 47.7 %copy-start = (f32[225,8,256]{2,1,0:T(8,128)}, f32[225,8,256]{2,1,0:T(8,128)S(1)}, u32[]{:S(2)}) copy-start(f32[225,8,256]{2,1,0:T(8,128)S(1)} %constant_dynamic-update-slice_fusion.refs_1_.refs_5_) | copy-start | bytes 5529604
  5.6 43.8 %collective-permute-start.2 = (f32[225,8,256]{2,1,0:T(8,128)S(1)}, f32[225,8,256]{2,1,0:T(8,128)S(1)}, u32[]{:S(2)}, u32[]{:S(2)}) collective-permute-start(f32[225,8,256]{2,1,0:T(8,128)S(1)} %constant_dynamic-update-slice_fusion.refs_1_.refs_5_), channel_id=1, source_target_pairs={{0,1},{7,6},{8,9},{15,14},{16,17},{23,22},{24,25},{31,30}} | collective-permute-start | bytes 5529608 | tf_op jit(solution)/shard_map/ppermute | solution.py:323
  6.9 46.0 %collective-permute-start.1 = (f32[225,8,256]{2,1,0:T(8,128)S(1)}, f32[225,8,256]{2,1,0:T(8,128)}, u32[]{:S(2)}, u32[]{:S(2)}) collective-permute-start(f32[225,8,256]{2,1,0:T(8,128)S(1)} %constant_dynamic-update-slice_fusion.refs_1_.refs_5_), channel_id=1, source_target_pairs={{3,1},{4,6},{11,9},{12,14},{19,17},{20,22},{27,25},{28,30}} | collective-permute-start | bytes 5529608 | tf_op jit(solution)/shard_map/ppermute | solution.py:323
  8.2 45.1 %collective-permute-start = (f32[225,8,256]{2,1,0:T(8,128)S(1)}, f32[225,8,256]{2,1,0:T(8,128)}, u32[]{:S(2)}, u32[]{:S(2)}) collective-permute-start(f32[225,8,256]{2,1,0:T(8,128)S(1)} %constant_dynamic-update-slice_fusion.refs_1_.refs_5_), channel_id=1, source_target_pairs={{2,1},{5,6},{10,9},{13,14},{18,17},{21,22},{26,25},{29,30}} | collective-permute-start | bytes 5529608 | tf_op jit(solution)/shard_map/ppermute | solution.py:323
  9.8 61.5 %copy-start.3 = (f32[6,8,16,256]{3,2,1,0:T(8,128)}, f32[6,8,16,256]{3,2,1,0:T(8,128)S(1)}, u32[]{:S(2)}) copy-start(f32[6,8,16,256]{3,2,1,0:T(8,128)S(1)} %pad_maximum_fusion.1) | copy-start | bytes 2359300
  9.8 60.0 %collective-permute-start.5 = (f32[96,8,256]{2,1,0:T(8,128)S(1)}, f32[96,8,256]{2,1,0:T(8,128)}, u32[]{:S(2)}, u32[]{:S(2)}) collective-permute-start(f32[96,8,256]{2,1,0:T(8,128)S(1)} %bitcast.36), channel_id=1, source_target_pairs={{0,1},{7,6},{8,9},{15,14},{16,17},{23,22},{24,25},{31,30}} | collective-permute-start | bytes 2359304 | tf_op jit(solution)/shard_map/ppermute | solution.py:323
  11.1 58.7 %collective-permute-start.4 = (f32[96,8,256]{2,1,0:T(8,128)S(1)}, f32[96,8,256]{2,1,0:T(8,128)}, u32[]{:S(2)}, u32[]{:S(2)}) collective-permute-start(f32[96,8,256]{2,1,0:T(8,128)S(1)} %bitcast.37), channel_id=1, source_target_pairs={{3,1},{4,6},{11,9},{12,14},{19,17},{20,22},{27,25},{28,30}} | collective-permute-start | bytes 2359304 | tf_op jit(solution)/shard_map/ppermute | solution.py:323
  49.3 1.3 copy-start.1
  50.6 20.8 %collective-permute-start.3 = (f32[96,8,256]{2,1,0:T(8,128)S(1)}, f32[96,8,256]{2,1,0:T(8,128)}, u32[]{:S(2)}, u32[]{:S(2)}) collective-permute-start(f32[96,8,256]{2,1,0:T(8,128)S(1)} %bitcast.38), channel_id=1, source_target_pairs={{2,1},{5,6},{10,9},{13,14},{18,17},{21,22},{26,25},{29,30}} | collective-permute-start | bytes 2359304 | tf_op jit(solution)/shard_map/ppermute | solution.py:323
  71.4 43.8 %copy-start.7 = (s32[4]{0:T(128)S(1)}, s32[4]{0:T(128)}, u32[]{:S(2)}) copy-start(s32[4]{0:T(128)} %broadcast_select_fusion.1.refs_0_) | copy-start | bytes 52
  110.6 13.1 %collective-permute-start.6 = (f32[64,8,256]{2,1,0:T(8,128)}, f32[64,8,256]{2,1,0:T(8,128)S(1)}, u32[]{:S(2)}, u32[]{:S(2)}) collective-permute-start(f32[64,8,256]{2,1,0:T(8,128)} %get-tuple-element.15), channel_id=1, source_target_pairs={{1,0},{6,7},{9,8},{14,15},{17,16},{22,23},{25,24},{30,31}} | collective-permute-start | bytes 1572872 | tf_op jit(solution)/shard_map/ppermute | solution.py:336
  111.9 11.7 %collective-permute-start.7 = (f32[64,8,256]{2,1,0:T(8,128)}, f32[64,8,256]{2,1,0:T(8,128)S(1)}, u32[]{:S(2)}, u32[]{:S(2)}) collective-permute-start(f32[64,8,256]{2,1,0:T(8,128)} %get-tuple-element.16), channel_id=1, source_target_pairs={{1,3},{6,4},{9,11},{14,12},{17,19},{22,20},{25,27},{30,28}} | collective-permute-start | bytes 1572872 | tf_op jit(solution)/shard_map/ppermute | solution.py:336
  113.2 12.6 %collective-permute-start.8 = (f32[64,8,256]{2,1,0:T(8,128)}, f32[64,8,256]{2,1,0:T(8,128)S(1)}, u32[]{:S(2)}, u32[]{:S(2)}) collective-permute-start(f32[64,8,256]{2,1,0:T(8,128)} %get-tuple-element.17), channel_id=1, source_target_pairs={{1,2},{6,5},{9,10},{14,13},{17,18},{22,21},{25,26},{30,29}} | collective-permute-start | bytes 1572872 | tf_op jit(solution)/shard_map/ppermute | solution.py:336
  115.2 12.1 %copy-start.6 = (f32[1,4,128,256]{3,2,1,0:T(8,128)S(1)}, f32[1,4,128,256]{3,2,1,0:T(8,128)}, u32[]{:S(2)}) copy-start(f32[1,4,128,256]{3,2,1,0:T(8,128)} %param.11) | copy-start | bytes 1572868
  127.2 0.8 copy-start.4

commit v5 on v4

--- a/solution.py
+++ b/solution.py
@@ -12,11 +12,12 @@
 SUB = 8
 LANE = 128
 EARLY = 2
-SPAN = 8
-
-
-def span_of(planes):
-    return max(n for n in range(1, SPAN + 1) if planes % n == 0)
+SPAN = 4
+CHUNKS = 4
+
+
+def span_of(planes, most):
+    return max(n for n in range(1, most + 1) if planes % n == 0)
 
 
 def steps_kernel(shape, slots, tile, first, steps, own_blocks, *refs):
@@ -94,7 +95,8 @@
     line = lax.broadcasted_iota(jnp.int32, (depth, depth), 0)
     column = lax.broadcasted_iota(jnp.int32, (depth, depth), 1)
     beside = jnp.where(jnp.abs(line - column) == 1, 1.0, 0.0).astype(jnp.bfloat16)
-    span = span_of(planes)
+    span = span_of(planes, SPAN)
+    chunks = span_of(planes // span, CHUNKS)
 
     def split(value):
         coarse = value.astype(jnp.bfloat16)
@@ -107,38 +109,53 @@
         )
 
     def sweep(src, dst, opening):
-        def chunk(n, _):
+        def sides_of(n):
             whole = src[pl.ds((n * span + 1) * rung, span * rung)].reshape(span * rung * SUB, depth)
-            along = product(whole, beside).reshape(span * rung, SUB, depth)
-            for p in range(span):
-                x = (n * span + p) * rung
-                center = [[src[x + rung + r, :, pl.ds(h * LANE, LANE)] for h in range(half)] for r in range(rung)]
+            return product(whole, beside).reshape(span * rung, SUB, depth)
+
+        def update(n, along):
+            base = n * span * rung
+            for h in range(half):
+                lanes = pl.ds(h * LANE, LANE)
+
+                def line_of(r, lead, tail):
+                    return [src[base + q * rung + r, :, lanes] for q in range(lead, span + 2 - tail)]
+
+                above = [jnp.where(top, 0.0, pltpu.roll(v, 1, 0)) for v in line_of(rung - 1, 1, 1)]
+                line = line_of(0, 0, 0)
                 for r in range(rung):
-                    for h in range(half):
-                        lanes = pl.ds(h * LANE, LANE)
-                        if r:
-                            above = center[r - 1][h]
+                    if r + 1 < rung:
+                        after = line_of(r + 1, 0, 0)
+                        below = after[1:-1]
+                    else:
+                        after = None
+                        below = [jnp.where(bottom, 0.0, pltpu.roll(v, SUB - 1, 0)) for v in line_of(0, 1, 1)]
+                    for p in range(span):
+                        at = base + p * rung + r
+                        total = (line[p] + line[p + 2]) + (above[p] + below[p])
+                        total = total + along[p * rung + r, :, h * LANE : (h + 1) * LANE]
+                        if opening:
+                            start = capacity[at, :, lanes] * line[p + 1] + source[at, :, lanes]
+                            rhs[at, :, lanes] = start
                         else:
-                            above = jnp.where(top, 0.0, pltpu.roll(center[rung - 1][h], 1, 0))
-                        if r + 1 < rung:
-                            below = center[r + 1][h]
-                        else:
-                            below = jnp.where(bottom, 0.0, pltpu.roll(center[0][h], SUB - 1, 0))
-                        total = src[x + r, :, lanes] + src[x + 2 * rung + r, :, lanes]
-                        total = total + (above + below) + along[p * rung + r, :, h * LANE : (h + 1) * LANE]
-                        if opening:
-                            base = capacity[x + r, :, lanes] * center[r][h] + source[x + r, :, lanes]
-                            rhs[x + r, :, lanes] = base
-                        else:
-                            base = rhs[x + r, :, lanes]
-                        dst[x + rung + r, :, lanes] = (base + COND * total) * inverse[x + r, :, lanes]
+                            start = rhs[at, :, lanes]
+                        dst[at + rung, :, lanes] = (start + COND * total) * inverse[at, :, lanes]
+                    above, line = line[1:-1], after
+
+        def batch(m, _):
+            along = sides_of(m * chunks)
+            for n in range(chunks):
+                coming = sides_of(m * chunks + n + 1) if n + 1 < chunks else None
+                update(m * chunks + n, along)
+                along = coming
             return 0
 
-        lax.fori_loop(0, planes // span, chunk, 0)
+        lax.fori_loop(0, planes // (span * chunks), batch, 0)
 
     quarter = lax.broadcasted_iota(jnp.int32, (1, depth), 1) // tile
     group = depth // tile
     gathers = jnp.where(line // tile == (column % tile) // share, 1.0, 0.0).astype(jnp.bfloat16)
+    repeats = jnp.where(line % tile == column % tile, 1.0, 0.0).astype(jnp.bfloat16)
     own_line = lax.broadcasted_iota(jnp.int32, (share, depth), 0)
     own_lane = lax.broadcasted_iota(jnp.int32, (share, depth), 1)
     diagonal = own_line == own_lane % share
@@ -171,26 +188,20 @@
             value = field[x, pl.ds(u, 1), :]
             current[n : n + 1, :] = value
             delta = jnp.where(quarter == part, value - kept[n : n + 1, :], 0.0)
-            whole = delta
-            for g in range(1, group):
-                whole = whole + pltpu.roll(delta, g * tile, 1)
-            picked[n : n + 1, :] = whole
+            picked[n : n + 1, :] = delta
         for copy in fetch_blocks(step, slot):
             copy.wait()
 
-        def multiply(b, _):
-            terms = [
-                held[slot, b, pl.ds(s * (share // SUB), share // SUB)].reshape(share, depth)
-                * picked[pl.ds(b * slots + s, 1), :]
-                for s in range(slots)
-            ]
-            sums = product(jnp.concatenate(terms, axis=0), gathers)
-            for s in range(slots):
-                fix = jnp.where(diagonal, sums[s * share : (s + 1) * share], 0.0)
-                fixes[pl.ds(b * slots + s, 1), :] = jnp.sum(fix, axis=0, keepdims=True)
-            return 0
-
-        lax.fori_loop(0, bricks, multiply, 0)
+        picked[...] = product(picked[...], repeats)
+        thin = share // SUB
+        terms = []
+        for n, (i, s) in enumerate(tiles):
+            block = held[slot, i, pl.ds(s * thin, thin)].reshape(share, depth)
+            terms.append(block * picked[n : n + 1, :])
+        sums = product(jnp.concatenate(terms, axis=0), gathers)
+        for n in range(count):
+            fix = jnp.where(diagonal, sums[n * share : (n + 1) * share], 0.0)
+            fixes[n : n + 1, :] = jnp.sum(fix, axis=0, keepdims=True)
 
         for n, (i, s) in enumerate(tiles):
             x, u, part = cell_of(step, i, s)

time: 164 us -> 158 us (0.963)
  Pallas kernels: 57.9 us -> 50.6 us
  waiting for transfers between devices: 49.8 us -> 52 us
    pallas_call x2, Pallas kernels: 55.8 us -> 48.5 us  [run_steps(): pl.pallas_call(body, out_shape=[jax.ShapeDtypeStruct((width * rung, SUB,...]
  transfers between devices with their start and end apart: 9 -> 9, of which waited for: 6 -> 6; matrix products, arithmetic and copies ran while one was open for 1% -> 1% of each run, Pallas kernels for 10% -> 9%
where the time goes in v5:
time: 158 us
  waiting for transfers between devices  52 us (33%)
  Pallas kernels  50.6 us (32%)
  blocking collectives  32.1 us (20%)
  starting transfers between devices  11.9 us (8%)
  local copies, waits for them, and re-layouts  5.84 us (4%)
  other arithmetic  4.12 us (3%)
    pallas_call x2, Pallas kernels, run_steps(): pl.pallas_call(body, out_shape=[jax.ShapeDtypeStruct((width * rung, SUB,...  48.5 us
    ppermute x6, waiting for transfers between devices, spread(): return [lax.ppermute(value, axes, pairs) for pairs in rounds]  40.8 us
    all_to_all x2, blocking collectives, swap(): return lax.all_to_all(value, 'tm', 0, 0, tiled=True)  32.1 us
    ppermute x3, waiting for transfers between devices, shards(): ending = ending + lax.ppermute(state, axes, [(b, a) for a, b in pairs])  11.2 us
    ppermute x6, starting transfers between devices, spread(): return [lax.ppermute(value, axes, pairs) for pairs in rounds]  7.92 us
    ppermute x3, starting transfers between devices, shards(): ending = ending + lax.ppermute(state, axes, [(b, a) for a, b in pairs])  3.97 us
  transfers between devices with their start and end apart: 9, of which 6 were waited for; matrix products, arithmetic and copies ran while one was open for 1% of the time, Pallas kernels for 9%

profile of v5, /device:TPU:8, one launch (start us, length us, event | category | flops | bytes accessed | tf_op | source)
XLA Modules:
  0.0 157.6 jit_solution(14849685058559050936)
XLA Ops:
  0.6 0.8 fusion.2
  1.5 0.1 copy.18
  1.6 0.1 convert_element_type.16
  1.7 0.0 copy-start.5
  1.7 1.5 copy.17
  3.2 1.4 copy.16
  4.6 0.3 copy.15
  4.9 0.3 fusion.13
  5.3 0.2 pad_maximum_fusion.4
  5.5 0.0 copy-start.8
  5.5 0.0 copy-start.9
  5.6 1.3 collective-permute-start.2
  6.9 1.3 collective-permute-start.1
  8.2 1.3 collective-permute-start
  9.5 0.4 pad_maximum_fusion.1
  9.8 0.0 copy-start.3
  9.8 1.3 collective-permute-start.5
  11.1 1.3 collective-permute-start.4
  12.4 36.9 %collective-permute-done.2.refs_4_.refs_8_ = f32[225,8,256]{2,1,0:T(8,128)S(1)} collective-permute-done((f32[225,8,256]{2,1,0:T(8,128)S(1)}, f32[225,8,256]{2,1,0:T(8,128)S(1)}, u32[]{:S(2)}, u32[]{:S(2)}) %collective-permute-start.2) | collective-permute-done | bytes 1843232 | tf_op jit(solution)/shard_map/ppermute | solution.py:334
  49.3 1.3 copy-done.1
  50.6 1.5 collective-permute-start.3
  52.0 0.0 copy-done.8
  52.1 0.0 copy-done.9
  52.1 0.5 broadcast_select_fusion.1.refs_0_
  52.6 0.3 collective-permute-done.1.refs_3_.refs_7_
  52.9 0.3 collective-permute-done.refs_2_.refs_6_
  53.2 14.8 %shard_map.95 = (f32[64,8,256]{2,1,0:T(8,128)}, f32[64,8,256]{2,1,0:T(8,128)}, f32[64,8,256]{2,1,0:T(8,128)}, f32[64,8,256]{2,1,0:T(8,128)}) custom-call(s32[4]{0:T(128)} %broadcast_select_fusion.1.refs_0_, f32[225,8,256]{2,1,0:T(8,128)} %copy-done, f32[225,8,256]{2,1,0:T(8,128)} %collective-permute-done.refs_2_.refs_6_, ...), custom_call_target="tpu_custom_call" | custom-call | flops 41943040 | bytes 33554432 | tf_op jit(solution)/shard_map/pallas_call | solution.py:233
  68.0 0.0 collective-permute-done.5.refs_12_
  68.0 0.0 collective-permute-done.4.refs_11_
  68.0 3.3 %collective-permute-done.3.refs_10_ = f32[96,8,256]{2,1,0:T(8,128)} collective-permute-done((f32[96,8,256]{2,1,0:T(8,128)S(1)}, f32[96,8,256]{2,1,0:T(8,128)}, u32[]{:S(2)}, u32[]{:S(2)}) %collective-permute-start.3) | collective-permute-done | bytes 786464 | tf_op jit(solution)/shard_map/ppermute | solution.py:334
  71.4 33.8 %shard_map.96 = (f32[64,8,256]{2,1,0:T(8,128)}, f32[64,8,256]{2,1,0:T(8,128)}, f32[64,8,256]{2,1,0:T(8,128)}, f32[64,8,256]{2,1,0:T(8,128)}) custom-call(s32[4]{0:T(128)} %broadcast_select_fusion.1.refs_0_, f32[64,8,256]{2,1,0:T(8,128)} %get-tuple-element.10.refs_1_, f32[64,8,256]{2,1,0:T(8,128)} %get-tuple-element.11.refs_2_, ...), custom_call_target="tpu_custom_call" | custom-call | flops 125829120 | bytes 100663296 | tf_op jit(solution)/shard_map/pallas_call | solution.py:233
  105.1 1.3 collective-permute-start.6
  106.5 1.3 collective-permute-start.7
  107.8 1.3 collective-permute-start.8
  109.1 0.0 copy-start.6
  109.2 9.0 %collective-permute-done.6 = f32[64,8,256]{2,1,0:T(8,128)S(1)} collective-permute-done((f32[64,8,256]{2,1,0:T(8,128)}, f32[64,8,256]{2,1,0:T(8,128)S(1)}, u32[]{:S(2)}, u32[]{:S(2)}) %collective-permute-start.6) | collective-permute-done | bytes 524320 | tf_op jit(solution)/shard_map/ppermute | solution.py:347
  118.2 0.0 collective-permute-done.7
  118.2 2.2 %collective-permute-done.8 = f32[64,8,256]{2,1,0:T(8,128)S(1)} collective-permute-done((f32[64,8,256]{2,1,0:T(8,128)}, f32[64,8,256]{2,1,0:T(8,128)S(1)}, u32[]{:S(2)}, u32[]{:S(2)}) %collective-permute-start.8) | collective-permute-done | bytes 524320 | tf_op jit(solution)/shard_map/ppermute | solution.py:347
  120.4 1.2 add_add_fusion
  121.6 0.2 copy.19
  121.8 0.0 copy-start.4
  121.8 0.1 subtract_select_fusion
  121.9 0.1 pad_maximum_fusion
  122.0 0.6 copy-done.4
  122.6 19.0 %all_to_all.10.part = f32[8,128,256]{2,1,0:T(8,128)} all-to-all(f32[8,128,256]{2,1,0:T(8,128)S(1)} %pad_maximum_fusion), channel_id=1, replica_groups=mesh['tm'=8,'space'=4] {'tm'}, dimensions={0} | all-to-all | bytes 2097152 | tf_op jit(solution)/shard_map/all_to_all | solution.py:337
  141.6 2.1 %shard_map.97 = f32[8,64,256]{2,1,0:T(8,128)} custom-call(f32[8,128,256]{2,1,0:T(8,128)} %all_to_all.10.part), custom_call_target="tpu_custom_call" | custom-call | tf_op jit(solution)/shard_map/pallas_call | solution.py:275
  143.6 13.1 %all_to_all.11 = f32[8,64,256]{2,1,0:T(8,128)S(1)} all-to-all(f32[8,64,256]{2,1,0:T(8,128)} %shard_map.97), channel_id=1, replica_groups=mesh['tm'=8,'space'=4] {'tm'}, dimensions={0} | all-to-all | bytes 1048576 | tf_op jit(solution)/shard_map/all_to_all | solution.py:337
  156.8 0.9 broadcast_select_fusion
  (16 shorter events, 0.2 us)
Async XLA Ops:
  0.6 3.9 %copy-start.2 = (f32[1,4,128,256]{3,2,1,0:T(8,128)S(1)}, f32[1,4,128,256]{3,2,1,0:T(8,128)}, u32[]{:S(2)}) copy-start(f32[1,4,128,256]{3,2,1,0:T(8,128)} %param.8) | copy-start | bytes 1572868
  1.7 3.2 %copy-start.5 = (f32[8,8,64,64]{3,2,1,0:T(8,128)S(1)}, f32[8,8,64,64]{3,2,1,0:T(8,128)}, u32[]{:S(2)}) copy-start(f32[8,8,64,64]{3,2,1,0:T(8,128)} %param.14) | copy-start | bytes 3145732
  5.5 46.6 %copy-start.8 = (s32[4]{0:T(128)S(1)}, s32[4]{0:T(128)}, u32[]{:S(2)}) copy-start(s32[4]{0:T(128)} %constant.103) | copy-start | bytes 52
  5.5 46.6 %copy-start.9 = (s32[4]{0:T(128)S(1)}, s32[4]{0:T(128)}, u32[]{:S(2)}) copy-start(s32[4]{0:T(128)} %constant.95.clone) | copy-start | bytes 52
  5.5 47.7 %copy-start = (f32[225,8,256]{2,1,0:T(8,128)}, f32[225,8,256]{2,1,0:T(8,128)S(1)}, u32[]{:S(2)}) copy-start(f32[225,8,256]{2,1,0:T(8,128)S(1)} %constant_dynamic-update-slice_fusion.refs_1_.refs_5_) | copy-start | bytes 5529604
  5.6 43.8 %collective-permute-start.2 = (f32[225,8,256]{2,1,0:T(8,128)S(1)}, f32[225,8,256]{2,1,0:T(8,128)S(1)}, u32[]{:S(2)}, u32[]{:S(2)}) collective-permute-start(f32[225,8,256]{2,1,0:T(8,128)S(1)} %constant_dynamic-update-slice_fusion.refs_1_.refs_5_), channel_id=1, source_target_pairs={{0,1},{7,6},{8,9},{15,14},{16,17},{23,22},{24,25},{31,30}} | collective-permute-start | bytes 5529608 | tf_op jit(solution)/shard_map/ppermute | solution.py:334
  6.9 46.0 %collective-permute-start.1 = (f32[225,8,256]{2,1,0:T(8,128)S(1)}, f32[225,8,256]{2,1,0:T(8,128)}, u32[]{:S(2)}, u32[]{:S(2)}) collective-permute-start(f32[225,8,256]{2,1,0:T(8,128)S(1)} %constant_dynamic-update-slice_fusion.refs_1_.refs_5_), channel_id=1, source_target_pairs={{3,1},{4,6},{11,9},{12,14},{19,17},{20,22},{27,25},{28,30}} | collective-permute-start | bytes 5529608 | tf_op jit(solution)/shard_map/ppermute | solution.py:334
  8.2 45.1 %collective-permute-start = (f32[225,8,256]{2,1,0:T(8,128)S(1)}, f32[225,8,256]{2,1,0:T(8,128)}, u32[]{:S(2)}, u32[]{:S(2)}) collective-permute-start(f32[225,8,256]{2,1,0:T(8,128)S(1)} %constant_dynamic-update-slice_fusion.refs_1_.refs_5_), channel_id=1, source_target_pairs={{2,1},{5,6},{10,9},{13,14},{18,17},{21,22},{26,25},{29,30}} | collective-permute-start | bytes 5529608 | tf_op jit(solution)/shard_map/ppermute | solution.py:334
  9.8 61.5 %copy-start.3 = (f32[6,8,16,256]{3,2,1,0:T(8,128)}, f32[6,8,16,256]{3,2,1,0:T(8,128)S(1)}, u32[]{:S(2)}) copy-start(f32[6,8,16,256]{3,2,1,0:T(8,128)S(1)} %pad_maximum_fusion.1) | copy-start | bytes 2359300
  9.8 58.2 %collective-permute-start.5 = (f32[96,8,256]{2,1,0:T(8,128)S(1)}, f32[96,8,256]{2,1,0:T(8,128)}, u32[]{:S(2)}, u32[]{:S(2)}) collective-permute-start(f32[96,8,256]{2,1,0:T(8,128)S(1)} %bitcast.36), channel_id=1, source_target_pairs={{0,1},{7,6},{8,9},{15,14},{16,17},{23,22},{24,25},{31,30}} | collective-permute-start | bytes 2359304 | tf_op jit(solution)/shard_map/ppermute | solution.py:334
  11.1 56.9 %collective-permute-start.4 = (f32[96,8,256]{2,1,0:T(8,128)S(1)}, f32[96,8,256]{2,1,0:T(8,128)}, u32[]{:S(2)}, u32[]{:S(2)}) collective-permute-start(f32[96,8,256]{2,1,0:T(8,128)S(1)} %bitcast.37), channel_id=1, source_target_pairs={{3,1},{4,6},{11,9},{12,14},{19,17},{20,22},{27,25},{28,30}} | collective-permute-start | bytes 2359304 | tf_op jit(solution)/shard_map/ppermute | solution.py:334
  49.3 1.3 copy-start.1
  50.6 20.8 %collective-permute-start.3 = (f32[96,8,256]{2,1,0:T(8,128)S(1)}, f32[96,8,256]{2,1,0:T(8,128)}, u32[]{:S(2)}, u32[]{:S(2)}) collective-permute-start(f32[96,8,256]{2,1,0:T(8,128)S(1)} %bitcast.38), channel_id=1, source_target_pairs={{2,1},{5,6},{10,9},{13,14},{18,17},{21,22},{26,25},{29,30}} | collective-permute-start | bytes 2359304 | tf_op jit(solution)/shard_map/ppermute | solution.py:334
  71.4 37.8 %copy-start.7 = (s32[4]{0:T(128)S(1)}, s32[4]{0:T(128)}, u32[]{:S(2)}) copy-start(s32[4]{0:T(128)} %broadcast_select_fusion.1.refs_0_) | copy-start | bytes 52
  105.1 13.1 %collective-permute-start.6 = (f32[64,8,256]{2,1,0:T(8,128)}, f32[64,8,256]{2,1,0:T(8,128)S(1)}, u32[]{:S(2)}, u32[]{:S(2)}) collective-permute-start(f32[64,8,256]{2,1,0:T(8,128)} %get-tuple-element.15), channel_id=1, source_target_pairs={{1,0},{6,7},{9,8},{14,15},{17,16},{22,23},{25,24},{30,31}} | collective-permute-start | bytes 1572872 | tf_op jit(solution)/shard_map/ppermute | solution.py:347
  106.5 11.7 %collective-permute-start.7 = (f32[64,8,256]{2,1,0:T(8,128)}, f32[64,8,256]{2,1,0:T(8,128)S(1)}, u32[]{:S(2)}, u32[]{:S(2)}) collective-permute-start(f32[64,8,256]{2,1,0:T(8,128)} %get-tuple-element.16), channel_id=1, source_target_pairs={{1,3},{6,4},{9,11},{14,12},{17,19},{22,20},{25,27},{30,28}} | collective-permute-start | bytes 1572872 | tf_op jit(solution)/shard_map/ppermute | solution.py:347
  107.8 12.6 %collective-permute-start.8 = (f32[64,8,256]{2,1,0:T(8,128)}, f32[64,8,256]{2,1,0:T(8,128)S(1)}, u32[]{:S(2)}, u32[]{:S(2)}) collective-permute-start(f32[64,8,256]{2,1,0:T(8,128)} %get-tuple-element.17), channel_id=1, source_target_pairs={{1,2},{6,5},{9,10},{14,13},{17,18},{22,21},{25,26},{30,29}} | collective-permute-start | bytes 1572872 | tf_op jit(solution)/shard_map/ppermute | solution.py:347
  109.1 12.7 %copy-start.6 = (f32[1,4,128,256]{3,2,1,0:T(8,128)S(1)}, f32[1,4,128,256]{3,2,1,0:T(8,128)}, u32[]{:S(2)}) copy-start(f32[1,4,128,256]{3,2,1,0:T(8,128)} %param.11) | copy-start | bytes 1572868
  121.8 0.8 copy-start.4

commit v6 on v5

--- a/solution.py
+++ b/solution.py
@@ -261,18 +261,15 @@
     )(place, *operands)
 
 
-def recurrence(parts):
-    windows, lines, depth = parts.shape
-    share = lines // 2
-
-    def body(part, out):
-        x = part[0, :share]
+def recurrence(factors, shifts):
+    def body(factor, shift, out):
+        x = shift[0]
         out[0] = x
-        for j in range(1, windows):
+        for j in range(1, shifts.shape[0]):
             out[j] = x
-            x = part[j, share:] * x + part[j, :share]
-
-    return pl.pallas_call(body, out_shape=jax.ShapeDtypeStruct((windows, share, depth), jnp.float32))(parts)
+            x = factor[j] * x + shift[j]
+
+    return pl.pallas_call(body, out_shape=jax.ShapeDtypeStruct(shifts.shape, jnp.float32))(factors, shifts)
 
 
 def routes(windows, bricks):
@@ -341,6 +338,7 @@
     states = run_steps(place, None, packs, None, shape, list_rows, 0, early, slots, tile)
     states = run_steps(place, states, packs, blocks_late, shape, list_rows, early, steps - early, slots, tile)
 
+    factors = swap((rough + states[0][0, 0, 0] * 0.0).reshape(windows, -1, depth))
     held_here = brick == place[0]
     ending = jnp.where(held_here, states[0], 0.0)
     for pairs, state in reversed(list(zip(rounds, states[1:]))):
@@ -348,8 +346,7 @@
 
     ending = ending.reshape(width, rung, SUB, depth).swapaxes(1, 2).reshape(width, rows, depth)
     shift = jnp.where(window == 0, ending, ending - rough * opening)
-    parts = jnp.concatenate([shift.reshape(windows, -1, depth), rough.reshape(windows, -1, depth)], axis=1)
-    result = swap(recurrence(swap(parts))).reshape(width, rows, depth)
+    result = swap(recurrence(factors, swap(shift.reshape(windows, -1, depth)))).reshape(width, rows, depth)
     updated = jnp.where(window == 0, opening, result)
     return (updated[None], ending[None])
 

time: 158 us -> 156 us (0.987)
  blocking collectives: 32.1 us -> 26 us
  starting transfers between devices: 11.9 us -> 16.5 us
  waiting for transfers between devices: 52 us -> 49.1 us
    ppermute x3, waiting for transfers between devices: 11.2 us -> 4.02 us  [shards(): ending = ending + lax.ppermute(state, axes, [(b, a) for a, b in pairs])]
    all_to_all x2, blocking collectives: 32.1 us -> 26 us  [swap(): return lax.all_to_all(value, 'tm', 0, 0, tiled=True)]
    all_to_all x0 -> x1, waiting for transfers between devices: none -> 4.28 us  [swap(): return lax.all_to_all(value, 'tm', 0, 0, tiled=True)]
    all_to_all x0 -> x1, starting transfers between devices: none -> 3.72 us  [swap(): return lax.all_to_all(value, 'tm', 0, 0, tiled=True)]
  transfers between devices with their start and end apart: 9 -> 10, of which waited for: 6 -> 7; matrix products, arithmetic and copies ran while one was open for 1% -> 3% of each run, Pallas kernels for 9% -> 10%
where the time goes in v6:
time: 156 us; the launch traced here: 155 us
  Pallas kernels  50.6 us (32%)
  waiting for transfers between devices  49.1 us (31%)
  blocking collectives  26 us (17%)
  starting transfers between devices  16.5 us (11%)
  local copies, waits for them, and re-layouts  6.44 us (4%)
  other arithmetic  4.9 us (3%)
  between operations  1.64 us (1%)
    pallas_call x2, Pallas kernels, run_steps(): pl.pallas_call(body, out_shape=[jax.ShapeDtypeStruct((width * rung, SUB,...  48.6 us
    ppermute x6, waiting for transfers between devices, spread(): return [lax.ppermute(value, axes, pairs) for pairs in rounds]  40.8 us
    all_to_all x2, blocking collectives, swap(): return lax.all_to_all(value, 'tm', 0, 0, tiled=True)  26 us
    ppermute x6, starting transfers between devices, spread(): return [lax.ppermute(value, axes, pairs) for pairs in rounds]  7.92 us
    ppermute x3, starting transfers between devices, shards(): ending = ending + lax.ppermute(state, axes, [(b, a) for a, b in pairs])  4.89 us
    all_to_all x1, waiting for transfers between devices, swap(): return lax.all_to_all(value, 'tm', 0, 0, tiled=True)  4.28 us
    ppermute x3, waiting for transfers between devices, shards(): ending = ending + lax.ppermute(state, axes, [(b, a) for a, b in pairs])  4.02 us
    all_to_all x1, starting transfers between devices, swap(): return lax.all_to_all(value, 'tm', 0, 0, tiled=True)  3.72 us
  transfers between devices with their start and end apart: 10, of which 7 were waited for; matrix products, arithmetic and copies ran while one was open for 3% of the time, Pallas kernels for 10%

profile of v6, /device:TPU:8, one launch (start us, length us, event | category | flops | bytes accessed | tf_op | source)
XLA Modules:
  0.0 155.2 jit_solution(18334865998734918692)
XLA Ops:
  0.6 0.8 fusion.2
  1.5 0.1 copy.18
  1.6 0.1 convert_element_type.16
  1.7 0.0 copy-start.5
  1.7 1.5 copy.17
  3.2 1.4 copy.16
  4.6 0.3 copy.15
  4.9 0.3 fusion.13
  5.3 0.2 pad_maximum_fusion.3
  5.5 0.0 copy-start.10
  5.5 0.0 copy-start.11
  5.6 1.3 collective-permute-start.2
  6.9 1.3 collective-permute-start.1
  8.2 1.3 collective-permute-start
  9.5 0.4 pad_maximum_fusion
  9.8 1.3 collective-permute-start.5
  11.1 1.3 collective-permute-start.4
  12.4 36.9 %collective-permute-done.2.refs_4_.refs_8_ = f32[225,8,256]{2,1,0:T(8,128)S(1)} collective-permute-done((f32[225,8,256]{2,1,0:T(8,128)S(1)}, f32[225,8,256]{2,1,0:T(8,128)S(1)}, u32[]{:S(2)}, u32[]{:S(2)}) %collective-permute-start.2) | collective-permute-done | bytes 1843232 | tf_op jit(solution)/shard_map/ppermute | solution.py:331
  49.3 1.2 copy-done.1
  50.6 1.5 collective-permute-start.3
  52.1 0.5 broadcast_select_fusion.1.refs_0_
  52.6 0.3 collective-permute-done.1.refs_3_.refs_7_
  52.9 0.3 collective-permute-done.refs_2_.refs_6_
  53.2 14.8 %shard_map.95 = (f32[64,8,256]{2,1,0:T(8,128)}, f32[64,8,256]{2,1,0:T(8,128)}, f32[64,8,256]{2,1,0:T(8,128)}, f32[64,8,256]{2,1,0:T(8,128)}) custom-call(s32[4]{0:T(128)} %broadcast_select_fusion.1.refs_0_, f32[225,8,256]{2,1,0:T(8,128)} %copy-done, f32[225,8,256]{2,1,0:T(8,128)} %collective-permute-done.refs_2_.refs_6_, ...), custom_call_target="tpu_custom_call" | custom-call | flops 41943040 | bytes 33554432 | tf_op jit(solution)/shard_map/pallas_call | solution.py:233
  68.0 0.0 collective-permute-done.5.refs_12_
  68.0 0.0 collective-permute-done.4.refs_11_
  68.0 3.3 %collective-permute-done.3.refs_10_ = f32[96,8,256]{2,1,0:T(8,128)} collective-permute-done((f32[96,8,256]{2,1,0:T(8,128)S(1)}, f32[96,8,256]{2,1,0:T(8,128)}, u32[]{:S(2)}, u32[]{:S(2)}) %collective-permute-start.3) | collective-permute-done | bytes 786464 | tf_op jit(solution)/shard_map/ppermute | solution.py:331
  71.4 0.0 copy-done.3
  71.4 33.8 %shard_map.96 = (f32[64,8,256]{2,1,0:T(8,128)}, f32[64,8,256]{2,1,0:T(8,128)}, f32[64,8,256]{2,1,0:T(8,128)}, f32[64,8,256]{2,1,0:T(8,128)}) custom-call(s32[4]{0:T(128)} %broadcast_select_fusion.1.refs_0_, f32[64,8,256]{2,1,0:T(8,128)} %get-tuple-element.10.refs_1_, f32[64,8,256]{2,1,0:T(8,128)} %get-tuple-element.11.refs_2_, ...), custom_call_target="tpu_custom_call" | custom-call | flops 125829120 | bytes 100663296 | tf_op jit(solution)/shard_map/pallas_call | solution.py:233
  105.2 1.5 collective-permute-start.6
  106.6 1.3 collective-permute-start.7
  108.0 2.1 %collective-permute-start.8 = (f32[64,8,256]{2,1,0:T(8,128)}, f32[64,8,256]{2,1,0:T(8,128)}, u32[]{:S(2)}, u32[]{:S(2)}) collective-permute-start(f32[64,8,256]{2,1,0:T(8,128)} %get-tuple-element.17), channel_id=1, source_target_pairs={{1,2},{6,5},{9,10},{14,13},{17,18},{22,21},{25,26},{30,29}} | collective-permute-start | bytes 1572872 | tf_op jit(solution)/shard_map/ppermute | solution.py:345
  110.1 1.2 slice.39
  111.9 0.0 copy-done.7
  112.0 0.9 fusion.14
  112.8 3.7 %all-to-all-start = ((f32[8,64,256]{2,1,0:T(8,128)}), f32[8,64,256]{2,1,0:T(8,128)S(1)}, u32[]{:S(2)}, u32[]{:S(2)}) async-start(f32[8,64,256]{2,1,0:T(8,128)} %bitcast.17), calls=%async_computation | async-start | bytes 1048576 | tf_op jit(solution)/shard_map/all_to_all | solution.py:334
  116.6 1.8 %collective-permute-done.6 = f32[64,8,256]{2,1,0:T(8,128)S(1)} collective-permute-done((f32[64,8,256]{2,1,0:T(8,128)}, f32[64,8,256]{2,1,0:T(8,128)S(1)}, u32[]{:S(2)}, u32[]{:S(2)}) %collective-permute-start.6) | collective-permute-done | bytes 524320 | tf_op jit(solution)/shard_map/ppermute | solution.py:345
  118.3 0.0 collective-permute-done.7
  118.3 2.2 %collective-permute-done.8 = f32[64,8,256]{2,1,0:T(8,128)} collective-permute-done((f32[64,8,256]{2,1,0:T(8,128)}, f32[64,8,256]{2,1,0:T(8,128)}, u32[]{:S(2)}, u32[]{:S(2)}) %collective-permute-start.8) | collective-permute-done | bytes 524320 | tf_op jit(solution)/shard_map/ppermute | solution.py:345
  120.6 1.2 add_add_fusion
  121.8 0.2 copy.19
  121.9 0.0 copy-start.6
  121.9 0.1 subtract_select_fusion
  122.0 4.3 %all-to-all-done.factor = f32[8,64,256]{2,1,0:T(8,128)S(1)} async-done(((f32[8,64,256]{2,1,0:T(8,128)}), f32[8,64,256]{2,1,0:T(8,128)S(1)}, u32[]{:S(2)}, u32[]{:S(2)}) %all-to-all-start) | async-done | bytes 524320 | tf_op jit(solution)/shard_map/all_to_all | solution.py:334
  126.3 12.8 %all_to_all.15.shift = f32[8,64,256]{2,1,0:T(8,128)} all-to-all(f32[8,64,256]{2,1,0:T(8,128)S(1)} %subtract_select_fusion), channel_id=1, replica_groups=mesh['tm'=8,'space'=4] {'tm'}, dimensions={0} | all-to-all | bytes 1048576 | tf_op jit(solution)/shard_map/all_to_all | solution.py:334
  139.1 2.1 %shard_map.97 = f32[8,64,256]{2,1,0:T(8,128)} custom-call(f32[8,64,256]{2,1,0:T(8,128)} %copy-done.4, f32[8,64,256]{2,1,0:T(8,128)} %all_to_all.15.shift), custom_call_target="tpu_custom_call" | custom-call | tf_op jit(solution)/shard_map/pallas_call | solution.py:272
  141.2 13.1 %all_to_all.16 = f32[8,64,256]{2,1,0:T(8,128)S(1)} all-to-all(f32[8,64,256]{2,1,0:T(8,128)} %shard_map.97), channel_id=1, replica_groups=mesh['tm'=8,'space'=4] {'tm'}, dimensions={0} | all-to-all | bytes 1048576 | tf_op jit(solution)/shard_map/all_to_all | solution.py:334
  154.3 0.9 broadcast_select_fusion
  (23 shorter events, 0.2 us)
Async XLA Ops:
  0.6 3.9 %copy-start.2 = (f32[1,4,128,256]{3,2,1,0:T(8,128)S(1)}, f32[1,4,128,256]{3,2,1,0:T(8,128)}, u32[]{:S(2)}) copy-start(f32[1,4,128,256]{3,2,1,0:T(8,128)} %param.8) | copy-start | bytes 1572868
  1.7 3.2 %copy-start.5 = (f32[8,8,64,64]{3,2,1,0:T(8,128)S(1)}, f32[8,8,64,64]{3,2,1,0:T(8,128)}, u32[]{:S(2)}) copy-start(f32[8,8,64,64]{3,2,1,0:T(8,128)} %param.14) | copy-start | bytes 3145732
  5.5 46.6 %copy-start.10 = (s32[4]{0:T(128)S(1)}, s32[4]{0:T(128)}, u32[]{:S(2)}) copy-start(s32[4]{0:T(128)} %constant.105) | copy-start | bytes 52
  5.5 46.6 %copy-start.11 = (s32[4]{0:T(128)S(1)}, s32[4]{0:T(128)}, u32[]{:S(2)}) copy-start(s32[4]{0:T(128)} %constant.97.clone) | copy-start | bytes 52
  5.5 47.7 %copy-start = (f32[225,8,256]{2,1,0:T(8,128)}, f32[225,8,256]{2,1,0:T(8,128)S(1)}, u32[]{:S(2)}) copy-start(f32[225,8,256]{2,1,0:T(8,128)S(1)} %constant_dynamic-update-slice_fusion.refs_1_.refs_5_) | copy-start | bytes 5529604
  5.6 43.8 %collective-permute-start.2 = (f32[225,8,256]{2,1,0:T(8,128)S(1)}, f32[225,8,256]{2,1,0:T(8,128)S(1)}, u32[]{:S(2)}, u32[]{:S(2)}) collective-permute-start(f32[225,8,256]{2,1,0:T(8,128)S(1)} %constant_dynamic-update-slice_fusion.refs_1_.refs_5_), channel_id=1, source_target_pairs={{0,1},{7,6},{8,9},{15,14},{16,17},{23,22},{24,25},{31,30}} | collective-permute-start | bytes 5529608 | tf_op jit(solution)/shard_map/ppermute | solution.py:331
  6.9 46.0 %collective-permute-start.1 = (f32[225,8,256]{2,1,0:T(8,128)S(1)}, f32[225,8,256]{2,1,0:T(8,128)}, u32[]{:S(2)}, u32[]{:S(2)}) collective-permute-start(f32[225,8,256]{2,1,0:T(8,128)S(1)} %constant_dynamic-update-slice_fusion.refs_1_.refs_5_), channel_id=1, source_target_pairs={{3,1},{4,6},{11,9},{12,14},{19,17},{20,22},{27,25},{28,30}} | collective-permute-start | bytes 5529608 | tf_op jit(solution)/shard_map/ppermute | solution.py:331
  8.2 45.1 %collective-permute-start = (f32[225,8,256]{2,1,0:T(8,128)S(1)}, f32[225,8,256]{2,1,0:T(8,128)}, u32[]{:S(2)}, u32[]{:S(2)}) collective-permute-start(f32[225,8,256]{2,1,0:T(8,128)S(1)} %constant_dynamic-update-slice_fusion.refs_1_.refs_5_), channel_id=1, source_target_pairs={{2,1},{5,6},{10,9},{13,14},{18,17},{21,22},{26,25},{29,30}} | collective-permute-start | bytes 5529608 | tf_op jit(solution)/shard_map/ppermute | solution.py:331
  9.8 61.5 %copy-start.3 = (f32[6,8,16,256]{3,2,1,0:T(8,128)}, f32[6,8,16,256]{3,2,1,0:T(8,128)S(1)}, u32[]{:S(2)}) copy-start(f32[6,8,16,256]{3,2,1,0:T(8,128)S(1)} %pad_maximum_fusion) | copy-start | bytes 2359300
  9.8 58.2 %collective-permute-start.5 = (f32[96,8,256]{2,1,0:T(8,128)S(1)}, f32[96,8,256]{2,1,0:T(8,128)}, u32[]{:S(2)}, u32[]{:S(2)}) collective-permute-start(f32[96,8,256]{2,1,0:T(8,128)S(1)} %bitcast.36), channel_id=1, source_target_pairs={{0,1},{7,6},{8,9},{15,14},{16,17},{23,22},{24,25},{31,30}} | collective-permute-start | bytes 2359304 | tf_op jit(solution)/shard_map/ppermute | solution.py:331
  11.1 56.9 %collective-permute-start.4 = (f32[96,8,256]{2,1,0:T(8,128)S(1)}, f32[96,8,256]{2,1,0:T(8,128)}, u32[]{:S(2)}, u32[]{:S(2)}) collective-permute-start(f32[96,8,256]{2,1,0:T(8,128)S(1)} %bitcast.37), channel_id=1, source_target_pairs={{3,1},{4,6},{11,9},{12,14},{19,17},{20,22},{27,25},{28,30}} | collective-permute-start | bytes 2359304 | tf_op jit(solution)/shard_map/ppermute | solution.py:331
  49.3 1.2 copy-start.1
  50.6 20.8 %collective-permute-start.3 = (f32[96,8,256]{2,1,0:T(8,128)S(1)}, f32[96,8,256]{2,1,0:T(8,128)}, u32[]{:S(2)}, u32[]{:S(2)}) collective-permute-start(f32[96,8,256]{2,1,0:T(8,128)S(1)} %bitcast.38), channel_id=1, source_target_pairs={{2,1},{5,6},{10,9},{13,14},{18,17},{21,22},{26,25},{29,30}} | collective-permute-start | bytes 2359304 | tf_op jit(solution)/shard_map/ppermute | solution.py:331
  71.4 38.7 %copy-start.9 = (s32[4]{0:T(128)S(1)}, s32[4]{0:T(128)}, u32[]{:S(2)}) copy-start(s32[4]{0:T(128)} %broadcast_select_fusion.1.refs_0_) | copy-start | bytes 52
  71.4 40.6 %copy-start.7 = (f32[1,4,128,256]{3,2,1,0:T(8,128)S(1)}, f32[1,4,128,256]{3,2,1,0:T(8,128)}, u32[]{:S(2)}) copy-start(f32[1,4,128,256]{3,2,1,0:T(8,128)} %param.11) | copy-start | bytes 1572868
  105.1 15.4 %copy-start.8 = (f32[64,8,256]{2,1,0:T(8,128)S(1)}, f32[64,8,256]{2,1,0:T(8,128)}, u32[]{:S(2)}) copy-start(f32[64,8,256]{2,1,0:T(8,128)} %get-tuple-element.14) | copy-start | bytes 1572868
  105.2 13.2 %collective-permute-start.6 = (f32[64,8,256]{2,1,0:T(8,128)}, f32[64,8,256]{2,1,0:T(8,128)S(1)}, u32[]{:S(2)}, u32[]{:S(2)}) collective-permute-start(f32[64,8,256]{2,1,0:T(8,128)} %get-tuple-element.15), channel_id=1, source_target_pairs={{1,0},{6,7},{9,8},{14,15},{17,16},{22,23},{25,24},{30,31}} | collective-permute-start | bytes 1572872 | tf_op jit(solution)/shard_map/ppermute | solution.py:345
  106.6 11.7 %collective-permute-start.7 = (f32[64,8,256]{2,1,0:T(8,128)}, f32[64,8,256]{2,1,0:T(8,128)S(1)}, u32[]{:S(2)}, u32[]{:S(2)}) collective-permute-start(f32[64,8,256]{2,1,0:T(8,128)} %get-tuple-element.16), channel_id=1, source_target_pairs={{1,3},{6,4},{9,11},{14,12},{17,19},{22,20},{25,27},{30,28}} | collective-permute-start | bytes 1572872 | tf_op jit(solution)/shard_map/ppermute | solution.py:345
  108.0 12.6 %collective-permute-start.8 = (f32[64,8,256]{2,1,0:T(8,128)}, f32[64,8,256]{2,1,0:T(8,128)}, u32[]{:S(2)}, u32[]{:S(2)}) collective-permute-start(f32[64,8,256]{2,1,0:T(8,128)} %get-tuple-element.17), channel_id=1, source_target_pairs={{1,2},{6,5},{9,10},{14,13},{17,18},{22,21},{25,26},{30,29}} | collective-permute-start | bytes 1572872 | tf_op jit(solution)/shard_map/ppermute | solution.py:345
  112.8 13.5 %all-to-all-start = ((f32[8,64,256]{2,1,0:T(8,128)}), f32[8,64,256]{2,1,0:T(8,128)S(1)}, u32[]{:S(2)}, u32[]{:S(2)}) async-start(f32[8,64,256]{2,1,0:T(8,128)} %bitcast.17), calls=%async_computation | async-start | bytes 1048576 | tf_op jit(solution)/shard_map/all_to_all | solution.py:334
  121.9 19.2 %copy-start.6 = (f32[4,16,8,256]{3,1,2,0:T(8,128)}, f32[4,16,8,256]{3,1,2,0:T(8,128)S(1)}, u32[]{:S(2)}) copy-start(f32[4,16,8,256]{3,1,2,0:T(8,128)S(1)} %copy.19) | copy-start | bytes 1572868
  126.3 12.8 %copy-start.4 = (f32[8,64,256]{2,1,0:T(8,128)}, f32[8,64,256]{2,1,0:T(8,128)S(1)}, u32[]{:S(2)}) copy-start(f32[8,64,256]{2,1,0:T(8,128)S(1)} %all-to-all-done.factor) | copy-start | bytes 1572868
